TPU v7x, 1024 devices: a whole 4x8x16 slice. The times are simulated.
1024 devices in a mesh: rows: 256 (over y, z, core), grp: 4 (over x).
Axes of the slice: x: 4, y: 8, z: 16, core: 2. Of those that a mesh axis runs over, the one named last changes fastest.
Arguments:
- a_tiles: bfloat16 [4096, 12, 128, 128], P(('rows', 'grp')), may hold values from -0.75 to 0.75
- a_cols: int32 [4096, 12], P(('rows', 'grp')), may hold values from 0 to 4095, as said below
- p_tiles: bfloat16 [4096, 128, 128], P(('rows', 'grp')), may hold values from -0.5 to 0.5
- p_agg: int32 [4096], P(('rows', 'grp')), may hold values from 0 to 1023, as said below
Outputs:
- coarse_band: float32 [1024, 7, 128, 128], P('rows', None, 'grp')
Inputs may be any that keep to these rules, and one draw needn't show every extreme that they name: `a_cols`: the 12 block columns of row i are distinct, include i itself, and lie among the 12 block rows starting at (i // 4 - 1) * 4, taken modulo 4096. p_agg[i] = (i // 4 + e) modulo 1024 with e in -1, 0, 1; e = -1 for the first row of each aligned group of 4 rows, e = 1 for the last, e is 0 or -1 in the first half of the group and 0 or 1 in the second, so rows 1 and 2 of each group (counting from 0) each take e from their own coin.
All inputs are finite; a program needn't handle non-finite values.
Results may differ from a plain program's by a relative error of at most 0.0029.
Values may be sent and summed in bfloat16 or wider, within the bound.
No kernel may reach another device: no remote copies, remote signals or barrier semaphores. Data moves between devices by JAX's collectives and lax.ppermute only.
A program may use at most 32 MiB of HBM per device.

v0:
```python
import jax
import jax.numpy as jnp
from jax import lax
from jax.sharding import PartitionSpec as P


def with_halo(block, sides, width):
    for axis, dim in sides:
        count = lax.axis_size(axis)
        forward = [(i, i + 1) for i in range(count - 1)]
        forward.append((count - 1, 0))
        backward = [(target, source) for source, target in forward]
        low = lax.ppermute(
            lax.slice_in_dim(block, block.shape[dim] - width, None, axis=dim), axis, forward
        )
        high = lax.ppermute(lax.slice_in_dim(block, 0, width, axis=dim), axis, backward)
        block = jnp.concatenate([low, block, high], axis=dim)
    return block


def from_behind(block, axis, distance):
    devices = range(lax.axis_size(axis))
    route = [((i - distance) % len(devices), i) for i in devices]
    return lax.ppermute(block, axis, route)


def shards(a_tiles, a_cols, p_tiles, p_agg):
    rows_here = p_tiles.shape[0]
    tile = p_tiles.shape[1]
    count = lax.axis_size(("rows", "grp"))
    whole = rows_here * count
    device = lax.axis_index(("rows", "grp"))
    padded_tiles, padded_agg = (
        with_halo(p_tiles, ((("rows", "grp"), 0),), rows_here),
        with_halo(p_agg, ((("rows", "grp"), 0),), rows_here),
    )
    first_row = device * rows_here - rows_here
    local_cols = jnp.mod(a_cols - first_row, whole)
    fetched = padded_tiles[local_cols]
    products = jnp.einsum(
        "rkxy,rkyz->rkxz", a_tiles, fetched, preferred_element_type=jnp.float32
    ).astype(jnp.bfloat16)
    terms = jnp.einsum("ryx,rkyz->rkxz", p_tiles, products, preferred_element_type=jnp.float32)
    row_slot = jnp.mod(p_agg - device + 1, count)
    col_slot = jnp.mod(padded_agg[local_cols] - device + 2, count).astype(jnp.int32)
    slot = (row_slot[:, None] * 5 + col_slot).reshape(-1)
    onehot = (jnp.arange(15, dtype=jnp.int32)[:, None] == slot[None, :]).astype(jnp.float32)
    sums = jnp.einsum(
        "um,mxz->uxz", onehot, terms.reshape(-1, tile, tile), precision=lax.Precision.HIGHEST
    ).reshape(3, 5, tile, tile)
    from_left = from_behind(sums[2], ("rows", "grp"), 1)
    from_right = from_behind(sums[0], ("rows", "grp"), -1)
    band = jnp.zeros((7, tile, tile), jnp.float32)
    band = band.at[1:6].add(sums[1])
    band = band.at[0:5].add(from_left)
    band = band.at[2:7].add(from_right)
    copies = lax.all_gather(band[None], "grp", axis=0, tiled=True)
    share = tile // lax.axis_size("grp")
    return lax.dynamic_slice_in_dim(copies, lax.axis_index("grp") * share, share, 2)


def solution(mesh):
    in_specs = (
        P(("rows", "grp"), None, None, None),
        P(("rows", "grp"), None),
        P(("rows", "grp"), None, None),
        P(("rows", "grp")),
    )
    out_specs = P("rows", None, "grp", None)
    return jax.shard_map(shards, mesh=mesh, in_specs=in_specs, out_specs=out_specs, check_vma=False)
```

profile of v0, /device:TPU:1, one launch (start us, length us, event | category | flops | bytes accessed | tf_op | source)
XLA Modules:
  0.0 120.1 jit_solution(8988246234828864963)
XLA Ops:
  6.5 0.0 copy-start
  6.5 0.0 copy-start.1
  6.5 0.0 all-gather.2.cloned.1.call-start
  6.5 4.1 %collective-permute-start = (s32[4]{0:T(128)}, s32[4]{0:T(128)S(1)}, u32[]{:S(2)}, u32[]{:S(2)}) collective-permute-start(s32[4]{0:T(128)} %param.13), channel_id=1, source_target_pairs={{0,1},{1,2},{2,3},{3,4},{4,5},{5,6},{6,7},{7,8},{8,9},{9,10},{10,1... | collective-permute-start | bytes 56 | tf_op jit(solution)/shard_map/ppermute | solution.py:13
  10.6 3.8 %collective-permute-start.1 = (s32[4]{0:T(128)}, s32[4]{0:T(128)S(1)}, u32[]{:S(2)}, u32[]{:S(2)}) collective-permute-start(s32[4]{0:T(128)} %param.13), channel_id=1, source_target_pairs={{1,0},{2,1},{3,2},{4,3},{5,4},{6,5},{7,6},{8,7},{9,8},{10,9},{11,1... | collective-permute-start | bytes 56 | tf_op jit(solution)/shard_map/ppermute | solution.py:16
  14.4 3.9 %collective-permute-start.3 = (bf16[4,128,128]{2,1,0:T(8,128)(2,1)}, bf16[4,128,128]{2,1,0:T(8,128)(2,1)S(1)}, u32[]{:S(2)}, u32[]{:S(2)}) collective-permute-start(bf16[4,128,128]{2,1,0:T(8,128)(2,1)} %param.12), channel_id=1, source_target_pairs={{1,0},{2,1},{3,2},{4,3},{5,4},{6,5},{7,6},{8,7},{9,8},{10,9},{11,1... | collective-permute-start | bytes 393224 | tf_op jit(solution)/shard_map/ppermute | solution.py:16
  18.3 1.9 %collective-permute-start.2 = (bf16[4,128,128]{2,1,0:T(8,128)(2,1)}, bf16[4,128,128]{2,1,0:T(8,128)(2,1)S(1)}, u32[]{:S(2)}, u32[]{:S(2)}) collective-permute-start(bf16[4,128,128]{2,1,0:T(8,128)(2,1)} %param.12), channel_id=1, source_target_pairs={{0,1},{1,2},{2,3},{3,4},{4,5},{5,6},{6,7},{7,8},{8,9},{9,10},{10,1... | collective-permute-start | bytes 393224 | tf_op jit(solution)/shard_map/ppermute | solution.py:13
  20.2 0.7 fusion.10
  20.9 0.1 add.85
  21.0 0.1 add.86
  21.1 0.7 compare_select_fusion
  21.8 0.1 reshape.134
  21.9 0.0 collective-permute-done
  21.9 0.0 collective-permute-done.1
  21.9 0.7 pad_add_fusion
  22.6 0.8 gather_fusion
  23.4 0.0 collective-permute-done.3
  23.4 2.6 %collective-permute-done.2 = bf16[4,128,128]{2,1,0:T(8,128)(2,1)S(1)} collective-permute-done((bf16[4,128,128]{2,1,0:T(8,128)(2,1)}, bf16[4,128,128]{2,1,0:T(8,128)(2,1)S(1)}, u32[]{:S(2)}, u32[]{:S(2)}) %collective-permute-start.2) | collective-permute-done | bytes 131104 | tf_op jit(solution)/shard_map/ppermute | solution.py:13
  26.0 0.0 copy-done.1
  26.1 0.8 gather_fusion.1
  26.9 0.0 copy-done
  26.9 4.2 %fusion = f32[4,12,128,128]{3,2,1,0:T(8,128)} fusion(bf16[4,12,128,128]{3,2,1,0:T(8,128)(2,1)S(1)} %bitcast.22, bf16[4,12,128,128]{3,2,1,0:T(8,128)(2,1)S(1)} %copy-done, bf16[4,128,128]{2,1,0:T(8,128)(2,1)} %param.12), kind=kOutput, calls=%fused_computation.3 | convolution fusion | flops 403439616 | bytes 6422528 | tf_op jit(solution)/shard_map/ryx,rkyz->rkxz/dot_general | solution.py:43
  31.1 3.6 %copy.10 = f32[48,128,128]{2,0,1:T(8,128)} copy(f32[48,128,128]{1,2,0:T(8,128)} %bitcast.21) | data formatting | bytes 6291456 | tf_op jit(solution)/shard_map/reshape | solution.py:49
  34.7 3.0 %fusion.5 = f32[15,128,128]{2,0,1:T(8,128)S(1)} fusion(f32[48,128,128]{2,0,1:T(8,128)} %copy.10, s32[48]{0:T(128)S(1)} %fusion.9), kind=kOutput, calls=%fused_computation.12 | convolution fusion | flops 141558480 | bytes 4128960 | tf_op jit(solution)/shard_map/um,mxz->uxz/dot_general | solution.py:48
  37.8 0.9 fusion.13
  38.6 1.9 %collective-permute-start.4 = (f32[5,128,128]{2,0,1:T(8,128)S(1)}, f32[5,128,128]{2,0,1:T(8,128)S(1)}, u32[]{:S(2)}, u32[]{:S(2)}) collective-permute-start(f32[5,128,128]{2,0,1:T(8,128)S(1)} %get-tuple-element.42), channel_id=1, source_target_pairs={{1023,0},{0,1},{1,2},{2,3},{3,4},{4,5},{5,6},{6,7},{7,8},{8,9},{9,... | collective-permute-start | bytes 983048 | tf_op jit(solution)/shard_map/ppermute | solution.py:24
  40.6 11.8 %collective-permute-start.5 = (f32[5,128,128]{2,0,1:T(8,128)}, f32[5,128,128]{2,0,1:T(8,128)S(1)}, u32[]{:S(2)}, u32[]{:S(2)}) collective-permute-start(f32[5,128,128]{2,0,1:T(8,128)} %get-tuple-element.41), channel_id=1, source_target_pairs={{1,0},{2,1},{3,2},{4,3},{5,4},{6,5},{7,6},{8,7},{9,8},{10,9},{11,1... | collective-permute-start | bytes 983048 | tf_op jit(solution)/shard_map/ppermute | solution.py:24
  52.4 0.1 scatter-add.10
  52.4 4.9 %collective-permute-done.4 = f32[5,128,128]{2,0,1:T(8,128)S(1)} collective-permute-done((f32[5,128,128]{2,0,1:T(8,128)S(1)}, f32[5,128,128]{2,0,1:T(8,128)S(1)}, u32[]{:S(2)}, u32[]{:S(2)}) %collective-permute-start.4) | collective-permute-done | bytes 327712 | tf_op jit(solution)/shard_map/ppermute | solution.py:24
  57.3 0.1 slice_add_fusion.1
  57.4 2.9 %scatter-add.11 = f32[7,128,128]{2,0,1:T(8,128)S(1)} dynamic-update-slice(f32[7,128,128]{2,0,1:T(8,128)S(1)} %scatter-add.10, f32[5,128,128]{2,0,1:T(8,128)S(1)} %slice_add_fusion.1, s32[]{:T(128)} %constant.131.clone.1, s32[]{:T(128)} %constant.131.clone.1, s32[]{:T(128)} %constant.131.clone.1) | dynamic-update-slice | bytes 655364 | tf_op jit(solution)/shard_map/scatter-add | solution.py:55
  60.3 0.6 collective-permute-done.5
  60.8 0.1 fusion.2
  60.9 2.9 %scatter-add.14 = f32[1,7,128,128]{3,1,2,0:T(8,128)S(1)} dynamic-update-slice(f32[1,7,128,128]{3,1,2,0:T(8,128)S(1)} %bitcast.23, f32[1,5,128,128]{3,1,2,0:T(8,128)S(1)} %fusion.2, s32[]{:T(128)} %constant.131.clone.1, s32[]{:T(128)} %constant.139.clone.1, s32[]{:T(128)} %constant.131.clone.1, s32[]{:T(128)} %constant.131.clone.1) | dynamic-update-slice | bytes 655364 | tf_op jit(solution)/shard_map/scatter-add | solution.py:56
  63.8 0.9 copy.11
  64.6 0.0 all-gather.2.cloned.1.call-update
  64.7 46.7 %all-gather.2.cloned.1.call-done = f32[4,7,128,128]{3,2,1,0:T(8,128)} async-done(((f32[1,7,128,128]{3,2,1,0:T(8,128)}), f32[4,7,128,128]{3,2,1,0:T(8,128)}) %all-gather.2.cloned.1.call-update) | async-done | bytes 1835024 | tf_op jit(solution)/shard_map/all_gather | solution.py:57
  111.4 1.8 %constant_dynamic-slice_fusion = f32[4,7,32,128]{3,2,1,0:T(8,128)} fusion(f32[4,7,128,128]{3,2,1,0:T(8,128)} %all-gather.2.cloned.1.call-done, s32[]{:T(128)S(6)} %select_n.32), kind=kLoop, calls=%fused_computation.31 | loop fusion | bytes 917508 | tf_op jit(solution)/shard_map/dynamic_slice | solution.py:59
  (3 shorter events, 0.1 us)
Async XLA Ops:
  6.5 20.4 %copy-start = (bf16[4,12,128,128]{3,2,1,0:T(8,128)(2,1)S(1)}, bf16[4,12,128,128]{3,2,1,0:T(8,128)(2,1)}, u32[]{:S(2)}) copy-start(bf16[4,12,128,128]{3,2,1,0:T(8,128)(2,1)} %param.10) | copy-start | bytes 4718596
  6.5 19.5 %copy-start.1 = (bf16[4,128,128]{2,1,0:T(8,128)(2,1)S(1)}, bf16[4,128,128]{2,1,0:T(8,128)(2,1)}, u32[]{:S(2)}) copy-start(bf16[4,128,128]{2,1,0:T(8,128)(2,1)} %param.12) | copy-start | bytes 393220
  6.5 104.9 %all-gather.2.cloned.1.call-start = ((), (), s32[]{:S(2)}) async-start(), calls=%async_computation | async-start | bytes 2293760 | tf_op jit(solution)/shard_map/all_gather | solution.py:57
  6.5 15.3 %collective-permute-start = (s32[4]{0:T(128)}, s32[4]{0:T(128)S(1)}, u32[]{:S(2)}, u32[]{:S(2)}) collective-permute-start(s32[4]{0:T(128)} %param.13), channel_id=1, source_target_pairs={{0,1},{1,2},{2,3},{3,4},{4,5},{5,6},{6,7},{7,8},{8,9},{9,10},{10,1... | collective-permute-start | bytes 56 | tf_op jit(solution)/shard_map/ppermute | solution.py:13
  10.6 11.3 %collective-permute-start.1 = (s32[4]{0:T(128)}, s32[4]{0:T(128)S(1)}, u32[]{:S(2)}, u32[]{:S(2)}) collective-permute-start(s32[4]{0:T(128)} %param.13), channel_id=1, source_target_pairs={{1,0},{2,1},{3,2},{4,3},{5,4},{6,5},{7,6},{8,7},{9,8},{10,9},{11,1... | collective-permute-start | bytes 56 | tf_op jit(solution)/shard_map/ppermute | solution.py:16
  14.4 9.0 %collective-permute-start.3 = (bf16[4,128,128]{2,1,0:T(8,128)(2,1)}, bf16[4,128,128]{2,1,0:T(8,128)(2,1)S(1)}, u32[]{:S(2)}, u32[]{:S(2)}) collective-permute-start(bf16[4,128,128]{2,1,0:T(8,128)(2,1)} %param.12), channel_id=1, source_target_pairs={{1,0},{2,1},{3,2},{4,3},{5,4},{6,5},{7,6},{8,7},{9,8},{10,9},{11,1... | collective-permute-start | bytes 393224 | tf_op jit(solution)/shard_map/ppermute | solution.py:16
  18.3 7.7 %collective-permute-start.2 = (bf16[4,128,128]{2,1,0:T(8,128)(2,1)}, bf16[4,128,128]{2,1,0:T(8,128)(2,1)S(1)}, u32[]{:S(2)}, u32[]{:S(2)}) collective-permute-start(bf16[4,128,128]{2,1,0:T(8,128)(2,1)} %param.12), channel_id=1, source_target_pairs={{0,1},{1,2},{2,3},{3,4},{4,5},{5,6},{6,7},{7,8},{8,9},{9,10},{10,1... | collective-permute-start | bytes 393224 | tf_op jit(solution)/shard_map/ppermute | solution.py:13
  38.6 18.6 %collective-permute-start.4 = (f32[5,128,128]{2,0,1:T(8,128)S(1)}, f32[5,128,128]{2,0,1:T(8,128)S(1)}, u32[]{:S(2)}, u32[]{:S(2)}) collective-permute-start(f32[5,128,128]{2,0,1:T(8,128)S(1)} %get-tuple-element.42), channel_id=1, source_target_pairs={{1023,0},{0,1},{1,2},{2,3},{3,4},{4,5},{5,6},{6,7},{7,8},{8,9},{9,... | collective-permute-start | bytes 983048 | tf_op jit(solution)/shard_map/ppermute | solution.py:24
  40.6 20.3 %collective-permute-start.5 = (f32[5,128,128]{2,0,1:T(8,128)}, f32[5,128,128]{2,0,1:T(8,128)S(1)}, u32[]{:S(2)}, u32[]{:S(2)}) collective-permute-start(f32[5,128,128]{2,0,1:T(8,128)} %get-tuple-element.41), channel_id=1, source_target_pairs={{1,0},{2,1},{3,2},{4,3},{5,4},{6,5},{7,6},{8,7},{9,8},{10,9},{11,1... | collective-permute-start | bytes 983048 | tf_op jit(solution)/shard_map/ppermute | solution.py:24
Sparse Core Ops, SparseCore 0:
  64.8 46.5 all-gather.1
where the time goes:
time: 120 us
  waiting for transfers between devices  54.8 us (46%)
  starting transfers between devices  27.4 us (23%)
  local copies, waits for them, and re-layouts  14.8 us (12%)
  between operations  13.5 us (11%)
  matrix products  7.25 us (6%)
  other arithmetic  2.35 us (2%)
    all_gather x1, waiting for transfers between devices, shards(): copies = lax.all_gather(band[None], 'grp', axis=0, tiled=True)  46.7 us
    ppermute x2, starting transfers between devices, from_behind(): return lax.ppermute(block, axis, route)  13.7 us
    ppermute x2, starting transfers between devices, with_halo(): lax.ppermute(lax.slice_in_dim(block, 0, width, axis=dim), axis, backward)  7.67 us
    ppermute x2, starting transfers between devices, with_halo(): lax.ppermute(lax.slice_in_dim(block, block.shape[dim] - width, None, axis...  5.99 us
    ppermute x2, waiting for transfers between devices, from_behind(): return lax.ppermute(block, axis, route)  5.41 us
    dot_general x1, matrix products, shards(): jnp.einsum('ryx,rkyz->rkxz', p_tiles, products, preferred_element_type=jn...  4.21 us
    scatter-add x2, local copies, waits for them, and re-layouts, shards(): band = band.at[2:7].add(from_right)  3.72 us
    reshape x1, local copies, waits for them, and re-layouts, shards(): terms.reshape(-1, tile, tile)  3.57 us
  transfers between devices with their start and end apart: 7, of which 4 were waited for; matrix products, arithmetic and copies ran while one was open for 5% of the time, Pallas kernels for 0%

commit v1 on v0

v1 whole, which is shorter than its diff:
```python
import functools

import jax
import jax.numpy as jnp
from jax import lax
from jax.experimental import pallas as pl
from jax.experimental.pallas import tpu as pltpu
from jax.sharding import PartitionSpec as P

BS = 128
RB = 4
KT = 12
HALO = RB * BS + 16
SMEM = pl.BlockSpec(memory_space=pltpu.SMEM)
VMEM = pl.BlockSpec(memory_space=pltpu.VMEM)
LIMIT = 32 << 20


def row_bits(count, agg_ref):
    first = agg_ref[0]
    low = (agg_ref[1] - first) & (count - 1)
    high = ((agg_ref[2] - first) & (count - 1)) - 1
    return low, high


def pack_kernel(count, agg_ref, p_ref, out_ref):
    low, high = row_bits(count, agg_ref)
    out_ref[: RB * BS, :] = p_ref[...].reshape(RB * BS, BS)
    half = lax.broadcasted_iota(jnp.int32, (16, BS), 0) < 8
    out_ref[RB * BS :, :] = jnp.where(half, low, high).astype(jnp.float32).astype(jnp.bfloat16)


def halo_bits(ref):
    flags = ref[RB * BS :, :].astype(jnp.float32)
    return (
        jnp.max(flags[:8, :]).astype(jnp.int32),
        jnp.max(flags[8:, :]).astype(jnp.int32),
    )


def terms_kernel(count, cols_ref, agg_ref, a_ref, p_ref, lo_ref, hi_ref, bnd_ref, out_ref, place, acc, left, weights):
    first = agg_ref[0]
    low, high = row_bits(count, agg_ref)
    for r in range(RB):
        for k in range(KT):
            place[r, (cols_ref[r, k] - first * RB) & (RB * count - 1)] = k

    zero = jnp.zeros((BS, BS), jnp.bfloat16)
    turned = [p_ref[r].astype(jnp.float32).T for r in range(RB)]
    keep1 = (low == 0).astype(jnp.float32)
    keep2 = (high == 0).astype(jnp.float32)
    left[0, :BS, :BS] = turned[0].astype(jnp.bfloat16)
    left[0, :BS, BS:] = (turned[1] * keep1).astype(jnp.bfloat16)
    left[0, BS:, :BS] = zero
    left[0, BS:, BS:] = (turned[1] * (1 - keep1)).astype(jnp.bfloat16)
    left[1, :BS, :BS] = (turned[2] * keep2).astype(jnp.bfloat16)
    left[1, :BS, BS:] = zero
    left[1, BS:, :BS] = (turned[2] * (1 - keep2)).astype(jnp.bfloat16)
    left[1, BS:, BS:] = turned[3].astype(jnp.bfloat16)

    acc[...] = jnp.zeros_like(acc)
    bits = (halo_bits(lo_ref), (low, high), halo_bits(hi_ref))

    for pair in range(6):
        n, top = pair // 2, 2 * (pair % 2)
        tiles = []
        for c in (top, top + 1):
            if n == 1:
                tiles.append(p_ref[c])
            else:
                tiles.append((lo_ref if n == 0 else hi_ref)[c * BS : (c + 1) * BS, :])
        w = weights.at[pair % 2]
        w[:BS, :BS] = tiles[0]
        w[:BS, BS:] = zero
        w[BS:, :BS] = zero
        w[BS:, BS:] = tiles[1]
        lhs = jnp.concatenate(
            [
                jnp.concatenate(
                    [a_ref[r, place[r, n * RB + top]], a_ref[r, place[r, n * RB + top + 1]]], axis=1
                )
                for r in range(RB)
            ],
            axis=0,
        )
        prod = jnp.dot(lhs, w[...], preferred_element_type=jnp.float32).astype(jnp.bfloat16)
        up = jnp.dot(left[0], prod[: 2 * BS], preferred_element_type=jnp.float32)
        down = jnp.dot(left[1], prod[2 * BS :], preferred_element_type=jnp.float32)
        b1, b2 = bits[n]
        slots = (n, n + b1) if top == 0 else (n + 1 + b2, n + 2)
        for c in range(2):
            lanes = slice(c * BS, (c + 1) * BS)
            acc[0, slots[c]] += up[:BS, lanes]
            acc[1, slots[c]] += up[BS:, lanes] + down[:BS, lanes]
            acc[2, slots[c]] += down[BS:, lanes]

    side = jnp.where(((first + 1) & 3) == 0, 0, 2)
    for j in range(5):
        bnd_ref[j] = acc[side, j].astype(jnp.bfloat16)
    for s in range(3):
        for j in range(5):
            block = acc[s, j].astype(jnp.bfloat16)
            for q in range(4):
                out_ref[q, s * 5 + j] = block[q * 32 : (q + 1) * 32, :]


def join_kernel(agg_ref, got_ref, sums_ref, out_ref):
    g = (agg_ref[0] + 1) & 3

    @pl.when(g == 0)
    def _():
        for j in range(5):
            for q in range(4):
                out_ref[q, j] = got_ref[j, q * 32 : (q + 1) * 32, :]

    @pl.when(g == 3)
    def _():
        for j in range(5):
            for q in range(4):
                out_ref[q, 10 + j] = got_ref[j, q * 32 : (q + 1) * 32, :]

    for q in range(4):
        out_ref[q, 5:10] = sums_ref[q, 5:10]

    @pl.when(g != 0)
    def _():
        for q in range(4):
            out_ref[q, :5] = sums_ref[q, :5]

    @pl.when(g != 3)
    def _():
        for q in range(4):
            out_ref[q, 10:] = sums_ref[q, 10:]


def band_kernel(in_ref, out_ref):
    def part(g, s, j):
        return in_ref[g, 5 * s + j].astype(jnp.float32)

    for c in range(4):
        for j in range(7):
            terms = []
            if 1 <= j < 6:
                terms.append(part(c, 1, j - 1))
            if j < 5:
                terms.append(part(c - 1, 2, j) if c > 0 else part(0, 0, j))
            if j >= 2:
                terms.append(part(c + 1, 0, j - 2) if c < 3 else part(3, 2, j - 2))
            total = terms[0]
            for term in terms[1:]:
                total = total + term
            out_ref[c, j] = total


def shards(a_tiles, a_cols, p_tiles, p_agg):
    axes = ("rows", "grp")
    count = lax.axis_size(axes)
    params = pltpu.CompilerParams(vmem_limit_bytes=LIMIT)
    packed = pl.pallas_call(
        functools.partial(pack_kernel, count),
        out_shape=jax.ShapeDtypeStruct((HALO, BS), jnp.bfloat16),
        in_specs=[SMEM, VMEM],
        out_specs=VMEM,
        compiler_params=params,
        name="pack",
    )(p_agg, p_tiles)
    ahead = [(i, (i + 1) % count) for i in range(count)]
    low = lax.ppermute(packed, axes, ahead)
    high = lax.ppermute(packed, axes, [(b, a) for a, b in ahead])
    edge, sums = pl.pallas_call(
        functools.partial(terms_kernel, count),
        out_shape=(
            jax.ShapeDtypeStruct((5, BS, BS), jnp.bfloat16),
            jax.ShapeDtypeStruct((4, 15, 32, BS), jnp.bfloat16),
        ),
        in_specs=[SMEM, SMEM, VMEM, VMEM, VMEM, VMEM],
        out_specs=(VMEM, VMEM),
        scratch_shapes=[
            pltpu.SMEM((RB, KT), jnp.int32),
            pltpu.VMEM((3, 5, BS, BS), jnp.float32),
            pltpu.VMEM((2, 2 * BS, 2 * BS), jnp.bfloat16),
            pltpu.VMEM((2, 2 * BS, 2 * BS), jnp.bfloat16),
        ],
        compiler_params=params,
        name="terms",
    )(a_cols, p_agg, a_tiles, p_tiles, low, high)
    cross = []
    for i in range(0, count, 4):
        cross.append((i, (i - 1) % count))
        cross.append((i + 3, (i + 4) % count))
    got = lax.ppermute(edge, axes, cross)
    joined = pl.pallas_call(
        join_kernel,
        out_shape=jax.ShapeDtypeStruct((4, 15, 32, BS), jnp.bfloat16),
        in_specs=[SMEM, VMEM, VMEM],
        out_specs=VMEM,
        compiler_params=params,
        name="join",
    )(p_agg, got, sums)
    parts = lax.all_to_all(joined, "grp", 0, 0, tiled=True)
    return pl.pallas_call(
        band_kernel,
        out_shape=jax.ShapeDtypeStruct((4, 7, 32, BS), jnp.float32),
        in_specs=[VMEM],
        out_specs=VMEM,
        compiler_params=params,
        name="band",
    )(parts)


def solution(mesh):
    in_specs = (
        P(("rows", "grp"), None, None, None),
        P(("rows", "grp"), None),
        P(("rows", "grp"), None, None),
        P(("rows", "grp")),
    )
    out_specs = P("rows", None, "grp", None)
    return jax.shard_map(shards, mesh=mesh, in_specs=in_specs, out_specs=out_specs, check_vma=False)
```

time: 120 us -> 64.6 us (0.54)
  the two profiles are of different devices: /device:TPU:1 before, /device:TPU:2 now
where the time goes in v1:
time: 64.6 us; the launch traced here: 64.3 us
  blocking collectives  27.8 us (43%)
  starting transfers between devices  17.7 us (27%)
  waiting for transfers between devices  11.2 us (17%)
  Pallas kernels  4 us (6%)
  local copies, waits for them, and re-layouts  3.65 us (6%)
    all_to_all x1, blocking collectives, shards(): parts = lax.all_to_all(joined, 'grp', 0, 0, tiled=True)  27.8 us
    ppermute x1, starting transfers between devices, shards(): high = lax.ppermute(packed, axes, [(b, a) for a, b in ahead])  15.1 us
    ppermute x1, waiting for transfers between devices, shards(): low = lax.ppermute(packed, axes, ahead)  10.6 us
    unnamed x8, local copies, waits for them, and re-layouts  3.65 us
    pallas_call x1, Pallas kernels, shards(): pl.pallas_call(functools.partial(terms_kernel, count), out_shape=(jax.Sha...  2.04 us
    ppermute x1, starting transfers between devices, shards(): low = lax.ppermute(packed, axes, ahead)  1.92 us
  transfers between devices with their start and end apart: 3, of which 2 were waited for; matrix products, arithmetic and copies ran while one was open for 0% of the time, Pallas kernels for 0%

profile of v1, /device:TPU:2, one launch (start us, length us, event | category | flops | bytes accessed | tf_op | source)
XLA Modules:
  0.0 64.3 jit_solution(6316816489112408281)
XLA Ops:
  0.0 0.0 copy-start.1
  0.0 0.9 %copy-done.1 = bf16[4,128,128]{2,1,0:T(8,128)(2,1)S(1)} copy-done((bf16[4,128,128]{2,1,0:T(8,128)(2,1)S(1)}, bf16[4,128,128]{2,1,0:T(8,128)(2,1)}, u32[]{:S(2)}) %copy-start.1) | copy-done | bytes 131096
  0.9 0.0 copy-start.2
  0.9 0.7 %copy-done.2 = s32[4]{0:T(128)S(1)} copy-done((s32[4]{0:T(128)S(1)}, s32[4]{0:T(128)}, u32[]{:S(2)}) %copy-start.2) | copy-done | bytes 40
  1.6 0.6 pack.1
  2.1 15.1 %collective-permute-start.1 = (bf16[528,128]{1,0:T(8,128)(2,1)S(1)}, bf16[528,128]{1,0:T(8,128)(2,1)S(1)}, u32[]{:S(2)}, u32[]{:S(2)}) collective-permute-start(bf16[528,128]{1,0:T(8,128)(2,1)S(1)} %pack.1), channel_id=1, source_target_pairs={{1,0},{2,1},{3,2},{4,3},{5,4},{6,5},{7,6},{8,7},{9,8},{10,9},{11,1... | collective-permute-start | bytes 405512 | tf_op jit(solution)/shard_map/ppermute | solution.py:169
  17.2 1.9 %collective-permute-start = (bf16[528,128]{1,0:T(8,128)(2,1)S(1)}, bf16[528,128]{1,0:T(8,128)(2,1)S(1)}, u32[]{:S(2)}, u32[]{:S(2)}) collective-permute-start(bf16[528,128]{1,0:T(8,128)(2,1)S(1)} %pack.1), channel_id=1, source_target_pairs={{0,1},{1,2},{2,3},{3,4},{4,5},{5,6},{6,7},{7,8},{8,9},{9,10},{10,1... | collective-permute-start | bytes 405512 | tf_op jit(solution)/shard_map/ppermute | solution.py:168
  19.1 0.6 collective-permute-done.1.hi_ref
  19.8 10.6 %collective-permute-done.lo_ref = bf16[528,128]{1,0:T(8,128)(2,1)S(1)} collective-permute-done((bf16[528,128]{1,0:T(8,128)(2,1)S(1)}, bf16[528,128]{1,0:T(8,128)(2,1)S(1)}, u32[]{:S(2)}, u32[]{:S(2)}) %collective-permute-start) | collective-permute-done | bytes 135200 | tf_op jit(solution)/shard_map/ppermute | solution.py:168
  30.3 0.0 copy-start
  30.3 1.4 %copy-done = bf16[4,12,128,128]{3,2,1,0:T(8,128)(2,1)S(1)} copy-done((bf16[4,12,128,128]{3,2,1,0:T(8,128)(2,1)S(1)}, bf16[4,12,128,128]{3,2,1,0:T(8,128)(2,1)}, u32[]{:S(2)}) %copy-start) | copy-done | bytes 1572888
  31.7 0.0 copy-start.3
  31.7 0.7 %copy-done.3 = s32[4,12]{1,0:T(4,128)S(1)} copy-done((s32[4,12]{1,0:T(4,128)S(1)}, s32[4,12]{1,0:T(4,128)}, u32[]{:S(2)}) %copy-start.3) | copy-done | bytes 216
  32.4 2.0 %terms.1 = (bf16[5,128,128]{2,1,0:T(8,128)(2,1)S(1)}, bf16[4,15,32,128]{3,2,1,0:T(8,128)(2,1)S(1)}) custom-call(s32[4,12]{1,0:T(4,128)S(1)} %copy-done.3, s32[4]{0:T(128)S(1)} %copy-done.2, bf16[4,12,128,128]{3,2,1,0:T(8,128)(2,1)S(1)} %copy-done, bf16[4,128,128]{2,1,0:T(8,128)(2,1)S(1)} %copy-done.1, bf16[528,128]{1,0:T(8,128)(2,1)S(1)} %collective-permute-done.lo_ref, ...), custom_call_target="tpu_custom_call" | custom-call | tf_op jit(solution)/shard_map/terms/pallas_call | solution.py:170
  34.5 0.7 %collective-permute-start.2 = (bf16[5,128,128]{2,1,0:T(8,128)(2,1)S(1)}, bf16[5,128,128]{2,1,0:T(8,128)(2,1)S(1)}, u32[]{:S(2)}, u32[]{:S(2)}) collective-permute-start(bf16[5,128,128]{2,1,0:T(8,128)(2,1)S(1)} %get-tuple-element.7), channel_id=1, source_target_pairs={{0,1023},{3,4},{4,3},{7,8},{8,7},{11,12},{12,11},{15,16},{16,15},{... | collective-permute-start | bytes 491528 | tf_op jit(solution)/shard_map/ppermute | solution.py:191
  35.1 0.0 collective-permute-done.2.got_ref
  35.1 0.6 join.1
  35.7 27.8 %all_to_all.5.in_ref = bf16[4,15,32,128]{3,2,1,0:T(8,128)(2,1)S(1)} all-to-all(bf16[4,15,32,128]{3,2,1,0:T(8,128)(2,1)S(1)} %join.1), channel_id=1, replica_groups=mesh['rows'=256,'grp'=4] {'grp'}, dimensions={0} | all-to-all | bytes 983040 | tf_op jit(solution)/shard_map/all_to_all | solution.py:200
  63.5 0.8 %band.1 = f32[4,7,32,128]{3,2,1,0:T(8,128)} custom-call(bf16[4,15,32,128]{3,2,1,0:T(8,128)(2,1)S(1)} %all_to_all.5.in_ref), custom_call_target="tpu_custom_call" | custom-call | tf_op jit(solution)/shard_map/band/pallas_call | solution.py:201
Async XLA Ops:
  0.0 0.9 %copy-start.1 = (bf16[4,128,128]{2,1,0:T(8,128)(2,1)S(1)}, bf16[4,128,128]{2,1,0:T(8,128)(2,1)}, u32[]{:S(2)}) copy-start(bf16[4,128,128]{2,1,0:T(8,128)(2,1)} %p_ref.3) | copy-start | bytes 393220
  0.9 0.7 %copy-start.2 = (s32[4]{0:T(128)S(1)}, s32[4]{0:T(128)}, u32[]{:S(2)}) copy-start(s32[4]{0:T(128)} %agg_ref.5) | copy-start | bytes 52
  2.1 17.6 %collective-permute-start.1 = (bf16[528,128]{1,0:T(8,128)(2,1)S(1)}, bf16[528,128]{1,0:T(8,128)(2,1)S(1)}, u32[]{:S(2)}, u32[]{:S(2)}) collective-permute-start(bf16[528,128]{1,0:T(8,128)(2,1)S(1)} %pack.1), channel_id=1, source_target_pairs={{1,0},{2,1},{3,2},{4,3},{5,4},{6,5},{7,6},{8,7},{9,8},{10,9},{11,1... | collective-permute-start | bytes 405512 | tf_op jit(solution)/shard_map/ppermute | solution.py:169
  17.2 13.1 %collective-permute-start = (bf16[528,128]{1,0:T(8,128)(2,1)S(1)}, bf16[528,128]{1,0:T(8,128)(2,1)S(1)}, u32[]{:S(2)}, u32[]{:S(2)}) collective-permute-start(bf16[528,128]{1,0:T(8,128)(2,1)S(1)} %pack.1), channel_id=1, source_target_pairs={{0,1},{1,2},{2,3},{3,4},{4,5},{5,6},{6,7},{7,8},{8,9},{9,10},{10,1... | collective-permute-start | bytes 405512 | tf_op jit(solution)/shard_map/ppermute | solution.py:168
  30.3 1.4 %copy-start = (bf16[4,12,128,128]{3,2,1,0:T(8,128)(2,1)S(1)}, bf16[4,12,128,128]{3,2,1,0:T(8,128)(2,1)}, u32[]{:S(2)}) copy-start(bf16[4,12,128,128]{3,2,1,0:T(8,128)(2,1)} %a_ref.1) | copy-start | bytes 4718596
  31.7 0.7 %copy-start.3 = (s32[4,12]{1,0:T(4,128)S(1)}, s32[4,12]{1,0:T(4,128)}, u32[]{:S(2)}) copy-start(s32[4,12]{1,0:T(4,128)} %cols_ref.1) | copy-start | bytes 580
  34.5 0.7 %collective-permute-start.2 = (bf16[5,128,128]{2,1,0:T(8,128)(2,1)S(1)}, bf16[5,128,128]{2,1,0:T(8,128)(2,1)S(1)}, u32[]{:S(2)}, u32[]{:S(2)}) collective-permute-start(bf16[5,128,128]{2,1,0:T(8,128)(2,1)S(1)} %get-tuple-element.7), channel_id=1, source_target_pairs={{0,1023},{3,4},{4,3},{7,8},{8,7},{11,12},{12,11},{15,16},{16,15},{... | collective-permute-start | bytes 491528 | tf_op jit(solution)/shard_map/ppermute | solution.py:191

commit v2 on v1

v2 whole, which is shorter than its diff:
```python
import functools

import jax
import jax.numpy as jnp
from jax import lax
from jax.experimental import pallas as pl
from jax.experimental.pallas import tpu as pltpu
from jax.sharding import PartitionSpec as P

BS = 128
RB = 4
KT = 12
HALO = RB * BS + 16
HBM = pl.BlockSpec(memory_space=pltpu.HBM)
VMEM = pl.BlockSpec(memory_space=pltpu.VMEM)
LIMIT = 32 << 20


def row_bits(count, agg_ref):
    first = agg_ref[0]
    low = (agg_ref[1] - first) & (count - 1)
    high = ((agg_ref[2] - first) & (count - 1)) - 1
    return low, high


def pack_kernel(count, agg_hbm, p_hbm, out_ref, agg_ref, agg_sem, p_sem):
    agg_copy = pltpu.make_async_copy(agg_hbm, agg_ref, agg_sem)
    agg_copy.start()
    copies = [
        pltpu.make_async_copy(p_hbm.at[r], out_ref.at[pl.ds(r * BS, BS)], p_sem.at[r])
        for r in range(RB)
    ]
    for copy in copies:
        copy.start()
    agg_copy.wait()
    low, high = row_bits(count, agg_ref)
    half = lax.broadcasted_iota(jnp.int32, (16, BS), 0) < 8
    out_ref[RB * BS :, :] = jnp.where(half, low, high).astype(jnp.float32).astype(jnp.bfloat16)
    for copy in copies:
        copy.wait()


def halo_bits(ref):
    flags = ref[RB * BS :, :].astype(jnp.float32)
    return (
        jnp.max(flags[:8, :]).astype(jnp.int32),
        jnp.max(flags[8:, :]).astype(jnp.int32),
    )


def fill_weights(w, tiles_ref, top):
    w[:BS, :BS] = tiles_ref[top * BS : (top + 1) * BS, :]
    w[BS:, BS:] = tiles_ref[(top + 1) * BS : (top + 2) * BS, :]


def clear_weights(weights):
    zero = jnp.zeros((BS, BS), jnp.bfloat16)
    for i in range(weights.shape[0]):
        weights[i, :BS, BS:] = zero
        weights[i, BS:, :BS] = zero


def add_pair(n, top, bits, lhs, w, left, acc):
    prod = jnp.dot(lhs, w[...], preferred_element_type=jnp.float32).astype(jnp.bfloat16)
    up = jnp.dot(left[0], prod[: 2 * BS], preferred_element_type=jnp.float32)
    down = jnp.dot(left[1], prod[2 * BS :], preferred_element_type=jnp.float32)
    b1, b2 = bits
    slots = (n, n + b1) if top == 0 else (n + 1 + b2, n + 2)
    for c in range(2):
        lanes = slice(c * BS, (c + 1) * BS)
        acc[0, slots[c]] += up[:BS, lanes]
        acc[1, slots[c]] += up[BS:, lanes] + down[:BS, lanes]
        acc[2, slots[c]] += down[BS:, lanes]


def near_kernel(
    count, cols_hbm, agg_hbm, a_hbm, p_ref, lhs_ref, left, acc, side_ref,
    cols_ref, agg_ref, place, tiles, weights, sems, a_sems,
):
    cols_copy = pltpu.make_async_copy(cols_hbm, cols_ref, sems.at[0])
    agg_copy = pltpu.make_async_copy(agg_hbm, agg_ref, sems.at[1])
    cols_copy.start()
    agg_copy.start()
    copies = [pltpu.make_async_copy(a_hbm.at[r], tiles.at[r], a_sems.at[r]) for r in range(RB)]
    for copy in copies:
        copy.start()
    clear_weights(weights)
    for i in range(2):
        fill_weights(weights.at[i], p_ref, 2 * i)
    acc[...] = jnp.zeros_like(acc)
    turned = [p_ref[r * BS : (r + 1) * BS, :].astype(jnp.float32).T for r in range(RB)]
    agg_copy.wait()
    first = agg_ref[0]
    low, high = row_bits(count, agg_ref)
    zero = jnp.zeros((BS, BS), jnp.bfloat16)
    keep1 = (low == 0).astype(jnp.float32)
    keep2 = (high == 0).astype(jnp.float32)
    left[0, :BS, :BS] = turned[0].astype(jnp.bfloat16)
    left[0, :BS, BS:] = (turned[1] * keep1).astype(jnp.bfloat16)
    left[0, BS:, :BS] = zero
    left[0, BS:, BS:] = (turned[1] * (1 - keep1)).astype(jnp.bfloat16)
    left[1, :BS, :BS] = (turned[2] * keep2).astype(jnp.bfloat16)
    left[1, :BS, BS:] = zero
    left[1, BS:, :BS] = (turned[2] * (1 - keep2)).astype(jnp.bfloat16)
    left[1, BS:, BS:] = turned[3].astype(jnp.bfloat16)
    side_ref[...] = jnp.full((8, BS), (first + 1) & 3, jnp.int32).astype(jnp.float32)

    cols_copy.wait()
    for r in range(RB):
        for k in range(KT):
            place[r, (cols_ref[r, k] - first * RB) & (RB * count - 1)] = k
    for copy in copies:
        copy.wait()
    for top in (0, 2):
        lhs = jnp.concatenate(
            [
                jnp.concatenate([tiles[r, place[r, RB + top + c]] for c in range(2)], axis=1)
                for r in range(RB)
            ],
            axis=0,
        )
        add_pair(1, top, (low, high), lhs, weights.at[top // 2], left, acc)
    base = ((first + 1) & 1) * 2 * RB
    for i in range(4):
        for r in range(RB):
            for c in range(2):
                col = (base if i < 2 else 2 * RB - base) + 2 * (i % 2) + c
                lhs_ref[i, r * BS : (r + 1) * BS, c * BS : (c + 1) * BS] = tiles[r, place[r, col]]


def add_half(h, slots, lhs, w, left, acc):
    prod = jnp.dot(lhs, w[...], preferred_element_type=jnp.float32).astype(jnp.bfloat16)
    sums = jnp.dot(left[h], prod, preferred_element_type=jnp.float32)
    for c in range(2):
        lanes = slice(c * BS, (c + 1) * BS)
        acc[h, slots[c]] += sums[:BS, lanes]
        acc[h + 1, slots[c]] += sums[BS:, lanes]


def far_half(other, lhs_ref, left, near, side_ref, two_ref, one_ref, acc, weights):
    clear_weights(weights)
    for i in range(4):
        fill_weights(weights.at[i], (one_ref, two_ref)[i // 2], 2 * (i % 2))
    acc[...] = near[...]
    side = jnp.max(side_ref[...]).astype(jnp.int32)
    h = 1 - side // 2 if other else side // 2
    offset = 2 * (side & 1)
    bits = (halo_bits(one_ref), halo_bits(two_ref))
    rows = pl.ds(pl.multiple_of(h * 2 * BS, 2 * BS), 2 * BS)
    for i in range(4):
        n = offset if i < 2 else 2 - offset
        b1, b2 = bits[i // 2]
        slots = (n, n + b1) if i % 2 == 0 else (n + 1 + b2, n + 2)
        add_half(h, slots, lhs_ref[i, rows, :], weights.at[i], left, acc)


def edge_kernel(lhs_ref, left, near, side_ref, two_ref, one_ref, edge_ref, acc, weights):
    far_half(False, lhs_ref, left, near, side_ref, two_ref, one_ref, acc, weights)
    first = side_ref[:1, :] < 2
    for j in range(5):
        edge_ref[j] = jnp.where(first, acc[0, j], acc[2, j]).astype(jnp.bfloat16)


def rest_kernel(lhs_ref, left, near, side_ref, two_ref, one_ref, out_ref, acc, weights):
    far_half(True, lhs_ref, left, near, side_ref, two_ref, one_ref, acc, weights)
    for s in range(3):
        for j in range(5):
            block = acc[s, j].astype(jnp.bfloat16)
            for q in range(4):
                out_ref[q, s * 5 + j] = block[q * 32 : (q + 1) * 32, :]


def join_kernel(side_ref, got_ref, sums_ref, out_ref):
    for side, base in ((0, 0), (3, 10)):
        here = side_ref[:1, :] == side
        for j in range(5):
            for q in range(4):
                new = got_ref[j, q * 32 : (q + 1) * 32, :].astype(jnp.float32)
                old = sums_ref[q, base + j].astype(jnp.float32)
                out_ref[q, base + j] = jnp.where(here, new, old).astype(jnp.bfloat16)
    for q in range(4):
        out_ref[q, 5:10] = sums_ref[q, 5:10]


def band_kernel(in_ref, out_ref):
    def part(g, s, j):
        return in_ref[g, 5 * s + j].astype(jnp.float32)

    for c in range(4):
        for j in range(7):
            terms = []
            if 1 <= j < 6:
                terms.append(part(c, 1, j - 1))
            if j < 5:
                terms.append(part(c - 1, 2, j) if c > 0 else part(0, 0, j))
            if j >= 2:
                terms.append(part(c + 1, 0, j - 2) if c < 3 else part(3, 2, j - 2))
            total = terms[0]
            for term in terms[1:]:
                total = total + term
            out_ref[c, j] = total


def shards(a_tiles, a_cols, p_tiles, p_agg):
    axes = ("rows", "grp")
    count = lax.axis_size(axes)
    params = pltpu.CompilerParams(vmem_limit_bytes=LIMIT)
    a_tiles, a_cols, p_tiles, p_agg = (
        pltpu.with_memory_space_constraint(x, pltpu.HBM) for x in (a_tiles, a_cols, p_tiles, p_agg)
    )
    packed = pl.pallas_call(
        functools.partial(pack_kernel, count),
        out_shape=jax.ShapeDtypeStruct((HALO, BS), jnp.bfloat16),
        in_specs=[HBM, HBM],
        out_specs=VMEM,
        scratch_shapes=[
            pltpu.SMEM((RB,), jnp.int32),
            pltpu.SemaphoreType.DMA,
            pltpu.SemaphoreType.DMA((RB,)),
        ],
        compiler_params=params,
        name="pack",
    )(p_agg, p_tiles)
    outer = [(i, (i + 1 if i % 2 else i - 1) % count) for i in range(count)]
    inner = [(i, i ^ 1) for i in range(count)]
    one = lax.ppermute(packed, axes, outer)
    two = lax.ppermute(packed, axes, inner)
    lhs, left, near, side = pl.pallas_call(
        functools.partial(near_kernel, count),
        out_shape=(
            jax.ShapeDtypeStruct((4, RB * BS, 2 * BS), jnp.bfloat16),
            jax.ShapeDtypeStruct((2, 2 * BS, 2 * BS), jnp.bfloat16),
            jax.ShapeDtypeStruct((3, 5, BS, BS), jnp.float32),
            jax.ShapeDtypeStruct((8, BS), jnp.float32),
        ),
        in_specs=[HBM, HBM, HBM, VMEM],
        out_specs=(VMEM, VMEM, VMEM, VMEM),
        scratch_shapes=[
            pltpu.SMEM((RB, KT), jnp.int32),
            pltpu.SMEM((RB,), jnp.int32),
            pltpu.SMEM((RB, KT), jnp.int32),
            pltpu.VMEM((RB, KT, BS, BS), jnp.bfloat16),
            pltpu.VMEM((2, 2 * BS, 2 * BS), jnp.bfloat16),
            pltpu.SemaphoreType.DMA((2,)),
            pltpu.SemaphoreType.DMA((RB,)),
        ],
        compiler_params=params,
        cost_estimate=pl.CostEstimate(flops=2 * 10**8, bytes_accessed=3 * 10**6, transcendentals=0),
        name="near",
    )(a_cols, p_agg, a_tiles, packed)
    far_in = (lhs, left, near, side, two, one)
    edge, most = pl.pallas_call(
        edge_kernel,
        out_shape=(
            jax.ShapeDtypeStruct((5, BS, BS), jnp.bfloat16),
            jax.ShapeDtypeStruct((3, 5, BS, BS), jnp.float32),
        ),
        in_specs=[VMEM] * 6,
        out_specs=(VMEM, VMEM),
        scratch_shapes=[pltpu.VMEM((4, 2 * BS, 2 * BS), jnp.bfloat16)],
        compiler_params=params,
        name="edge",
    )(*far_in)
    sums = pl.pallas_call(
        rest_kernel,
        out_shape=jax.ShapeDtypeStruct((4, 15, 32, BS), jnp.bfloat16),
        in_specs=[VMEM] * 6,
        out_specs=VMEM,
        scratch_shapes=[
            pltpu.VMEM((3, 5, BS, BS), jnp.float32),
            pltpu.VMEM((4, 2 * BS, 2 * BS), jnp.bfloat16),
        ],
        compiler_params=params,
        cost_estimate=pl.CostEstimate(flops=2 * 10**8, bytes_accessed=3 * 10**6, transcendentals=0),
        name="rest",
    )(lhs, left, most, side, two, one)
    cross = []
    for i in range(0, count, 4):
        cross.append((i, (i - 1) % count))
        cross.append((i + 3, (i + 4) % count))
    got = lax.ppermute(edge, axes, cross)
    joined = pl.pallas_call(
        join_kernel,
        out_shape=jax.ShapeDtypeStruct((4, 15, 32, BS), jnp.bfloat16),
        in_specs=[VMEM, VMEM, VMEM],
        out_specs=VMEM,
        compiler_params=params,
        name="join",
    )(side, got, sums)
    parts = lax.all_to_all(joined, "grp", 0, 0, tiled=True)
    return pl.pallas_call(
        band_kernel,
        out_shape=jax.ShapeDtypeStruct((4, 7, 32, BS), jnp.float32),
        in_specs=[VMEM],
        out_specs=VMEM,
        compiler_params=params,
        name="band",
    )(parts)


def solution(mesh):
    in_specs = (
        P(("rows", "grp"), None, None, None),
        P(("rows", "grp"), None),
        P(("rows", "grp"), None, None),
        P(("rows", "grp")),
    )
    out_specs = P("rows", None, "grp", None)
    return jax.shard_map(shards, mesh=mesh, in_specs=in_specs, out_specs=out_specs, check_vma=False)
```

time: 64.6 us -> 54.4 us (0.84)
  waiting for transfers between devices: 11.2 us -> 1.49 us
  starting transfers between devices: 17.7 us -> 25.9 us
  blocking collectives: 27.8 us -> 21.2 us
  local copies, waits for them, and re-layouts: 3.65 us -> 0 us
  Pallas kernels: 4 us -> 5.51 us
    ppermute x2, waiting for transfers between devices: 11.2 us -> 1.48 us  [the longest x1 1.48 us: shards(): two = lax.ppermute(packed, axes, inner)]
    ppermute x2, starting transfers between devices: 17 us -> 25.2 us  [the longest x1 21.8 us: shards(): two = lax.ppermute(packed, axes, inner)]
    all_to_all x1, blocking collectives: 27.8 us -> 21.2 us  [shards(): parts = lax.all_to_all(joined, 'grp', 0, 0, tiled=True)]
    unnamed x8 -> x0, local copies, waits for them, and re-layouts: 3.65 us -> none
    pallas_call x1 -> x3, Pallas kernels: 2.04 us -> 3.75 us  [the longest x1 2.21 us: shards(): pl.pallas_call(functools.partial(near_kernel, count), out_shape=(jax.Shap...]
  transfers between devices with their start and end apart: 3 -> 3, of which waited for: 2 -> 1; matrix products, arithmetic and copies ran while one was open for 0% -> 0% of each run, Pallas kernels for 0% -> 6%
where the time goes in v2:
time: 54.4 us; the launch traced here: 54.1 us
  starting transfers between devices  25.9 us (48%)
  blocking collectives  21.2 us (39%)
  Pallas kernels  5.51 us (10%)
  waiting for transfers between devices  1.49 us (3%)
    ppermute x1, starting transfers between devices, shards(): two = lax.ppermute(packed, axes, inner)  21.8 us
    all_to_all x1, blocking collectives, shards(): parts = lax.all_to_all(joined, 'grp', 0, 0, tiled=True)  21.2 us
    ppermute x1, starting transfers between devices, shards(): one = lax.ppermute(packed, axes, outer)  3.4 us
    pallas_call x1, Pallas kernels, shards(): pl.pallas_call(functools.partial(near_kernel, count), out_shape=(jax.Shap...  2.21 us
    ppermute x1, waiting for transfers between devices, shards(): two = lax.ppermute(packed, axes, inner)  1.48 us
  transfers between devices with their start and end apart: 3, of which 1 were waited for; matrix products, arithmetic and copies ran while one was open for 0% of the time, Pallas kernels for 6%

profile of v2, /device:TPU:2, one launch (start us, length us, event | category | flops | bytes accessed | tf_op | source)
XLA Modules:
  0.0 54.1 jit_solution(4768403297545860897)
XLA Ops:
  0.0 0.9 %pack.1.p_ref = bf16[528,128]{1,0:T(8,128)(2,1)S(1)} custom-call(s32[4]{0:T(128)} %agg_hbm.3, bf16[4,128,128]{2,1,0:T(8,128)(2,1)} %p_hbm.1), custom_call_target="tpu_custom_call" | custom-call | tf_op jit(solution)/shard_map/pack/pallas_call | solution.py:211
  0.9 3.4 %collective-permute-start.1 = (bf16[528,128]{1,0:T(8,128)(2,1)S(1)}, bf16[528,128]{1,0:T(8,128)(2,1)S(1)}, u32[]{:S(2)}, u32[]{:S(2)}) collective-permute-start(bf16[528,128]{1,0:T(8,128)(2,1)S(1)} %pack.1.p_ref), channel_id=1, source_target_pairs={{0,1023},{1,2},{2,1},{3,4},{4,3},{5,6},{6,5},{7,8},{8,7},{9,10},{1... | collective-permute-start | bytes 405512 | tf_op jit(solution)/shard_map/ppermute | solution.py:226
  4.3 21.8 %collective-permute-start = (bf16[528,128]{1,0:T(8,128)(2,1)S(1)}, bf16[528,128]{1,0:T(8,128)(2,1)S(1)}, u32[]{:S(2)}, u32[]{:S(2)}) collective-permute-start(bf16[528,128]{1,0:T(8,128)(2,1)S(1)} %pack.1.p_ref), channel_id=1, source_target_pairs={{0,1},{1,0},{2,3},{3,2},{4,5},{5,4},{6,7},{7,6},{8,9},{9,8},{10,11... | collective-permute-start | bytes 405512 | tf_op jit(solution)/shard_map/ppermute | solution.py:227
  26.1 2.2 %near.1 = (bf16[4,512,256]{2,1,0:T(8,128)(2,1)S(1)}, bf16[2,256,256]{2,1,0:T(8,128)(2,1)S(1)}, f32[3,5,128,128]{3,2,1,0:T(8,128)S(1)}, f32[8,128]{1,0:T(8,128)S(1)}) custom-call(s32[4,12]{1,0:T(4,128)} %cols_hbm.1, s32[4]{0:T(128)} %agg_hbm.3, bf16[4,12,128,128]{3,2,1,0:T(8,128)(2,1)} %a_hbm.1, bf16[528,128]{1,0:T(8,128)(2,1)S(1)} %pack.1.p_ref), custom_call_target="tpu_custom_call" | custom-call | flops 200000000 | bytes 3000000 | tf_op jit(solution)/shard_map/near/pallas_call | solution.py:228
  28.3 0.0 collective-permute-done.1.one_ref
  28.3 1.5 %collective-permute-done.two_ref = bf16[528,128]{1,0:T(8,128)(2,1)S(1)} collective-permute-done((bf16[528,128]{1,0:T(8,128)(2,1)S(1)}, bf16[528,128]{1,0:T(8,128)(2,1)S(1)}, u32[]{:S(2)}, u32[]{:S(2)}) %collective-permute-start) | collective-permute-done | bytes 135200 | tf_op jit(solution)/shard_map/ppermute | solution.py:227
  29.8 0.8 %edge.1 = (bf16[5,128,128]{2,1,0:T(8,128)(2,1)S(1)}, f32[3,5,128,128]{3,2,1,0:T(8,128)S(1)}) custom-call(bf16[4,512,256]{2,1,0:T(8,128)(2,1)S(1)} %get-tuple-element.12.lhs_ref, bf16[2,256,256]{2,1,0:T(8,128)(2,1)S(1)} %get-tuple-element.13.left, f32[3,5,128,128]{3,2,1,0:T(8,128)S(1)} %get-tuple-element.14.near, f32[8,128]{1,0:T(8,128)S(1)} %get-tuple-element.11.side_ref, ...), custom_call_target="tpu_custom_call" | custom-call | tf_op jit(solution)/shard_map/edge/pallas_call | solution.py:252
  30.6 0.7 %collective-permute-start.2 = (bf16[5,128,128]{2,1,0:T(8,128)(2,1)S(1)}, bf16[5,128,128]{2,1,0:T(8,128)(2,1)S(1)}, u32[]{:S(2)}, u32[]{:S(2)}) collective-permute-start(bf16[5,128,128]{2,1,0:T(8,128)(2,1)S(1)} %get-tuple-element.15), channel_id=1, source_target_pairs={{0,1023},{3,4},{4,3},{7,8},{8,7},{11,12},{12,11},{15,16},{16,15},{... | collective-permute-start | bytes 491528 | tf_op jit(solution)/shard_map/ppermute | solution.py:281
  31.2 0.8 %rest.1.sums_ref = bf16[4,15,32,128]{3,2,1,0:T(8,128)(2,1)S(1)} custom-call(bf16[4,512,256]{2,1,0:T(8,128)(2,1)S(1)} %get-tuple-element.12.lhs_ref, bf16[2,256,256]{2,1,0:T(8,128)(2,1)S(1)} %get-tuple-element.13.left, f32[3,5,128,128]{3,2,1,0:T(8,128)S(1)} %get-tuple-element.16.near, f32[8,128]{1,0:T(8,128)S(1)} %get-tuple-element.11.side_ref, ...), custom_call_target="tpu_custom_call" | custom-call | flops 200000000 | bytes 3000000 | tf_op jit(solution)/shard_map/rest/pallas_call | solution.py:264
  32.0 0.0 collective-permute-done.2.got_ref
  32.0 0.1 join.1
  32.1 21.2 %all_to_all.5.in_ref = bf16[4,15,32,128]{3,2,1,0:T(8,128)(2,1)S(1)} all-to-all(bf16[4,15,32,128]{3,2,1,0:T(8,128)(2,1)S(1)} %join.1), channel_id=1, replica_groups=mesh['rows'=256,'grp'=4] {'grp'}, dimensions={0} | all-to-all | bytes 983040 | tf_op jit(solution)/shard_map/all_to_all | solution.py:290
  53.3 0.8 %band.1 = f32[4,7,32,128]{3,2,1,0:T(8,128)} custom-call(bf16[4,15,32,128]{3,2,1,0:T(8,128)(2,1)S(1)} %all_to_all.5.in_ref), custom_call_target="tpu_custom_call" | custom-call | tf_op jit(solution)/shard_map/band/pallas_call | solution.py:291
Async XLA Ops:
  0.9 27.4 %collective-permute-start.1 = (bf16[528,128]{1,0:T(8,128)(2,1)S(1)}, bf16[528,128]{1,0:T(8,128)(2,1)S(1)}, u32[]{:S(2)}, u32[]{:S(2)}) collective-permute-start(bf16[528,128]{1,0:T(8,128)(2,1)S(1)} %pack.1.p_ref), channel_id=1, source_target_pairs={{0,1023},{1,2},{2,1},{3,4},{4,3},{5,6},{6,5},{7,8},{8,7},{9,10},{1... | collective-permute-start | bytes 405512 | tf_op jit(solution)/shard_map/ppermute | solution.py:226
  4.3 25.5 %collective-permute-start = (bf16[528,128]{1,0:T(8,128)(2,1)S(1)}, bf16[528,128]{1,0:T(8,128)(2,1)S(1)}, u32[]{:S(2)}, u32[]{:S(2)}) collective-permute-start(bf16[528,128]{1,0:T(8,128)(2,1)S(1)} %pack.1.p_ref), channel_id=1, source_target_pairs={{0,1},{1,0},{2,3},{3,2},{4,5},{5,4},{6,7},{7,6},{8,9},{9,8},{10,11... | collective-permute-start | bytes 405512 | tf_op jit(solution)/shard_map/ppermute | solution.py:227
  30.6 1.5 %collective-permute-start.2 = (bf16[5,128,128]{2,1,0:T(8,128)(2,1)S(1)}, bf16[5,128,128]{2,1,0:T(8,128)(2,1)S(1)}, u32[]{:S(2)}, u32[]{:S(2)}) collective-permute-start(bf16[5,128,128]{2,1,0:T(8,128)(2,1)S(1)} %get-tuple-element.15), channel_id=1, source_target_pairs={{0,1023},{3,4},{4,3},{7,8},{8,7},{11,12},{12,11},{15,16},{16,15},{... | collective-permute-start | bytes 491528 | tf_op jit(solution)/shard_map/ppermute | solution.py:281

commit v3 on v2

--- a/solution.py
+++ b/solution.py
@@ -64,8 +64,7 @@
     prod = jnp.dot(lhs, w[...], preferred_element_type=jnp.float32).astype(jnp.bfloat16)
     up = jnp.dot(left[0], prod[: 2 * BS], preferred_element_type=jnp.float32)
     down = jnp.dot(left[1], prod[2 * BS :], preferred_element_type=jnp.float32)
-    b1, b2 = bits
-    slots = (n, n + b1) if top == 0 else (n + 1 + b2, n + 2)
+    slots = pair_slots(n, top, bits)
     for c in range(2):
         lanes = slice(c * BS, (c + 1) * BS)
         acc[0, slots[c]] += up[:BS, lanes]
@@ -73,8 +72,13 @@
         acc[2, slots[c]] += down[BS:, lanes]
 
 
+def pair_slots(n, top, bits):
+    b1, b2 = bits
+    return (n, n + b1) if top == 0 else (n + 1 + b2, n + 2)
+
+
 def near_kernel(
-    count, cols_hbm, agg_hbm, a_hbm, p_ref, lhs_ref, left, acc, side_ref,
+    count, cols_hbm, agg_hbm, a_hbm, p_ref, two_ref, lhs_ref, left, acc, side_ref,
     cols_ref, agg_ref, place, tiles, weights, sems, a_sems,
 ):
     cols_copy = pltpu.make_async_copy(cols_hbm, cols_ref, sems.at[0])
@@ -85,10 +89,11 @@
     for copy in copies:
         copy.start()
     clear_weights(weights)
-    for i in range(2):
-        fill_weights(weights.at[i], p_ref, 2 * i)
+    for i in range(4):
+        fill_weights(weights.at[i], (p_ref, two_ref)[i // 2], 2 * (i % 2))
     acc[...] = jnp.zeros_like(acc)
     turned = [p_ref[r * BS : (r + 1) * BS, :].astype(jnp.float32).T for r in range(RB)]
+    two_bits = halo_bits(two_ref)
     agg_copy.wait()
     first = agg_ref[0]
     low, high = row_bits(count, agg_ref)
@@ -109,60 +114,57 @@
     for r in range(RB):
         for k in range(KT):
             place[r, (cols_ref[r, k] - first * RB) & (RB * count - 1)] = k
+    odd = (first + 1) & 1
+    inner = (1 - odd) * 2 * RB
+    outer = odd * 2 * RB
     for copy in copies:
         copy.wait()
-    for top in (0, 2):
+    for i in range(4):
+        start = (RB if i < 2 else inner) + 2 * (i % 2)
         lhs = jnp.concatenate(
             [
-                jnp.concatenate([tiles[r, place[r, RB + top + c]] for c in range(2)], axis=1)
+                jnp.concatenate([tiles[r, place[r, start + c]] for c in range(2)], axis=1)
                 for r in range(RB)
             ],
             axis=0,
         )
-        add_pair(1, top, (low, high), lhs, weights.at[top // 2], left, acc)
-    base = ((first + 1) & 1) * 2 * RB
-    for i in range(4):
+        n = 1 if i < 2 else 2 * (1 - odd)
+        add_pair(n, 2 * (i % 2), (low, high) if i < 2 else two_bits, lhs, weights.at[i], left, acc)
+    for i in range(2):
         for r in range(RB):
             for c in range(2):
-                col = (base if i < 2 else 2 * RB - base) + 2 * (i % 2) + c
-                lhs_ref[i, r * BS : (r + 1) * BS, c * BS : (c + 1) * BS] = tiles[r, place[r, col]]
-
-
-def add_half(h, slots, lhs, w, left, acc):
-    prod = jnp.dot(lhs, w[...], preferred_element_type=jnp.float32).astype(jnp.bfloat16)
-    sums = jnp.dot(left[h], prod, preferred_element_type=jnp.float32)
-    for c in range(2):
-        lanes = slice(c * BS, (c + 1) * BS)
-        acc[h, slots[c]] += sums[:BS, lanes]
-        acc[h + 1, slots[c]] += sums[BS:, lanes]
-
-
-def far_half(other, lhs_ref, left, near, side_ref, two_ref, one_ref, acc, weights):
+                tile = tiles[r, place[r, outer + 2 * i + c]]
+                lhs_ref[i, r * BS : (r + 1) * BS, c * BS : (c + 1) * BS] = tile
+
+
+def edge_kernel(lhs_ref, left, near, side_ref, one_ref, edge_ref, acc, weights):
     clear_weights(weights)
-    for i in range(4):
-        fill_weights(weights.at[i], (one_ref, two_ref)[i // 2], 2 * (i % 2))
+    for i in range(2):
+        fill_weights(weights.at[i], one_ref, 2 * i)
+    side = jnp.max(side_ref[...]).astype(jnp.int32)
+    h = side // 2
+    acc[...] = near[2 * h]
+    bits = halo_bits(one_ref)
+    rows = pl.ds(pl.multiple_of(h * 2 * BS, 2 * BS), 2 * BS)
+    part = left[h, pl.ds(pl.multiple_of(h * BS, BS), BS), :]
+    for i in range(2):
+        prod = jnp.dot(lhs_ref[i, rows, :], weights[i], preferred_element_type=jnp.float32)
+        sums = jnp.dot(part, prod.astype(jnp.bfloat16), preferred_element_type=jnp.float32)
+        slots = pair_slots(2 * (side & 1), 2 * i, bits)
+        for c in range(2):
+            acc[slots[c]] += sums[:, c * BS : (c + 1) * BS]
+    edge_ref[...] = acc[...].astype(jnp.bfloat16)
+
+
+def rest_kernel(lhs_ref, left, near, side_ref, one_ref, out_ref, acc, weights):
+    clear_weights(weights)
+    for i in range(2):
+        fill_weights(weights.at[i], one_ref, 2 * i)
     acc[...] = near[...]
     side = jnp.max(side_ref[...]).astype(jnp.int32)
-    h = 1 - side // 2 if other else side // 2
-    offset = 2 * (side & 1)
-    bits = (halo_bits(one_ref), halo_bits(two_ref))
-    rows = pl.ds(pl.multiple_of(h * 2 * BS, 2 * BS), 2 * BS)
-    for i in range(4):
-        n = offset if i < 2 else 2 - offset
-        b1, b2 = bits[i // 2]
-        slots = (n, n + b1) if i % 2 == 0 else (n + 1 + b2, n + 2)
-        add_half(h, slots, lhs_ref[i, rows, :], weights.at[i], left, acc)
-
-
-def edge_kernel(lhs_ref, left, near, side_ref, two_ref, one_ref, edge_ref, acc, weights):
-    far_half(False, lhs_ref, left, near, side_ref, two_ref, one_ref, acc, weights)
-    first = side_ref[:1, :] < 2
-    for j in range(5):
-        edge_ref[j] = jnp.where(first, acc[0, j], acc[2, j]).astype(jnp.bfloat16)
-
-
-def rest_kernel(lhs_ref, left, near, side_ref, two_ref, one_ref, out_ref, acc, weights):
-    far_half(True, lhs_ref, left, near, side_ref, two_ref, one_ref, acc, weights)
+    bits = halo_bits(one_ref)
+    for i in range(2):
+        add_pair(2 * (side & 1), 2 * i, bits, lhs_ref[i], weights.at[i], left, acc)
     for s in range(3):
         for j in range(5):
             block = acc[s, j].astype(jnp.bfloat16)
@@ -182,23 +184,28 @@
         out_ref[q, 5:10] = sums_ref[q, 5:10]
 
 
-def band_kernel(in_ref, out_ref):
+def band_kernel(in_ref, out_hbm, out_ref, sems):
     def part(g, s, j):
         return in_ref[g, 5 * s + j].astype(jnp.float32)
 
+    copies = []
     for c in range(4):
         for j in range(7):
             terms = []
             if 1 <= j < 6:
                 terms.append(part(c, 1, j - 1))
             if j < 5:
-                terms.append(part(c - 1, 2, j) if c > 0 else part(0, 0, j))
+                terms.append(part(c - 1, 2, j) if c > 0 else part(3, 2, j))
             if j >= 2:
-                terms.append(part(c + 1, 0, j - 2) if c < 3 else part(3, 2, j - 2))
+                terms.append(part(c + 1, 0, j - 2) if c < 3 else part(0, 0, j - 2))
             total = terms[0]
             for term in terms[1:]:
                 total = total + term
             out_ref[c, j] = total
+        copies.append(pltpu.make_async_copy(out_ref.at[c], out_hbm.at[c], sems.at[c]))
+        copies[-1].start()
+    for copy in copies:
+        copy.wait()
 
 
 def shards(a_tiles, a_cols, p_tiles, p_agg):
@@ -221,64 +228,62 @@
         compiler_params=params,
         name="pack",
     )(p_agg, p_tiles)
-    outer = [(i, (i + 1 if i % 2 else i - 1) % count) for i in range(count)]
-    inner = [(i, i ^ 1) for i in range(count)]
-    one = lax.ppermute(packed, axes, outer)
-    two = lax.ppermute(packed, axes, inner)
+    two = lax.ppermute(packed, axes, [(i, i ^ 1) for i in range(count)])
+    one = lax.ppermute(packed, axes, [(i, (i + 1 if i % 2 else i - 1) % count) for i in range(count)])
     lhs, left, near, side = pl.pallas_call(
         functools.partial(near_kernel, count),
         out_shape=(
-            jax.ShapeDtypeStruct((4, RB * BS, 2 * BS), jnp.bfloat16),
+            jax.ShapeDtypeStruct((2, RB * BS, 2 * BS), jnp.bfloat16),
             jax.ShapeDtypeStruct((2, 2 * BS, 2 * BS), jnp.bfloat16),
             jax.ShapeDtypeStruct((3, 5, BS, BS), jnp.float32),
             jax.ShapeDtypeStruct((8, BS), jnp.float32),
         ),
-        in_specs=[HBM, HBM, HBM, VMEM],
+        in_specs=[HBM, HBM, HBM, VMEM, VMEM],
         out_specs=(VMEM, VMEM, VMEM, VMEM),
         scratch_shapes=[
             pltpu.SMEM((RB, KT), jnp.int32),
             pltpu.SMEM((RB,), jnp.int32),
             pltpu.SMEM((RB, KT), jnp.int32),
             pltpu.VMEM((RB, KT, BS, BS), jnp.bfloat16),
-            pltpu.VMEM((2, 2 * BS, 2 * BS), jnp.bfloat16),
+            pltpu.VMEM((4, 2 * BS, 2 * BS), jnp.bfloat16),
             pltpu.SemaphoreType.DMA((2,)),
             pltpu.SemaphoreType.DMA((RB,)),
         ],
         compiler_params=params,
-        cost_estimate=pl.CostEstimate(flops=2 * 10**8, bytes_accessed=3 * 10**6, transcendentals=0),
+        cost_estimate=pl.CostEstimate(flops=2 * 10**8, bytes_accessed=4 * 10**6, transcendentals=0),
         name="near",
-    )(a_cols, p_agg, a_tiles, packed)
-    far_in = (lhs, left, near, side, two, one)
-    edge, most = pl.pallas_call(
+    )(a_cols, p_agg, a_tiles, packed, two)
+    far = (lhs, left, near, side, one)
+    edge = pl.pallas_call(
         edge_kernel,
-        out_shape=(
-            jax.ShapeDtypeStruct((5, BS, BS), jnp.bfloat16),
-            jax.ShapeDtypeStruct((3, 5, BS, BS), jnp.float32),
-        ),
-        in_specs=[VMEM] * 6,
-        out_specs=(VMEM, VMEM),
-        scratch_shapes=[pltpu.VMEM((4, 2 * BS, 2 * BS), jnp.bfloat16)],
+        out_shape=jax.ShapeDtypeStruct((5, BS, BS), jnp.bfloat16),
+        in_specs=[VMEM] * 5,
+        out_specs=VMEM,
+        scratch_shapes=[
+            pltpu.VMEM((5, BS, BS), jnp.float32),
+            pltpu.VMEM((2, 2 * BS, 2 * BS), jnp.bfloat16),
+        ],
         compiler_params=params,
         name="edge",
-    )(*far_in)
+    )(*far)
+    cross = []
+    for i in range(0, count, 4):
+        cross.append((i, (i - 4) % count))
+        cross.append((i + 3, (i + 7) % count))
+    got = lax.ppermute(edge, axes, cross)
     sums = pl.pallas_call(
         rest_kernel,
         out_shape=jax.ShapeDtypeStruct((4, 15, 32, BS), jnp.bfloat16),
-        in_specs=[VMEM] * 6,
+        in_specs=[VMEM] * 5,
         out_specs=VMEM,
         scratch_shapes=[
             pltpu.VMEM((3, 5, BS, BS), jnp.float32),
-            pltpu.VMEM((4, 2 * BS, 2 * BS), jnp.bfloat16),
+            pltpu.VMEM((2, 2 * BS, 2 * BS), jnp.bfloat16),
         ],
         compiler_params=params,
         cost_estimate=pl.CostEstimate(flops=2 * 10**8, bytes_accessed=3 * 10**6, transcendentals=0),
         name="rest",
-    )(lhs, left, most, side, two, one)
-    cross = []
-    for i in range(0, count, 4):
-        cross.append((i, (i - 1) % count))
-        cross.append((i + 3, (i + 4) % count))
-    got = lax.ppermute(edge, axes, cross)
+    )(*far)
     joined = pl.pallas_call(
         join_kernel,
         out_shape=jax.ShapeDtypeStruct((4, 15, 32, BS), jnp.bfloat16),
@@ -292,7 +297,11 @@
         band_kernel,
         out_shape=jax.ShapeDtypeStruct((4, 7, 32, BS), jnp.float32),
         in_specs=[VMEM],
-        out_specs=VMEM,
+        out_specs=HBM,
+        scratch_shapes=[
+            pltpu.VMEM((4, 7, 32, BS), jnp.float32),
+            pltpu.SemaphoreType.DMA((4,)),
+        ],
         compiler_params=params,
         name="band",
     )(parts)

time: 54.4 us -> 51.4 us (0.945)
  starting transfers between devices: 25.9 us -> 17.7 us
  blocking collectives: 21.2 us -> 25.2 us
  waiting for transfers between devices: 1.49 us -> 2.52 us
    ppermute x2, starting transfers between devices: 25.2 us -> 17 us  [the longest x1 15.1 us: shards(): two = lax.ppermute(packed, axes, [(i, i ^ 1) for i in range(count)])]
    all_to_all x1, blocking collectives: 21.2 us -> 25.2 us  [shards(): parts = lax.all_to_all(joined, 'grp', 0, 0, tiled=True)]
    ppermute x2, waiting for transfers between devices: 1.48 us -> 2.52 us  [the longest x1 1.47 us: shards(): lax.ppermute(packed, axes, [(i, (i + 1 if i % 2 else i - 1) % count) for...]
  transfers between devices with their start and end apart: 3 -> 3, of which waited for: 1 -> 2; matrix products, arithmetic and copies ran while one was open for 0% -> 0% of each run, Pallas kernels for 6% -> 6%
where the time goes in v3:
time: 51.4 us; the launch traced here: 51.1 us
  blocking collectives  25.2 us (49%)
  starting transfers between devices  17.7 us (34%)
  Pallas kernels  5.64 us (11%)
  waiting for transfers between devices  2.52 us (5%)
    all_to_all x1, blocking collectives, shards(): parts = lax.all_to_all(joined, 'grp', 0, 0, tiled=True)  25.2 us
    ppermute x1, starting transfers between devices, shards(): two = lax.ppermute(packed, axes, [(i, i ^ 1) for i in range(count)])  15.1 us
    pallas_call x1, Pallas kernels, shards(): pl.pallas_call(functools.partial(near_kernel, count), out_shape=(jax.Shap...  2.45 us
    ppermute x1, starting transfers between devices, shards(): lax.ppermute(packed, axes, [(i, (i + 1 if i % 2 else i - 1) % count) for...  1.92 us
    ppermute x1, waiting for transfers between devices, shards(): lax.ppermute(packed, axes, [(i, (i + 1 if i % 2 else i - 1) % count) for...  1.47 us
    ppermute x1, waiting for transfers between devices, shards(): two = lax.ppermute(packed, axes, [(i, i ^ 1) for i in range(count)])  1.05 us
  transfers between devices with their start and end apart: 3, of which 2 were waited for; matrix products, arithmetic and copies ran while one was open for 0% of the time, Pallas kernels for 6%

profile of v3, /device:TPU:2, one launch (start us, length us, event | category | flops | bytes accessed | tf_op | source)
XLA Modules:
  0.0 51.1 jit_solution(6469374066841049151)
XLA Ops:
  0.0 0.9 %pack.1.p_ref = bf16[528,128]{1,0:T(8,128)(2,1)S(1)} custom-call(s32[4]{0:T(128)} %agg_hbm.3, bf16[4,128,128]{2,1,0:T(8,128)(2,1)} %p_hbm.1), custom_call_target="tpu_custom_call" | custom-call | tf_op jit(solution)/shard_map/pack/pallas_call | solution.py:218
  0.9 15.1 %collective-permute-start = (bf16[528,128]{1,0:T(8,128)(2,1)S(1)}, bf16[528,128]{1,0:T(8,128)(2,1)S(1)}, u32[]{:S(2)}, u32[]{:S(2)}) collective-permute-start(bf16[528,128]{1,0:T(8,128)(2,1)S(1)} %pack.1.p_ref), channel_id=1, source_target_pairs={{0,1},{1,0},{2,3},{3,2},{4,5},{5,4},{6,7},{7,6},{8,9},{9,8},{10,11... | collective-permute-start | bytes 405512 | tf_op jit(solution)/shard_map/ppermute | solution.py:231
  16.0 1.9 %collective-permute-start.1 = (bf16[528,128]{1,0:T(8,128)(2,1)S(1)}, bf16[528,128]{1,0:T(8,128)(2,1)S(1)}, u32[]{:S(2)}, u32[]{:S(2)}) collective-permute-start(bf16[528,128]{1,0:T(8,128)(2,1)S(1)} %pack.1.p_ref), channel_id=1, source_target_pairs={{0,1023},{1,2},{2,1},{3,4},{4,3},{5,6},{6,5},{7,8},{8,7},{9,10},{1... | collective-permute-start | bytes 405512 | tf_op jit(solution)/shard_map/ppermute | solution.py:232
  17.9 1.0 %collective-permute-done.two_ref = bf16[528,128]{1,0:T(8,128)(2,1)S(1)} collective-permute-done((bf16[528,128]{1,0:T(8,128)(2,1)S(1)}, bf16[528,128]{1,0:T(8,128)(2,1)S(1)}, u32[]{:S(2)}, u32[]{:S(2)}) %collective-permute-start) | collective-permute-done | bytes 135200 | tf_op jit(solution)/shard_map/ppermute | solution.py:231
  18.9 2.4 %near.1 = (bf16[2,512,256]{2,1,0:T(8,128)(2,1)S(1)}, bf16[2,256,256]{2,1,0:T(8,128)(2,1)S(1)}, f32[3,5,128,128]{3,2,1,0:T(8,128)S(1)}, f32[8,128]{1,0:T(8,128)S(1)}) custom-call(s32[4,12]{1,0:T(4,128)} %cols_hbm.1, s32[4]{0:T(128)} %agg_hbm.3, bf16[4,12,128,128]{3,2,1,0:T(8,128)(2,1)} %a_hbm.1, bf16[528,128]{1,0:T(8,128)(2,1)S(1)} %pack.1.p_ref, ...), custom_call_target="tpu_custom_call" | custom-call | flops 200000000 | bytes 4000000 | tf_op jit(solution)/shard_map/near/pallas_call | solution.py:233
  21.4 1.5 %collective-permute-done.1.one_ref = bf16[528,128]{1,0:T(8,128)(2,1)S(1)} collective-permute-done((bf16[528,128]{1,0:T(8,128)(2,1)S(1)}, bf16[528,128]{1,0:T(8,128)(2,1)S(1)}, u32[]{:S(2)}, u32[]{:S(2)}) %collective-permute-start.1) | collective-permute-done | bytes 135200 | tf_op jit(solution)/shard_map/ppermute | solution.py:232
  22.9 0.7 %edge.1 = bf16[5,128,128]{2,1,0:T(8,128)(2,1)S(1)} custom-call(bf16[2,512,256]{2,1,0:T(8,128)(2,1)S(1)} %get-tuple-element.10.lhs_ref, bf16[2,256,256]{2,1,0:T(8,128)(2,1)S(1)} %get-tuple-element.11.left, f32[3,5,128,128]{3,2,1,0:T(8,128)S(1)} %get-tuple-element.12.near, f32[8,128]{1,0:T(8,128)S(1)} %get-tuple-element.9.side_ref, ...), custom_call_target="tpu_custom_call" | custom-call | tf_op jit(solution)/shard_map/edge/pallas_call | solution.py:257
  23.6 0.7 %collective-permute-start.2 = (bf16[5,128,128]{2,1,0:T(8,128)(2,1)S(1)}, bf16[5,128,128]{2,1,0:T(8,128)(2,1)S(1)}, u32[]{:S(2)}, u32[]{:S(2)}) collective-permute-start(bf16[5,128,128]{2,1,0:T(8,128)(2,1)S(1)} %edge.1), channel_id=1, source_target_pairs={{0,1020},{3,7},{4,0},{7,11},{8,4},{11,15},{12,8},{15,19},{16,12},{... | collective-permute-start | bytes 491528 | tf_op jit(solution)/shard_map/ppermute | solution.py:273
  24.3 0.7 %rest.1.sums_ref = bf16[4,15,32,128]{3,2,1,0:T(8,128)(2,1)S(1)} custom-call(bf16[2,512,256]{2,1,0:T(8,128)(2,1)S(1)} %get-tuple-element.10.lhs_ref, bf16[2,256,256]{2,1,0:T(8,128)(2,1)S(1)} %get-tuple-element.11.left, f32[3,5,128,128]{3,2,1,0:T(8,128)S(1)} %get-tuple-element.12.near, f32[8,128]{1,0:T(8,128)S(1)} %get-tuple-element.9.side_ref, ...), custom_call_target="tpu_custom_call" | custom-call | flops 200000000 | bytes 3000000 | tf_op jit(solution)/shard_map/rest/pallas_call | solution.py:274
  25.0 0.0 collective-permute-done.2.got_ref
  25.0 0.1 join.1
  25.1 25.2 %all_to_all.5.in_ref = bf16[4,15,32,128]{3,2,1,0:T(8,128)(2,1)S(1)} all-to-all(bf16[4,15,32,128]{3,2,1,0:T(8,128)(2,1)S(1)} %join.1), channel_id=1, replica_groups=mesh['rows'=256,'grp'=4] {'grp'}, dimensions={0} | all-to-all | bytes 983040 | tf_op jit(solution)/shard_map/all_to_all | solution.py:295
  50.3 0.8 %band.1 = f32[4,7,32,128]{3,2,1,0:T(8,128)} custom-call(bf16[4,15,32,128]{3,2,1,0:T(8,128)(2,1)S(1)} %all_to_all.5.in_ref), custom_call_target="tpu_custom_call" | custom-call | tf_op jit(solution)/shard_map/band/pallas_call | solution.py:296
Async XLA Ops:
  0.9 18.1 %collective-permute-start = (bf16[528,128]{1,0:T(8,128)(2,1)S(1)}, bf16[528,128]{1,0:T(8,128)(2,1)S(1)}, u32[]{:S(2)}, u32[]{:S(2)}) collective-permute-start(bf16[528,128]{1,0:T(8,128)(2,1)S(1)} %pack.1.p_ref), channel_id=1, source_target_pairs={{0,1},{1,0},{2,3},{3,2},{4,5},{5,4},{6,7},{7,6},{8,9},{9,8},{10,11... | collective-permute-start | bytes 405512 | tf_op jit(solution)/shard_map/ppermute | solution.py:231
  16.0 6.9 %collective-permute-start.1 = (bf16[528,128]{1,0:T(8,128)(2,1)S(1)}, bf16[528,128]{1,0:T(8,128)(2,1)S(1)}, u32[]{:S(2)}, u32[]{:S(2)}) collective-permute-start(bf16[528,128]{1,0:T(8,128)(2,1)S(1)} %pack.1.p_ref), channel_id=1, source_target_pairs={{0,1023},{1,2},{2,1},{3,4},{4,3},{5,6},{6,5},{7,8},{8,7},{9,10},{1... | collective-permute-start | bytes 405512 | tf_op jit(solution)/shard_map/ppermute | solution.py:232
  23.6 1.4 %collective-permute-start.2 = (bf16[5,128,128]{2,1,0:T(8,128)(2,1)S(1)}, bf16[5,128,128]{2,1,0:T(8,128)(2,1)S(1)}, u32[]{:S(2)}, u32[]{:S(2)}) collective-permute-start(bf16[5,128,128]{2,1,0:T(8,128)(2,1)S(1)} %edge.1), channel_id=1, source_target_pairs={{0,1020},{3,7},{4,0},{7,11},{8,4},{11,15},{12,8},{15,19},{16,12},{... | collective-permute-start | bytes 491528 | tf_op jit(solution)/shard_map/ppermute | solution.py:273

commit v4 on v3

--- a/solution.py
+++ b/solution.py
@@ -108,7 +108,7 @@
     left[1, :BS, BS:] = zero
     left[1, BS:, :BS] = (turned[2] * (1 - keep2)).astype(jnp.bfloat16)
     left[1, BS:, BS:] = turned[3].astype(jnp.bfloat16)
-    side_ref[...] = jnp.full((8, BS), (first + 1) & 3, jnp.int32).astype(jnp.float32)
+    side_ref[...] = jnp.full((8, BS), (first + 1) & 7, jnp.int32).astype(jnp.float32)
 
     cols_copy.wait()
     for r in range(RB):
@@ -137,26 +137,7 @@
                 lhs_ref[i, r * BS : (r + 1) * BS, c * BS : (c + 1) * BS] = tile
 
 
-def edge_kernel(lhs_ref, left, near, side_ref, one_ref, edge_ref, acc, weights):
-    clear_weights(weights)
-    for i in range(2):
-        fill_weights(weights.at[i], one_ref, 2 * i)
-    side = jnp.max(side_ref[...]).astype(jnp.int32)
-    h = side // 2
-    acc[...] = near[2 * h]
-    bits = halo_bits(one_ref)
-    rows = pl.ds(pl.multiple_of(h * 2 * BS, 2 * BS), 2 * BS)
-    part = left[h, pl.ds(pl.multiple_of(h * BS, BS), BS), :]
-    for i in range(2):
-        prod = jnp.dot(lhs_ref[i, rows, :], weights[i], preferred_element_type=jnp.float32)
-        sums = jnp.dot(part, prod.astype(jnp.bfloat16), preferred_element_type=jnp.float32)
-        slots = pair_slots(2 * (side & 1), 2 * i, bits)
-        for c in range(2):
-            acc[slots[c]] += sums[:, c * BS : (c + 1) * BS]
-    edge_ref[...] = acc[...].astype(jnp.bfloat16)
-
-
-def rest_kernel(lhs_ref, left, near, side_ref, one_ref, out_ref, acc, weights):
+def far_kernel(lhs_ref, left, near, side_ref, one_ref, out_ref, acc, weights):
     clear_weights(weights)
     for i in range(2):
         fill_weights(weights.at[i], one_ref, 2 * i)
@@ -172,37 +153,48 @@
                 out_ref[q, s * 5 + j] = block[q * 32 : (q + 1) * 32, :]
 
 
-def join_kernel(side_ref, got_ref, sums_ref, out_ref):
-    for side, base in ((0, 0), (3, 10)):
-        here = side_ref[:1, :] == side
-        for j in range(5):
-            for q in range(4):
-                new = got_ref[j, q * 32 : (q + 1) * 32, :].astype(jnp.float32)
-                old = sums_ref[q, base + j].astype(jnp.float32)
-                out_ref[q, base + j] = jnp.where(here, new, old).astype(jnp.bfloat16)
-    for q in range(4):
-        out_ref[q, 5:10] = sums_ref[q, 5:10]
-
-
-def band_kernel(in_ref, out_hbm, out_ref, sems):
+def split_kernel(side_ref, in_ref, down_ref, up_ref):
+    lower = side_ref[:1, :] < 4
+    for j in range(5):
+        after = in_ref[3, 10 + j].astype(jnp.float32)
+        before = in_ref[0, j].astype(jnp.float32)
+        down_ref[j] = jnp.where(lower, after, before).astype(jnp.bfloat16)
+        up_ref[j] = jnp.where(lower, before, after).astype(jnp.bfloat16)
+
+
+def band_kernel(in_ref, out_ref):
     def part(g, s, j):
         return in_ref[g, 5 * s + j].astype(jnp.float32)
 
-    copies = []
     for c in range(4):
         for j in range(7):
             terms = []
             if 1 <= j < 6:
                 terms.append(part(c, 1, j - 1))
-            if j < 5:
-                terms.append(part(c - 1, 2, j) if c > 0 else part(3, 2, j))
-            if j >= 2:
-                terms.append(part(c + 1, 0, j - 2) if c < 3 else part(0, 0, j - 2))
-            total = terms[0]
+            if j < 5 and c > 0:
+                terms.append(part(c - 1, 2, j))
+            if j >= 2 and c < 3:
+                terms.append(part(c + 1, 0, j - 2))
+            total = terms[0] if terms else jnp.zeros((32, BS), jnp.float32)
             for term in terms[1:]:
                 total = total + term
             out_ref[c, j] = total
-        copies.append(pltpu.make_async_copy(out_ref.at[c], out_hbm.at[c], sems.at[c]))
+
+
+def finish_kernel(side_ref, band_ref, up_ref, down_ref, out_hbm, rows_ref, sems):
+    middle = pltpu.make_async_copy(band_ref.at[pl.ds(1, 2)], out_hbm.at[pl.ds(1, 2)], sems.at[0])
+    middle.start()
+    lower = side_ref[:1, :] < 4
+    copies = [middle]
+    for i, (c, first) in enumerate(((0, 0), (3, 2))):
+        for j in range(7):
+            total = band_ref[c, j]
+            if first <= j < first + 5:
+                down = down_ref[j - first].astype(jnp.float32)
+                up = up_ref[j - first].astype(jnp.float32)
+                total = total + (jnp.where(lower, up, down) if c == 0 else jnp.where(lower, down, up))
+            rows_ref[i, j] = total
+        copies.append(pltpu.make_async_copy(rows_ref.at[i], out_hbm.at[c], sems.at[1 + i]))
         copies[-1].start()
     for copy in copies:
         copy.wait()
@@ -253,26 +245,8 @@
         cost_estimate=pl.CostEstimate(flops=2 * 10**8, bytes_accessed=4 * 10**6, transcendentals=0),
         name="near",
     )(a_cols, p_agg, a_tiles, packed, two)
-    far = (lhs, left, near, side, one)
-    edge = pl.pallas_call(
-        edge_kernel,
-        out_shape=jax.ShapeDtypeStruct((5, BS, BS), jnp.bfloat16),
-        in_specs=[VMEM] * 5,
-        out_specs=VMEM,
-        scratch_shapes=[
-            pltpu.VMEM((5, BS, BS), jnp.float32),
-            pltpu.VMEM((2, 2 * BS, 2 * BS), jnp.bfloat16),
-        ],
-        compiler_params=params,
-        name="edge",
-    )(*far)
-    cross = []
-    for i in range(0, count, 4):
-        cross.append((i, (i - 4) % count))
-        cross.append((i + 3, (i + 7) % count))
-    got = lax.ppermute(edge, axes, cross)
     sums = pl.pallas_call(
-        rest_kernel,
+        far_kernel,
         out_shape=jax.ShapeDtypeStruct((4, 15, 32, BS), jnp.bfloat16),
         in_specs=[VMEM] * 5,
         out_specs=VMEM,
@@ -281,30 +255,40 @@
             pltpu.VMEM((2, 2 * BS, 2 * BS), jnp.bfloat16),
         ],
         compiler_params=params,
-        cost_estimate=pl.CostEstimate(flops=2 * 10**8, bytes_accessed=3 * 10**6, transcendentals=0),
-        name="rest",
-    )(*far)
-    joined = pl.pallas_call(
-        join_kernel,
-        out_shape=jax.ShapeDtypeStruct((4, 15, 32, BS), jnp.bfloat16),
-        in_specs=[VMEM, VMEM, VMEM],
-        out_specs=VMEM,
-        compiler_params=params,
-        name="join",
-    )(side, got, sums)
-    parts = lax.all_to_all(joined, "grp", 0, 0, tiled=True)
-    return pl.pallas_call(
+        name="far",
+    )(lhs, left, near, side, one)
+    parts = lax.all_to_all(sums, "grp", 0, 0, tiled=True)
+    down, up = pl.pallas_call(
+        split_kernel,
+        out_shape=(jax.ShapeDtypeStruct((5, 32, BS), jnp.bfloat16),) * 2,
+        in_specs=[VMEM, VMEM],
+        out_specs=(VMEM, VMEM),
+        compiler_params=params,
+        name="split",
+    )(side, parts)
+    got_up = lax.ppermute(up, axes, [(i, (i + 4 if i & 4 else i - 4) % count) for i in range(count)])
+    got_down = lax.ppermute(down, axes, [(i, i ^ 4) for i in range(count)])
+    band = pl.pallas_call(
         band_kernel,
         out_shape=jax.ShapeDtypeStruct((4, 7, 32, BS), jnp.float32),
         in_specs=[VMEM],
+        out_specs=VMEM,
+        compiler_params=params,
+        cost_estimate=pl.CostEstimate(flops=10**7, bytes_accessed=2 * 10**6, transcendentals=0),
+        name="band",
+    )(parts)
+    return pl.pallas_call(
+        finish_kernel,
+        out_shape=jax.ShapeDtypeStruct((4, 7, 32, BS), jnp.float32),
+        in_specs=[VMEM] * 4,
         out_specs=HBM,
         scratch_shapes=[
-            pltpu.VMEM((4, 7, 32, BS), jnp.float32),
-            pltpu.SemaphoreType.DMA((4,)),
+            pltpu.VMEM((2, 7, 32, BS), jnp.float32),
+            pltpu.SemaphoreType.DMA((3,)),
         ],
         compiler_params=params,
-        name="band",
-    )(parts)
+        name="finish",
+    )(side, band, got_up, got_down)
 
 
 def solution(mesh):

time: 51.4 us -> 52.5 us (1.021)
  the two profiles are of different devices: /device:TPU:2 before, /device:TPU:1 now
where the time goes in v4:
time: 52.5 us; the launch traced here: 52.1 us
  starting transfers between devices  35.2 us (67%)
  blocking collectives  10.2 us (19%)
  Pallas kernels  4.87 us (9%)
  waiting for transfers between devices  1.71 us (3%)
    ppermute x1, starting transfers between devices, shards(): got_down = lax.ppermute(down, axes, [(i, i ^ 4) for i in range(count)])  19.5 us
    all_to_all x1, blocking collectives, shards(): parts = lax.all_to_all(sums, 'grp', 0, 0, tiled=True)  10.2 us
    ppermute x1, starting transfers between devices, shards(): lax.ppermute(up, axes, [(i, (i + 4 if i & 4 else i - 4) % count) for i in...  7.21 us
    ppermute x1, starting transfers between devices, shards(): lax.ppermute(packed, axes, [(i, (i + 1 if i % 2 else i - 1) % count) for...  4.56 us
    ppermute x1, starting transfers between devices, shards(): two = lax.ppermute(packed, axes, [(i, i ^ 1) for i in range(count)])  3.95 us
    pallas_call x1, Pallas kernels, shards(): pl.pallas_call(functools.partial(near_kernel, count), out_shape=(jax.Shap...  2.45 us
  transfers between devices with their start and end apart: 4, of which 2 were waited for; matrix products, arithmetic and copies ran while one was open for 0% of the time, Pallas kernels for 5%

profile of v4, /device:TPU:1, one launch (start us, length us, event | category | flops | bytes accessed | tf_op | source)
XLA Modules:
  0.0 52.1 jit_solution(14629693563191088718)
XLA Ops:
  0.0 0.9 %pack.1.p_ref = bf16[528,128]{1,0:T(8,128)(2,1)S(1)} custom-call(s32[4]{0:T(128)} %agg_hbm.3, bf16[4,128,128]{2,1,0:T(8,128)(2,1)} %p_hbm.1), custom_call_target="tpu_custom_call" | custom-call | tf_op jit(solution)/shard_map/pack/pallas_call | solution.py:210
  0.9 3.9 %collective-permute-start = (bf16[528,128]{1,0:T(8,128)(2,1)S(1)}, bf16[528,128]{1,0:T(8,128)(2,1)S(1)}, u32[]{:S(2)}, u32[]{:S(2)}) collective-permute-start(bf16[528,128]{1,0:T(8,128)(2,1)S(1)} %pack.1.p_ref), channel_id=1, source_target_pairs={{0,1},{1,0},{2,3},{3,2},{4,5},{5,4},{6,7},{7,6},{8,9},{9,8},{10,11... | collective-permute-start | bytes 405512 | tf_op jit(solution)/shard_map/ppermute | solution.py:223
  4.8 4.6 %collective-permute-start.1 = (bf16[528,128]{1,0:T(8,128)(2,1)S(1)}, bf16[528,128]{1,0:T(8,128)(2,1)S(1)}, u32[]{:S(2)}, u32[]{:S(2)}) collective-permute-start(bf16[528,128]{1,0:T(8,128)(2,1)S(1)} %pack.1.p_ref), channel_id=1, source_target_pairs={{0,1023},{1,2},{2,1},{3,4},{4,3},{5,6},{6,5},{7,8},{8,7},{9,10},{1... | collective-permute-start | bytes 405512 | tf_op jit(solution)/shard_map/ppermute | solution.py:224
  9.4 0.0 collective-permute-done.two_ref
  9.4 2.5 %near.1 = (bf16[2,512,256]{2,1,0:T(8,128)(2,1)S(1)}, bf16[2,256,256]{2,1,0:T(8,128)(2,1)S(1)}, f32[3,5,128,128]{3,2,1,0:T(8,128)S(1)}, f32[8,128]{1,0:T(8,128)S(1)}) custom-call(s32[4,12]{1,0:T(4,128)} %cols_hbm.1, s32[4]{0:T(128)} %agg_hbm.3, bf16[4,12,128,128]{3,2,1,0:T(8,128)(2,1)} %a_hbm.1, bf16[528,128]{1,0:T(8,128)(2,1)S(1)} %pack.1.p_ref, ...), custom_call_target="tpu_custom_call" | custom-call | flops 200000000 | bytes 4000000 | tf_op jit(solution)/shard_map/near/pallas_call | solution.py:225
  11.9 0.9 %collective-permute-done.1.one_ref = bf16[528,128]{1,0:T(8,128)(2,1)S(1)} collective-permute-done((bf16[528,128]{1,0:T(8,128)(2,1)S(1)}, bf16[528,128]{1,0:T(8,128)(2,1)S(1)}, u32[]{:S(2)}, u32[]{:S(2)}) %collective-permute-start.1) | collective-permute-done | bytes 135200 | tf_op jit(solution)/shard_map/ppermute | solution.py:224
  12.8 0.7 %far.1 = bf16[4,15,32,128]{3,2,1,0:T(8,128)(2,1)S(1)} custom-call(bf16[2,512,256]{2,1,0:T(8,128)(2,1)S(1)} %get-tuple-element.12.lhs_ref, bf16[2,256,256]{2,1,0:T(8,128)(2,1)S(1)} %get-tuple-element.13.left, f32[3,5,128,128]{3,2,1,0:T(8,128)S(1)} %get-tuple-element.14.near, f32[8,128]{1,0:T(8,128)S(1)} %get-tuple-element.11.side_ref, ...), custom_call_target="tpu_custom_call" | custom-call | tf_op jit(solution)/shard_map/far/pallas_call | solution.py:248
  13.5 10.2 %all_to_all.5.in_ref = bf16[4,15,32,128]{3,2,1,0:T(8,128)(2,1)S(1)} all-to-all(bf16[4,15,32,128]{3,2,1,0:T(8,128)(2,1)S(1)} %far.1), channel_id=1, replica_groups=mesh['rows'=256,'grp'=4] {'grp'}, dimensions={0} | all-to-all | bytes 983040 | tf_op jit(solution)/shard_map/all_to_all | solution.py:260
  23.8 7.2 %collective-permute-start.2 = (bf16[5,32,128]{2,1,0:T(8,128)(2,1)S(1)}, bf16[5,32,128]{2,1,0:T(8,128)(2,1)S(1)}, u32[]{:S(2)}, u32[]{:S(2)}) collective-permute-start(bf16[5,32,128]{2,1,0:T(8,128)(2,1)S(1)} %get-tuple-element.15), channel_id=1, source_target_pairs={{0,1020},{1,1021},{2,1022},{3,1023},{4,8},{5,9},{6,10},{7,11},{8,4... | collective-permute-start | bytes 122888 | tf_op jit(solution)/shard_map/ppermute | solution.py:269
  31.0 19.5 %collective-permute-start.3 = (bf16[5,32,128]{2,1,0:T(8,128)(2,1)S(1)}, bf16[5,32,128]{2,1,0:T(8,128)(2,1)S(1)}, u32[]{:S(2)}, u32[]{:S(2)}) collective-permute-start(bf16[5,32,128]{2,1,0:T(8,128)(2,1)S(1)} %get-tuple-element.16), channel_id=1, source_target_pairs={{0,4},{1,5},{2,6},{3,7},{4,0},{5,1},{6,2},{7,3},{8,12},{9,13},{10,... | collective-permute-start | bytes 122888 | tf_op jit(solution)/shard_map/ppermute | solution.py:270
  50.5 0.0 collective-permute-done.2.up_ref
  50.5 0.8 %collective-permute-done.3.down_ref = bf16[5,32,128]{2,1,0:T(8,128)(2,1)S(1)} collective-permute-done((bf16[5,32,128]{2,1,0:T(8,128)(2,1)S(1)}, bf16[5,32,128]{2,1,0:T(8,128)(2,1)S(1)}, u32[]{:S(2)}, u32[]{:S(2)}) %collective-permute-start.3) | collective-permute-done | bytes 40992 | tf_op jit(solution)/shard_map/ppermute | solution.py:270
  51.3 0.8 %finish.1 = f32[4,7,32,128]{3,2,1,0:T(8,128)} custom-call(f32[8,128]{1,0:T(8,128)S(1)} %get-tuple-element.11.side_ref, f32[4,7,32,128]{3,2,1,0:T(8,128)S(1)} %band.1.band_ref, bf16[5,32,128]{2,1,0:T(8,128)(2,1)S(1)} %collective-permute-done.2.up_ref, bf16[5,32,128]{2,1,0:T(8,128)(2,1)S(1)} %collective-permute-done.3.down_ref), custom_call_target="tpu_custom_call" | custom-call | tf_op jit(solution)/shard_map/finish/pallas_call | solution.py:280
  (2 shorter events, 0.1 us)
Async XLA Ops:
  0.9 8.5 %collective-permute-start = (bf16[528,128]{1,0:T(8,128)(2,1)S(1)}, bf16[528,128]{1,0:T(8,128)(2,1)S(1)}, u32[]{:S(2)}, u32[]{:S(2)}) collective-permute-start(bf16[528,128]{1,0:T(8,128)(2,1)S(1)} %pack.1.p_ref), channel_id=1, source_target_pairs={{0,1},{1,0},{2,3},{3,2},{4,5},{5,4},{6,7},{7,6},{8,9},{9,8},{10,11... | collective-permute-start | bytes 405512 | tf_op jit(solution)/shard_map/ppermute | solution.py:223
  4.8 8.0 %collective-permute-start.1 = (bf16[528,128]{1,0:T(8,128)(2,1)S(1)}, bf16[528,128]{1,0:T(8,128)(2,1)S(1)}, u32[]{:S(2)}, u32[]{:S(2)}) collective-permute-start(bf16[528,128]{1,0:T(8,128)(2,1)S(1)} %pack.1.p_ref), channel_id=1, source_target_pairs={{0,1023},{1,2},{2,1},{3,4},{4,3},{5,6},{6,5},{7,8},{8,7},{9,10},{1... | collective-permute-start | bytes 405512 | tf_op jit(solution)/shard_map/ppermute | solution.py:224
  23.8 26.8 %collective-permute-start.2 = (bf16[5,32,128]{2,1,0:T(8,128)(2,1)S(1)}, bf16[5,32,128]{2,1,0:T(8,128)(2,1)S(1)}, u32[]{:S(2)}, u32[]{:S(2)}) collective-permute-start(bf16[5,32,128]{2,1,0:T(8,128)(2,1)S(1)} %get-tuple-element.15), channel_id=1, source_target_pairs={{0,1020},{1,1021},{2,1022},{3,1023},{4,8},{5,9},{6,10},{7,11},{8,4... | collective-permute-start | bytes 122888 | tf_op jit(solution)/shard_map/ppermute | solution.py:269
  31.0 20.3 %collective-permute-start.3 = (bf16[5,32,128]{2,1,0:T(8,128)(2,1)S(1)}, bf16[5,32,128]{2,1,0:T(8,128)(2,1)S(1)}, u32[]{:S(2)}, u32[]{:S(2)}) collective-permute-start(bf16[5,32,128]{2,1,0:T(8,128)(2,1)S(1)} %get-tuple-element.16), channel_id=1, source_target_pairs={{0,4},{1,5},{2,6},{3,7},{4,0},{5,1},{6,2},{7,3},{8,12},{9,13},{10,... | collective-permute-start | bytes 122888 | tf_op jit(solution)/shard_map/ppermute | solution.py:270

commit v5 on v4

--- a/solution.py
+++ b/solution.py
@@ -78,7 +78,7 @@
 
 
 def near_kernel(
-    count, cols_hbm, agg_hbm, a_hbm, p_ref, two_ref, lhs_ref, left, acc, side_ref,
+    count, cols_hbm, agg_hbm, a_hbm, p_ref, one_ref, lhs_ref, left, acc, side_ref,
     cols_ref, agg_ref, place, tiles, weights, sems, a_sems,
 ):
     cols_copy = pltpu.make_async_copy(cols_hbm, cols_ref, sems.at[0])
@@ -90,10 +90,10 @@
         copy.start()
     clear_weights(weights)
     for i in range(4):
-        fill_weights(weights.at[i], (p_ref, two_ref)[i // 2], 2 * (i % 2))
+        fill_weights(weights.at[i], (p_ref, one_ref)[i // 2], 2 * (i % 2))
     acc[...] = jnp.zeros_like(acc)
     turned = [p_ref[r * BS : (r + 1) * BS, :].astype(jnp.float32).T for r in range(RB)]
-    two_bits = halo_bits(two_ref)
+    one_bits = halo_bits(one_ref)
     agg_copy.wait()
     first = agg_ref[0]
     low, high = row_bits(count, agg_ref)
@@ -120,7 +120,7 @@
     for copy in copies:
         copy.wait()
     for i in range(4):
-        start = (RB if i < 2 else inner) + 2 * (i % 2)
+        start = (RB if i < 2 else outer) + 2 * (i % 2)
         lhs = jnp.concatenate(
             [
                 jnp.concatenate([tiles[r, place[r, start + c]] for c in range(2)], axis=1)
@@ -128,24 +128,24 @@
             ],
             axis=0,
         )
-        n = 1 if i < 2 else 2 * (1 - odd)
-        add_pair(n, 2 * (i % 2), (low, high) if i < 2 else two_bits, lhs, weights.at[i], left, acc)
+        n = 1 if i < 2 else 2 * odd
+        add_pair(n, 2 * (i % 2), (low, high) if i < 2 else one_bits, lhs, weights.at[i], left, acc)
     for i in range(2):
         for r in range(RB):
             for c in range(2):
-                tile = tiles[r, place[r, outer + 2 * i + c]]
+                tile = tiles[r, place[r, inner + 2 * i + c]]
                 lhs_ref[i, r * BS : (r + 1) * BS, c * BS : (c + 1) * BS] = tile
 
 
-def far_kernel(lhs_ref, left, near, side_ref, one_ref, out_ref, acc, weights):
+def far_kernel(lhs_ref, left, near, side_ref, two_ref, out_ref, acc, weights):
     clear_weights(weights)
     for i in range(2):
-        fill_weights(weights.at[i], one_ref, 2 * i)
+        fill_weights(weights.at[i], two_ref, 2 * i)
     acc[...] = near[...]
     side = jnp.max(side_ref[...]).astype(jnp.int32)
-    bits = halo_bits(one_ref)
+    bits = halo_bits(two_ref)
     for i in range(2):
-        add_pair(2 * (side & 1), 2 * i, bits, lhs_ref[i], weights.at[i], left, acc)
+        add_pair(2 - 2 * (side & 1), 2 * i, bits, lhs_ref[i], weights.at[i], left, acc)
     for s in range(3):
         for j in range(5):
             block = acc[s, j].astype(jnp.bfloat16)
@@ -153,48 +153,48 @@
                 out_ref[q, s * 5 + j] = block[q * 32 : (q + 1) * 32, :]
 
 
-def split_kernel(side_ref, in_ref, down_ref, up_ref):
-    lower = side_ref[:1, :] < 4
-    for j in range(5):
-        after = in_ref[3, 10 + j].astype(jnp.float32)
-        before = in_ref[0, j].astype(jnp.float32)
-        down_ref[j] = jnp.where(lower, after, before).astype(jnp.bfloat16)
-        up_ref[j] = jnp.where(lower, before, after).astype(jnp.bfloat16)
-
-
-def band_kernel(in_ref, out_ref):
+def split_kernel(in_ref, up_ref, down_ref):
+    up_ref[...] = in_ref[3, 10:]
+    down_ref[...] = in_ref[0, :5]
+
+
+def band_kernel(in_ref, out_hbm, open_ref, rows_ref, sems):
     def part(g, s, j):
         return in_ref[g, 5 * s + j].astype(jnp.float32)
 
-    for c in range(4):
-        for j in range(7):
-            terms = []
-            if 1 <= j < 6:
-                terms.append(part(c, 1, j - 1))
-            if j < 5 and c > 0:
-                terms.append(part(c - 1, 2, j))
-            if j >= 2 and c < 3:
-                terms.append(part(c + 1, 0, j - 2))
-            total = terms[0] if terms else jnp.zeros((32, BS), jnp.float32)
-            for term in terms[1:]:
-                total = total + term
-            out_ref[c, j] = total
-
-
-def finish_kernel(side_ref, band_ref, up_ref, down_ref, out_hbm, rows_ref, sems):
-    middle = pltpu.make_async_copy(band_ref.at[pl.ds(1, 2)], out_hbm.at[pl.ds(1, 2)], sems.at[0])
-    middle.start()
-    lower = side_ref[:1, :] < 4
-    copies = [middle]
-    for i, (c, first) in enumerate(((0, 0), (3, 2))):
-        for j in range(7):
-            total = band_ref[c, j]
-            if first <= j < first + 5:
-                down = down_ref[j - first].astype(jnp.float32)
-                up = up_ref[j - first].astype(jnp.float32)
-                total = total + (jnp.where(lower, up, down) if c == 0 else jnp.where(lower, down, up))
-            rows_ref[i, j] = total
-        copies.append(pltpu.make_async_copy(rows_ref.at[i], out_hbm.at[c], sems.at[1 + i]))
+    def block(c, j):
+        terms = []
+        if 1 <= j < 6:
+            terms.append(part(c, 1, j - 1))
+        if j < 5 and c > 0:
+            terms.append(part(c - 1, 2, j))
+        if j >= 2 and c < 3:
+            terms.append(part(c + 1, 0, j - 2))
+        total = terms[0] if terms else jnp.zeros((32, BS), jnp.float32)
+        for term in terms[1:]:
+            total = total + term
+        return total
+
+    copies = []
+    for i, (c, js) in enumerate(((1, (0, 7)), (2, (0, 7)), (0, (5, 7)), (3, (0, 2)))):
+        for j in range(*js):
+            rows_ref[c, j] = block(c, j)
+        here = pl.ds(js[0], js[1] - js[0])
+        copies.append(pltpu.make_async_copy(rows_ref.at[c, here], out_hbm.at[c, here], sems.at[i]))
+        copies[-1].start()
+    for j in range(5):
+        open_ref[0, j] = block(0, j)
+        open_ref[1, j] = block(3, j + 2)
+    for copy in copies:
+        copy.wait()
+
+
+def finish_kernel(open_ref, up_ref, down_ref, band_hbm, out_hbm, rows_ref, sems):
+    del band_hbm
+    copies = []
+    for i, (got_ref, c, first) in enumerate(((up_ref, 0, 0), (down_ref, 3, 2))):
+        rows_ref[i] = open_ref[i] + got_ref[...].astype(jnp.float32)
+        copies.append(pltpu.make_async_copy(rows_ref.at[i], out_hbm.at[c, pl.ds(first, 5)], sems.at[i]))
         copies[-1].start()
     for copy in copies:
         copy.wait()
@@ -220,8 +220,8 @@
         compiler_params=params,
         name="pack",
     )(p_agg, p_tiles)
+    one = lax.ppermute(packed, axes, [(i, (i + 1 if i % 2 else i - 1) % count) for i in range(count)])
     two = lax.ppermute(packed, axes, [(i, i ^ 1) for i in range(count)])
-    one = lax.ppermute(packed, axes, [(i, (i + 1 if i % 2 else i - 1) % count) for i in range(count)])
     lhs, left, near, side = pl.pallas_call(
         functools.partial(near_kernel, count),
         out_shape=(
@@ -244,7 +244,7 @@
         compiler_params=params,
         cost_estimate=pl.CostEstimate(flops=2 * 10**8, bytes_accessed=4 * 10**6, transcendentals=0),
         name="near",
-    )(a_cols, p_agg, a_tiles, packed, two)
+    )(a_cols, p_agg, a_tiles, packed, one)
     sums = pl.pallas_call(
         far_kernel,
         out_shape=jax.ShapeDtypeStruct((4, 15, 32, BS), jnp.bfloat16),
@@ -256,23 +256,30 @@
         ],
         compiler_params=params,
         name="far",
-    )(lhs, left, near, side, one)
+    )(lhs, left, near, side, two)
     parts = lax.all_to_all(sums, "grp", 0, 0, tiled=True)
-    down, up = pl.pallas_call(
+    up, down = pl.pallas_call(
         split_kernel,
         out_shape=(jax.ShapeDtypeStruct((5, 32, BS), jnp.bfloat16),) * 2,
-        in_specs=[VMEM, VMEM],
+        in_specs=[VMEM],
         out_specs=(VMEM, VMEM),
         compiler_params=params,
         name="split",
-    )(side, parts)
-    got_up = lax.ppermute(up, axes, [(i, (i + 4 if i & 4 else i - 4) % count) for i in range(count)])
-    got_down = lax.ppermute(down, axes, [(i, i ^ 4) for i in range(count)])
-    band = pl.pallas_call(
+    )(parts)
+    got_up = lax.ppermute(up, axes, [(i, (i + 4) % count) for i in range(count)])
+    got_down = lax.ppermute(down, axes, [(i, (i - 4) % count) for i in range(count)])
+    band, unfinished = pl.pallas_call(
         band_kernel,
-        out_shape=jax.ShapeDtypeStruct((4, 7, 32, BS), jnp.float32),
+        out_shape=(
+            jax.ShapeDtypeStruct((4, 7, 32, BS), jnp.float32),
+            jax.ShapeDtypeStruct((2, 5, 32, BS), jnp.float32),
+        ),
         in_specs=[VMEM],
-        out_specs=VMEM,
+        out_specs=(HBM, VMEM),
+        scratch_shapes=[
+            pltpu.VMEM((4, 7, 32, BS), jnp.float32),
+            pltpu.SemaphoreType.DMA((4,)),
+        ],
         compiler_params=params,
         cost_estimate=pl.CostEstimate(flops=10**7, bytes_accessed=2 * 10**6, transcendentals=0),
         name="band",
@@ -280,15 +287,16 @@
     return pl.pallas_call(
         finish_kernel,
         out_shape=jax.ShapeDtypeStruct((4, 7, 32, BS), jnp.float32),
-        in_specs=[VMEM] * 4,
+        in_specs=[VMEM, VMEM, VMEM, HBM],
         out_specs=HBM,
-        scratch_shapes=[
-            pltpu.VMEM((2, 7, 32, BS), jnp.float32),
-            pltpu.SemaphoreType.DMA((3,)),
+        input_output_aliases={3: 0},
+        scratch_shapes=[
+            pltpu.VMEM((2, 5, 32, BS), jnp.float32),
+            pltpu.SemaphoreType.DMA((2,)),
         ],
         compiler_params=params,
         name="finish",
-    )(side, band, got_up, got_down)
+    )(unfinished, got_up, got_down, band)
 
 
 def solution(mesh):

time: 52.5 us -> 52.2 us (level)
  the two profiles are of different devices: /device:TPU:1 before, /device:TPU:2 now
where the time goes in v5:
time: 52.2 us; the launch traced here: 51.9 us
  starting transfers between devices  34.1 us (65%)
  blocking collectives  10.9 us (21%)
  Pallas kernels  5.47 us (10%)
  waiting for transfers between devices  1.39 us (3%)
    ppermute x1, starting transfers between devices, shards(): two = lax.ppermute(packed, axes, [(i, i ^ 1) for i in range(count)])  21.8 us
    all_to_all x1, blocking collectives, shards(): parts = lax.all_to_all(sums, 'grp', 0, 0, tiled=True)  10.9 us
    ppermute x1, starting transfers between devices, shards(): lax.ppermute(down, axes, [(i, (i - 4) % count) for i in range(count)])  6.96 us
    ppermute x1, starting transfers between devices, shards(): lax.ppermute(packed, axes, [(i, (i + 1 if i % 2 else i - 1) % count) for...  3.4 us
    pallas_call x1, Pallas kernels, shards(): pl.pallas_call(functools.partial(near_kernel, count), out_shape=(jax.Shap...  2.45 us
    ppermute x1, starting transfers between devices, shards(): lax.ppermute(up, axes, [(i, (i + 4) % count) for i in range(count)])  1.91 us
  transfers between devices with their start and end apart: 4, of which 2 were waited for; matrix products, arithmetic and copies ran while one was open for 0% of the time, Pallas kernels for 6%

profile of v5, /device:TPU:2, one launch (start us, length us, event | category | flops | bytes accessed | tf_op | source)
XLA Modules:
  0.0 51.9 jit_solution(18257131762308612986)
XLA Ops:
  0.0 0.9 %pack.1.p_ref = bf16[528,128]{1,0:T(8,128)(2,1)S(1)} custom-call(s32[4]{0:T(128)} %agg_hbm.3, bf16[4,128,128]{2,1,0:T(8,128)(2,1)} %p_hbm.1), custom_call_target="tpu_custom_call" | custom-call | tf_op jit(solution)/shard_map/pack/pallas_call | solution.py:210
  0.9 3.4 %collective-permute-start = (bf16[528,128]{1,0:T(8,128)(2,1)S(1)}, bf16[528,128]{1,0:T(8,128)(2,1)S(1)}, u32[]{:S(2)}, u32[]{:S(2)}) collective-permute-start(bf16[528,128]{1,0:T(8,128)(2,1)S(1)} %pack.1.p_ref), channel_id=1, source_target_pairs={{0,1023},{1,2},{2,1},{3,4},{4,3},{5,6},{6,5},{7,8},{8,7},{9,10},{1... | collective-permute-start | bytes 405512 | tf_op jit(solution)/shard_map/ppermute | solution.py:223
  4.3 21.8 %collective-permute-start.1 = (bf16[528,128]{1,0:T(8,128)(2,1)S(1)}, bf16[528,128]{1,0:T(8,128)(2,1)S(1)}, u32[]{:S(2)}, u32[]{:S(2)}) collective-permute-start(bf16[528,128]{1,0:T(8,128)(2,1)S(1)} %pack.1.p_ref), channel_id=1, source_target_pairs={{0,1},{1,0},{2,3},{3,2},{4,5},{5,4},{6,7},{7,6},{8,9},{9,8},{10,11... | collective-permute-start | bytes 405512 | tf_op jit(solution)/shard_map/ppermute | solution.py:224
  26.1 0.0 collective-permute-done.one_ref
  26.1 2.5 %near.1 = (bf16[2,512,256]{2,1,0:T(8,128)(2,1)S(1)}, bf16[2,256,256]{2,1,0:T(8,128)(2,1)S(1)}, f32[3,5,128,128]{3,2,1,0:T(8,128)S(1)}, f32[8,128]{1,0:T(8,128)S(1)}) custom-call(s32[4,12]{1,0:T(4,128)} %cols_hbm.1, s32[4]{0:T(128)} %agg_hbm.3, bf16[4,12,128,128]{3,2,1,0:T(8,128)(2,1)} %a_hbm.1, bf16[528,128]{1,0:T(8,128)(2,1)S(1)} %pack.1.p_ref, ...), custom_call_target="tpu_custom_call" | custom-call | flops 200000000 | bytes 4000000 | tf_op jit(solution)/shard_map/near/pallas_call | solution.py:225
  28.6 0.5 collective-permute-done.1.two_ref
  29.1 0.7 %far.1 = bf16[4,15,32,128]{3,2,1,0:T(8,128)(2,1)S(1)} custom-call(bf16[2,512,256]{2,1,0:T(8,128)(2,1)S(1)} %get-tuple-element.13.lhs_ref, bf16[2,256,256]{2,1,0:T(8,128)(2,1)S(1)} %get-tuple-element.14.left, f32[3,5,128,128]{3,2,1,0:T(8,128)S(1)} %get-tuple-element.15.near, f32[8,128]{1,0:T(8,128)S(1)} %get-tuple-element.16.side_ref, ...), custom_call_target="tpu_custom_call" | custom-call | tf_op jit(solution)/shard_map/far/pallas_call | solution.py:248
  29.8 10.9 %all_to_all.5.in_ref = bf16[4,15,32,128]{3,2,1,0:T(8,128)(2,1)S(1)} all-to-all(bf16[4,15,32,128]{3,2,1,0:T(8,128)(2,1)S(1)} %far.1), channel_id=1, replica_groups=mesh['rows'=256,'grp'=4] {'grp'}, dimensions={0} | all-to-all | bytes 983040 | tf_op jit(solution)/shard_map/all_to_all | solution.py:260
  40.7 1.9 %collective-permute-start.2 = (bf16[5,32,128]{2,1,0:T(8,128)(2,1)S(1)}, bf16[5,32,128]{2,1,0:T(8,128)(2,1)S(1)}, u32[]{:S(2)}, u32[]{:S(2)}) collective-permute-start(bf16[5,32,128]{2,1,0:T(8,128)(2,1)S(1)} %get-tuple-element.18), channel_id=1, source_target_pairs={{0,4},{1,5},{2,6},{3,7},{4,8},{5,9},{6,10},{7,11},{8,12},{9,13},{1... | collective-permute-start | bytes 122888 | tf_op jit(solution)/shard_map/ppermute | solution.py:269
  42.6 7.0 %collective-permute-start.3 = (bf16[5,32,128]{2,1,0:T(8,128)(2,1)S(1)}, bf16[5,32,128]{2,1,0:T(8,128)(2,1)S(1)}, u32[]{:S(2)}, u32[]{:S(2)}) collective-permute-start(bf16[5,32,128]{2,1,0:T(8,128)(2,1)S(1)} %get-tuple-element.19), channel_id=1, source_target_pairs={{0,1020},{1,1021},{2,1022},{3,1023},{4,0},{5,1},{6,2},{7,3},{8,4},... | collective-permute-start | bytes 122888 | tf_op jit(solution)/shard_map/ppermute | solution.py:270
  49.5 0.8 %band.1 = (f32[4,7,32,128]{3,2,1,0:T(8,128)}, f32[2,5,32,128]{3,2,1,0:T(8,128)S(1)}) custom-call(bf16[4,15,32,128]{3,2,1,0:T(8,128)(2,1)S(1)} %all_to_all.5.in_ref), custom_call_target="tpu_custom_call" | custom-call | flops 10000000 | bytes 2000000 | tf_op jit(solution)/shard_map/band/pallas_call | solution.py:271
  50.3 0.0 collective-permute-done.2.up_ref
  50.3 0.9 %collective-permute-done.3.down_ref = bf16[5,32,128]{2,1,0:T(8,128)(2,1)S(1)} collective-permute-done((bf16[5,32,128]{2,1,0:T(8,128)(2,1)S(1)}, bf16[5,32,128]{2,1,0:T(8,128)(2,1)S(1)}, u32[]{:S(2)}, u32[]{:S(2)}) %collective-permute-start.3) | collective-permute-done | bytes 40992 | tf_op jit(solution)/shard_map/ppermute | solution.py:270
  51.2 0.7 %finish.1 = f32[4,7,32,128]{3,2,1,0:T(8,128)} custom-call(f32[2,5,32,128]{3,2,1,0:T(8,128)S(1)} %get-tuple-element.17.open_ref, bf16[5,32,128]{2,1,0:T(8,128)(2,1)S(1)} %collective-permute-done.2.up_ref, bf16[5,32,128]{2,1,0:T(8,128)(2,1)S(1)} %collective-permute-done.3.down_ref, ...), custom_call_target="tpu_custom_call", output_to_operand_aliasing={{}: (3, {})} | custom-call | tf_op jit(solution)/shard_map/finish/pallas_call | solution.py:287
  (1 shorter events, 0.0 us)
Async XLA Ops:
  0.9 25.2 %collective-permute-start = (bf16[528,128]{1,0:T(8,128)(2,1)S(1)}, bf16[528,128]{1,0:T(8,128)(2,1)S(1)}, u32[]{:S(2)}, u32[]{:S(2)}) collective-permute-start(bf16[528,128]{1,0:T(8,128)(2,1)S(1)} %pack.1.p_ref), channel_id=1, source_target_pairs={{0,1023},{1,2},{2,1},{3,4},{4,3},{5,6},{6,5},{7,8},{8,7},{9,10},{1... | collective-permute-start | bytes 405512 | tf_op jit(solution)/shard_map/ppermute | solution.py:223
  4.3 24.8 %collective-permute-start.1 = (bf16[528,128]{1,0:T(8,128)(2,1)S(1)}, bf16[528,128]{1,0:T(8,128)(2,1)S(1)}, u32[]{:S(2)}, u32[]{:S(2)}) collective-permute-start(bf16[528,128]{1,0:T(8,128)(2,1)S(1)} %pack.1.p_ref), channel_id=1, source_target_pairs={{0,1},{1,0},{2,3},{3,2},{4,5},{5,4},{6,7},{7,6},{8,9},{9,8},{10,11... | collective-permute-start | bytes 405512 | tf_op jit(solution)/shard_map/ppermute | solution.py:224
  40.7 9.7 %collective-permute-start.2 = (bf16[5,32,128]{2,1,0:T(8,128)(2,1)S(1)}, bf16[5,32,128]{2,1,0:T(8,128)(2,1)S(1)}, u32[]{:S(2)}, u32[]{:S(2)}) collective-permute-start(bf16[5,32,128]{2,1,0:T(8,128)(2,1)S(1)} %get-tuple-element.18), channel_id=1, source_target_pairs={{0,4},{1,5},{2,6},{3,7},{4,8},{5,9},{6,10},{7,11},{8,12},{9,13},{1... | collective-permute-start | bytes 122888 | tf_op jit(solution)/shard_map/ppermute | solution.py:269
  42.6 8.6 %collective-permute-start.3 = (bf16[5,32,128]{2,1,0:T(8,128)(2,1)S(1)}, bf16[5,32,128]{2,1,0:T(8,128)(2,1)S(1)}, u32[]{:S(2)}, u32[]{:S(2)}) collective-permute-start(bf16[5,32,128]{2,1,0:T(8,128)(2,1)S(1)} %get-tuple-element.19), channel_id=1, source_target_pairs={{0,1020},{1,1021},{2,1022},{3,1023},{4,0},{5,1},{6,2},{7,3},{8,4},... | collective-permute-start | bytes 122888 | tf_op jit(solution)/shard_map/ppermute | solution.py:270

commit v6 on v3

--- a/solution.py
+++ b/solution.py
@@ -40,8 +40,38 @@
         copy.wait()
 
 
+def extend_kernel(count, cols_hbm, agg_hbm, a_hbm, p_ref, out_ref, cols_ref, agg_ref, place, sems, a_sems):
+    cols_copy = pltpu.make_async_copy(cols_hbm, cols_ref, sems.at[0])
+    agg_copy = pltpu.make_async_copy(agg_hbm, agg_ref, sems.at[1])
+    cols_copy.start()
+    agg_copy.start()
+    out_ref[:HALO, :] = p_ref[...]
+    agg_copy.wait()
+    cols_copy.wait()
+    first = agg_ref[0]
+    group_place = (first + 1) & 3
+    top = group_place // 2 * 2
+    base = (group_place & 1) * 2 * RB
+    for r in range(2):
+        for k in range(KT):
+            place[r, (cols_ref[top + r, k] - first * RB) & (RB * count - 1)] = k
+    copies = []
+    for r in range(2):
+        for c in range(RB):
+            copies.append(
+                pltpu.make_async_copy(
+                    a_hbm.at[top + r, place[r, base + c]],
+                    out_ref.at[pl.ds(HALO + (r * RB + c) * BS, BS)],
+                    a_sems.at[r * RB + c],
+                )
+            )
+            copies[-1].start()
+    for copy in copies:
+        copy.wait()
+
+
 def halo_bits(ref):
-    flags = ref[RB * BS :, :].astype(jnp.float32)
+    flags = ref[RB * BS : HALO, :].astype(jnp.float32)
     return (
         jnp.max(flags[:8, :]).astype(jnp.int32),
         jnp.max(flags[8:, :]).astype(jnp.int32),
@@ -78,7 +108,7 @@
 
 
 def near_kernel(
-    count, cols_hbm, agg_hbm, a_hbm, p_ref, two_ref, lhs_ref, left, acc, side_ref,
+    count, cols_hbm, agg_hbm, a_hbm, p_ref, two_ref, lhs_ref, left, acc, side_ref, edge_ref,
     cols_ref, agg_ref, place, tiles, weights, sems, a_sems,
 ):
     cols_copy = pltpu.make_async_copy(cols_hbm, cols_ref, sems.at[0])
@@ -135,36 +165,55 @@
             for c in range(2):
                 tile = tiles[r, place[r, outer + 2 * i + c]]
                 lhs_ref[i, r * BS : (r + 1) * BS, c * BS : (c + 1) * BS] = tile
-
-
-def edge_kernel(lhs_ref, left, near, side_ref, one_ref, edge_ref, acc, weights):
+    lower = side_ref[:1, :] < 2
+    for j in range(5):
+        edge_ref[j] = jnp.where(lower, acc[0, j], acc[2, j]).astype(jnp.bfloat16)
+
+
+def rest_kernel(lhs_ref, left, near, side_ref, p_ref, one_ref, out_ref, acc, weights):
     clear_weights(weights)
     for i in range(2):
         fill_weights(weights.at[i], one_ref, 2 * i)
-    side = jnp.max(side_ref[...]).astype(jnp.int32)
-    h = side // 2
-    acc[...] = near[2 * h]
-    bits = halo_bits(one_ref)
-    rows = pl.ds(pl.multiple_of(h * 2 * BS, 2 * BS), 2 * BS)
-    part = left[h, pl.ds(pl.multiple_of(h * BS, BS), BS), :]
-    for i in range(2):
-        prod = jnp.dot(lhs_ref[i, rows, :], weights[i], preferred_element_type=jnp.float32)
-        sums = jnp.dot(part, prod.astype(jnp.bfloat16), preferred_element_type=jnp.float32)
-        slots = pair_slots(2 * (side & 1), 2 * i, bits)
-        for c in range(2):
-            acc[slots[c]] += sums[:, c * BS : (c + 1) * BS]
-    edge_ref[...] = acc[...].astype(jnp.bfloat16)
-
-
-def rest_kernel(lhs_ref, left, near, side_ref, one_ref, out_ref, acc, weights):
-    clear_weights(weights)
-    for i in range(2):
-        fill_weights(weights.at[i], one_ref, 2 * i)
+        fill_weights(weights.at[2 + i], p_ref, 2 * i)
     acc[...] = near[...]
     side = jnp.max(side_ref[...]).astype(jnp.int32)
     bits = halo_bits(one_ref)
+    own_bits = halo_bits(p_ref)
+    before, after = side == 0, side == 3
+    top = jnp.where(before, 2 * BS, 0)
+    keep = (
+        jnp.where(before, bits[1], jnp.where(after, 1, 0)),
+        jnp.where(before, 1, jnp.where(after, 1 - bits[0], 0)),
+    )
+    part = jnp.concatenate(
+        [
+            (
+                one_ref[pl.ds(pl.multiple_of(top + r * BS, BS), BS), :].astype(jnp.float32).T
+                * keep[r].astype(jnp.float32)
+            ).astype(jnp.bfloat16)
+            for r in range(2)
+        ],
+        axis=1,
+    )
     for i in range(2):
         add_pair(2 * (side & 1), 2 * i, bits, lhs_ref[i], weights.at[i], left, acc)
+        rows = [
+            jnp.concatenate(
+                [
+                    one_ref[HALO + (r * RB + 2 * i + c) * BS : HALO + (r * RB + 2 * i + c + 1) * BS, :]
+                    for c in range(2)
+                ],
+                axis=1,
+            )
+            for r in range(2)
+        ]
+        prod = jnp.dot(
+            jnp.concatenate(rows, axis=0), weights[2 + i], preferred_element_type=jnp.float32
+        ).astype(jnp.bfloat16)
+        sums = jnp.dot(part, prod, preferred_element_type=jnp.float32)
+        slots = pair_slots(1, 2 * i, own_bits)
+        for c in range(2):
+            acc[1, slots[c]] += sums[:, c * BS : (c + 1) * BS]
     for s in range(3):
         for j in range(5):
             block = acc[s, j].astype(jnp.bfloat16)
@@ -229,17 +278,33 @@
         name="pack",
     )(p_agg, p_tiles)
     two = lax.ppermute(packed, axes, [(i, i ^ 1) for i in range(count)])
-    one = lax.ppermute(packed, axes, [(i, (i + 1 if i % 2 else i - 1) % count) for i in range(count)])
-    lhs, left, near, side = pl.pallas_call(
+    wide = pl.pallas_call(
+        functools.partial(extend_kernel, count),
+        out_shape=jax.ShapeDtypeStruct((HALO + 2 * RB * BS, BS), jnp.bfloat16),
+        in_specs=[HBM, HBM, HBM, VMEM],
+        out_specs=VMEM,
+        scratch_shapes=[
+            pltpu.SMEM((RB, KT), jnp.int32),
+            pltpu.SMEM((RB,), jnp.int32),
+            pltpu.SMEM((2, KT), jnp.int32),
+            pltpu.SemaphoreType.DMA((2,)),
+            pltpu.SemaphoreType.DMA((2 * RB,)),
+        ],
+        compiler_params=params,
+        name="extend",
+    )(a_cols, p_agg, a_tiles, packed)
+    one = lax.ppermute(wide, axes, [(i, (i + 1 if i % 2 else i - 1) % count) for i in range(count)])
+    lhs, left, near, side, edge = pl.pallas_call(
         functools.partial(near_kernel, count),
         out_shape=(
             jax.ShapeDtypeStruct((2, RB * BS, 2 * BS), jnp.bfloat16),
             jax.ShapeDtypeStruct((2, 2 * BS, 2 * BS), jnp.bfloat16),
             jax.ShapeDtypeStruct((3, 5, BS, BS), jnp.float32),
             jax.ShapeDtypeStruct((8, BS), jnp.float32),
+            jax.ShapeDtypeStruct((5, BS, BS), jnp.bfloat16),
         ),
         in_specs=[HBM, HBM, HBM, VMEM, VMEM],
-        out_specs=(VMEM, VMEM, VMEM, VMEM),
+        out_specs=(VMEM, VMEM, VMEM, VMEM, VMEM),
         scratch_shapes=[
             pltpu.SMEM((RB, KT), jnp.int32),
             pltpu.SMEM((RB,), jnp.int32),
@@ -250,22 +315,9 @@
             pltpu.SemaphoreType.DMA((RB,)),
         ],
         compiler_params=params,
-        cost_estimate=pl.CostEstimate(flops=2 * 10**8, bytes_accessed=4 * 10**6, transcendentals=0),
+        cost_estimate=pl.CostEstimate(flops=2 * 10**10, bytes_accessed=10**8, transcendentals=0),
         name="near",
     )(a_cols, p_agg, a_tiles, packed, two)
-    far = (lhs, left, near, side, one)
-    edge = pl.pallas_call(
-        edge_kernel,
-        out_shape=jax.ShapeDtypeStruct((5, BS, BS), jnp.bfloat16),
-        in_specs=[VMEM] * 5,
-        out_specs=VMEM,
-        scratch_shapes=[
-            pltpu.VMEM((5, BS, BS), jnp.float32),
-            pltpu.VMEM((2, 2 * BS, 2 * BS), jnp.bfloat16),
-        ],
-        compiler_params=params,
-        name="edge",
-    )(*far)
     cross = []
     for i in range(0, count, 4):
         cross.append((i, (i - 4) % count))
@@ -274,16 +326,16 @@
     sums = pl.pallas_call(
         rest_kernel,
         out_shape=jax.ShapeDtypeStruct((4, 15, 32, BS), jnp.bfloat16),
-        in_specs=[VMEM] * 5,
+        in_specs=[VMEM] * 6,
         out_specs=VMEM,
         scratch_shapes=[
             pltpu.VMEM((3, 5, BS, BS), jnp.float32),
-            pltpu.VMEM((2, 2 * BS, 2 * BS), jnp.bfloat16),
+            pltpu.VMEM((4, 2 * BS, 2 * BS), jnp.bfloat16),
         ],
         compiler_params=params,
         cost_estimate=pl.CostEstimate(flops=2 * 10**8, bytes_accessed=3 * 10**6, transcendentals=0),
         name="rest",
-    )(*far)
+    )(lhs, left, near, side, packed, one)
     joined = pl.pallas_call(
         join_kernel,
         out_shape=jax.ShapeDtypeStruct((4, 15, 32, BS), jnp.bfloat16),

time: 51.4 us -> 46.9 us (0.912)
  blocking collectives: 25.2 us -> 17.1 us
  waiting for transfers between devices: 2.52 us -> 4.6 us
  Pallas kernels: 5.64 us -> 7.02 us
    all_to_all x1, blocking collectives: 25.2 us -> 17.1 us  [shards(): parts = lax.all_to_all(joined, 'grp', 0, 0, tiled=True)]
    ppermute x1, waiting for transfers between devices: 1.47 us -> 4.6 us  [shards(): lax.ppermute(wide, axes, [(i, (i + 1 if i % 2 else i - 1) % count) for i...]
    ppermute x1, waiting for transfers between devices: 1.05 us -> 0.01 us  [shards(): two = lax.ppermute(packed, axes, [(i, i ^ 1) for i in range(count)])]
    pallas_call x1, Pallas kernels: 0.71 us -> 1.75 us  [shards(): pl.pallas_call(functools.partial(extend_kernel, count), out_shape=jax.Sha...]
  transfers between devices with their start and end apart: 3 -> 3, of which waited for: 2 -> 1; matrix products, arithmetic and copies ran while one was open for 0% -> 0% of each run, Pallas kernels for 6% -> 11%
where the time goes in v6:
time: 46.9 us; the launch traced here: 46.5 us
  starting transfers between devices  17.7 us (38%)
  blocking collectives  17.1 us (36%)
  Pallas kernels  7.02 us (15%)
  waiting for transfers between devices  4.6 us (10%)
    all_to_all x1, blocking collectives, shards(): parts = lax.all_to_all(joined, 'grp', 0, 0, tiled=True)  17.1 us
    ppermute x1, starting transfers between devices, shards(): two = lax.ppermute(packed, axes, [(i, i ^ 1) for i in range(count)])  15.1 us
    ppermute x1, waiting for transfers between devices, shards(): lax.ppermute(wide, axes, [(i, (i + 1 if i % 2 else i - 1) % count) for i...  4.6 us
    pallas_call x1, Pallas kernels, shards(): pl.pallas_call(functools.partial(near_kernel, count), out_shape=(jax.Shap...  2.49 us
    ppermute x1, starting transfers between devices, shards(): lax.ppermute(wide, axes, [(i, (i + 1 if i % 2 else i - 1) % count) for i...  1.92 us
    pallas_call x1, Pallas kernels, shards(): pl.pallas_call(functools.partial(extend_kernel, count), out_shape=jax.Sha...  1.75 us
    pallas_call x1, Pallas kernels, shards(): pl.pallas_call(rest_kernel, out_shape=jax.ShapeDtypeStruct((4, 15, 32, BS...  1.04 us
  transfers between devices with their start and end apart: 3, of which 1 were waited for; matrix products, arithmetic and copies ran while one was open for 0% of the time, Pallas kernels for 11%

profile of v6, /device:TPU:2, one launch (start us, length us, event | category | flops | bytes accessed | tf_op | source)
XLA Modules:
  0.0 46.5 jit_solution(11600461917137025161)
XLA Ops:
  0.0 0.9 %pack.1.p_ref = bf16[528,128]{1,0:T(8,128)(2,1)S(1)} custom-call(s32[4]{0:T(128)} %agg_hbm.5, bf16[4,128,128]{2,1,0:T(8,128)(2,1)} %p_hbm.1), custom_call_target="tpu_custom_call" | custom-call | tf_op jit(solution)/shard_map/pack/pallas_call | solution.py:267
  0.9 15.1 %collective-permute-start = (bf16[528,128]{1,0:T(8,128)(2,1)S(1)}, bf16[528,128]{1,0:T(8,128)(2,1)S(1)}, u32[]{:S(2)}, u32[]{:S(2)}) collective-permute-start(bf16[528,128]{1,0:T(8,128)(2,1)S(1)} %pack.1.p_ref), channel_id=1, source_target_pairs={{0,1},{1,0},{2,3},{3,2},{4,5},{5,4},{6,7},{7,6},{8,9},{9,8},{10,11... | collective-permute-start | bytes 405512 | tf_op jit(solution)/shard_map/ppermute | solution.py:280
  16.0 1.7 %extend.1 = bf16[1552,128]{1,0:T(8,128)(2,1)S(1)} custom-call(s32[4,12]{1,0:T(4,128)} %cols_hbm.3, s32[4]{0:T(128)} %agg_hbm.5, bf16[4,12,128,128]{3,2,1,0:T(8,128)(2,1)} %a_hbm.3, bf16[528,128]{1,0:T(8,128)(2,1)S(1)} %pack.1.p_ref), custom_call_target="tpu_custom_call" | custom-call | tf_op jit(solution)/shard_map/extend/pallas_call | solution.py:281
  17.7 1.9 %collective-permute-start.2 = (bf16[1552,128]{1,0:T(8,128)(2,1)S(1)}, bf16[1552,128]{1,0:T(8,128)(2,1)S(1)}, u32[]{:S(2)}, u32[]{:S(2)}) collective-permute-start(bf16[1552,128]{1,0:T(8,128)(2,1)S(1)} %extend.1), channel_id=1, source_target_pairs={{0,1023},{1,2},{2,1},{3,4},{4,3},{5,6},{6,5},{7,8},{8,7},{9,10},{1... | collective-permute-start | bytes 1191944 | tf_op jit(solution)/shard_map/ppermute | solution.py:296
  19.6 0.0 collective-permute-done.two_ref
  19.7 2.5 %near.1 = (bf16[2,512,256]{2,1,0:T(8,128)(2,1)S(1)}, bf16[2,256,256]{2,1,0:T(8,128)(2,1)S(1)}, f32[3,5,128,128]{3,2,1,0:T(8,128)S(1)}, f32[8,128]{1,0:T(8,128)S(1)}, bf16[5,128,128]{2,1,0:T(8,128)(2,1)S(1)}) custom-call(s32[4,12]{1,0:T(4,128)} %cols_hbm.3, s32[4]{0:T(128)} %agg_hbm.5, bf16[4,12,128,128]{3,2,1,0:T(8,128)(2,1)} %a_hbm.3, ...), custom_call_target="tpu_custom_call" | custom-call | flops 20000000000 | bytes 100000000 | tf_op jit(solution)/shard_map/near/pallas_call | solution.py:297
  22.2 0.7 %collective-permute-start.1 = (bf16[5,128,128]{2,1,0:T(8,128)(2,1)S(1)}, bf16[5,128,128]{2,1,0:T(8,128)(2,1)S(1)}, u32[]{:S(2)}, u32[]{:S(2)}) collective-permute-start(bf16[5,128,128]{2,1,0:T(8,128)(2,1)S(1)} %get-tuple-element.11), channel_id=1, source_target_pairs={{0,1020},{3,7},{4,0},{7,11},{8,4},{11,15},{12,8},{15,19},{16,12},{... | collective-permute-start | bytes 491528 | tf_op jit(solution)/shard_map/ppermute | solution.py:325
  22.8 4.6 %collective-permute-done.2.one_ref = bf16[1552,128]{1,0:T(8,128)(2,1)S(1)} collective-permute-done((bf16[1552,128]{1,0:T(8,128)(2,1)S(1)}, bf16[1552,128]{1,0:T(8,128)(2,1)S(1)}, u32[]{:S(2)}, u32[]{:S(2)}) %collective-permute-start.2) | collective-permute-done | bytes 397344 | tf_op jit(solution)/shard_map/ppermute | solution.py:296
  27.4 1.0 %rest.1.sums_ref = bf16[4,15,32,128]{3,2,1,0:T(8,128)(2,1)S(1)} custom-call(bf16[2,512,256]{2,1,0:T(8,128)(2,1)S(1)} %get-tuple-element.12.lhs_ref, bf16[2,256,256]{2,1,0:T(8,128)(2,1)S(1)} %get-tuple-element.13.left, f32[3,5,128,128]{3,2,1,0:T(8,128)S(1)} %get-tuple-element.14.near, f32[8,128]{1,0:T(8,128)S(1)} %get-tuple-element.10.side_ref, ...), custom_call_target="tpu_custom_call" | custom-call | flops 200000000 | bytes 3000000 | tf_op jit(solution)/shard_map/rest/pallas_call | solution.py:326
  28.5 0.0 collective-permute-done.1.got_ref
  28.5 0.1 join.1
  28.6 17.1 %all_to_all.5.in_ref = bf16[4,15,32,128]{3,2,1,0:T(8,128)(2,1)S(1)} all-to-all(bf16[4,15,32,128]{3,2,1,0:T(8,128)(2,1)S(1)} %join.1), channel_id=1, replica_groups=mesh['rows'=256,'grp'=4] {'grp'}, dimensions={0} | all-to-all | bytes 983040 | tf_op jit(solution)/shard_map/all_to_all | solution.py:347
  45.7 0.8 %band.1 = f32[4,7,32,128]{3,2,1,0:T(8,128)} custom-call(bf16[4,15,32,128]{3,2,1,0:T(8,128)(2,1)S(1)} %all_to_all.5.in_ref), custom_call_target="tpu_custom_call" | custom-call | tf_op jit(solution)/shard_map/band/pallas_call | solution.py:348
Async XLA Ops:
  0.9 18.8 %collective-permute-start = (bf16[528,128]{1,0:T(8,128)(2,1)S(1)}, bf16[528,128]{1,0:T(8,128)(2,1)S(1)}, u32[]{:S(2)}, u32[]{:S(2)}) collective-permute-start(bf16[528,128]{1,0:T(8,128)(2,1)S(1)} %pack.1.p_ref), channel_id=1, source_target_pairs={{0,1},{1,0},{2,3},{3,2},{4,5},{5,4},{6,7},{7,6},{8,9},{9,8},{10,11... | collective-permute-start | bytes 405512 | tf_op jit(solution)/shard_map/ppermute | solution.py:280
  17.7 9.7 %collective-permute-start.2 = (bf16[1552,128]{1,0:T(8,128)(2,1)S(1)}, bf16[1552,128]{1,0:T(8,128)(2,1)S(1)}, u32[]{:S(2)}, u32[]{:S(2)}) collective-permute-start(bf16[1552,128]{1,0:T(8,128)(2,1)S(1)} %extend.1), channel_id=1, source_target_pairs={{0,1023},{1,2},{2,1},{3,4},{4,3},{5,6},{6,5},{7,8},{8,7},{9,10},{1... | collective-permute-start | bytes 1191944 | tf_op jit(solution)/shard_map/ppermute | solution.py:296
  22.2 6.3 %collective-permute-start.1 = (bf16[5,128,128]{2,1,0:T(8,128)(2,1)S(1)}, bf16[5,128,128]{2,1,0:T(8,128)(2,1)S(1)}, u32[]{:S(2)}, u32[]{:S(2)}) collective-permute-start(bf16[5,128,128]{2,1,0:T(8,128)(2,1)S(1)} %get-tuple-element.11), channel_id=1, source_target_pairs={{0,1020},{3,7},{4,0},{7,11},{8,4},{11,15},{12,8},{15,19},{16,12},{... | collective-permute-start | bytes 491528 | tf_op jit(solution)/shard_map/ppermute | solution.py:325

commit v7 on v6

--- a/solution.py
+++ b/solution.py
@@ -40,93 +40,26 @@
         copy.wait()
 
 
-def extend_kernel(count, cols_hbm, agg_hbm, a_hbm, p_ref, out_ref, cols_ref, agg_ref, place, sems, a_sems):
-    cols_copy = pltpu.make_async_copy(cols_hbm, cols_ref, sems.at[0])
-    agg_copy = pltpu.make_async_copy(agg_hbm, agg_ref, sems.at[1])
-    cols_copy.start()
-    agg_copy.start()
-    out_ref[:HALO, :] = p_ref[...]
-    agg_copy.wait()
-    cols_copy.wait()
-    first = agg_ref[0]
-    group_place = (first + 1) & 3
-    top = group_place // 2 * 2
-    base = (group_place & 1) * 2 * RB
-    for r in range(2):
-        for k in range(KT):
-            place[r, (cols_ref[top + r, k] - first * RB) & (RB * count - 1)] = k
-    copies = []
-    for r in range(2):
-        for c in range(RB):
-            copies.append(
-                pltpu.make_async_copy(
-                    a_hbm.at[top + r, place[r, base + c]],
-                    out_ref.at[pl.ds(HALO + (r * RB + c) * BS, BS)],
-                    a_sems.at[r * RB + c],
-                )
-            )
-            copies[-1].start()
-    for copy in copies:
-        copy.wait()
-
-
-def halo_bits(ref):
-    flags = ref[RB * BS : HALO, :].astype(jnp.float32)
-    return (
-        jnp.max(flags[:8, :]).astype(jnp.int32),
-        jnp.max(flags[8:, :]).astype(jnp.int32),
-    )
-
-
-def fill_weights(w, tiles_ref, top):
-    w[:BS, :BS] = tiles_ref[top * BS : (top + 1) * BS, :]
-    w[BS:, BS:] = tiles_ref[(top + 1) * BS : (top + 2) * BS, :]
-
-
-def clear_weights(weights):
-    zero = jnp.zeros((BS, BS), jnp.bfloat16)
-    for i in range(weights.shape[0]):
-        weights[i, :BS, BS:] = zero
-        weights[i, BS:, :BS] = zero
-
-
-def add_pair(n, top, bits, lhs, w, left, acc):
-    prod = jnp.dot(lhs, w[...], preferred_element_type=jnp.float32).astype(jnp.bfloat16)
-    up = jnp.dot(left[0], prod[: 2 * BS], preferred_element_type=jnp.float32)
-    down = jnp.dot(left[1], prod[2 * BS :], preferred_element_type=jnp.float32)
-    slots = pair_slots(n, top, bits)
-    for c in range(2):
-        lanes = slice(c * BS, (c + 1) * BS)
-        acc[0, slots[c]] += up[:BS, lanes]
-        acc[1, slots[c]] += up[BS:, lanes] + down[:BS, lanes]
-        acc[2, slots[c]] += down[BS:, lanes]
-
-
-def pair_slots(n, top, bits):
-    b1, b2 = bits
-    return (n, n + b1) if top == 0 else (n + 1 + b2, n + 2)
-
-
-def near_kernel(
-    count, cols_hbm, agg_hbm, a_hbm, p_ref, two_ref, lhs_ref, left, acc, side_ref, edge_ref,
-    cols_ref, agg_ref, place, tiles, weights, sems, a_sems,
+def extend_kernel(
+    count, cols_hbm, agg_hbm, a_hbm, p_ref, out_ref, lhs_ref, left, side_ref,
+    cols_ref, agg_ref, place, tiles, sems, a_sems,
 ):
     cols_copy = pltpu.make_async_copy(cols_hbm, cols_ref, sems.at[0])
     agg_copy = pltpu.make_async_copy(agg_hbm, agg_ref, sems.at[1])
     cols_copy.start()
     agg_copy.start()
-    copies = [pltpu.make_async_copy(a_hbm.at[r], tiles.at[r], a_sems.at[r]) for r in range(RB)]
+    copies = [
+        pltpu.make_async_copy(a_hbm.at[r, pl.ds(6 * h, 6)], tiles.at[r, pl.ds(6 * h, 6)], a_sems.at[r, h])
+        for r in range(RB)
+        for h in range(2)
+    ]
     for copy in copies:
         copy.start()
-    clear_weights(weights)
-    for i in range(4):
-        fill_weights(weights.at[i], (p_ref, two_ref)[i // 2], 2 * (i % 2))
-    acc[...] = jnp.zeros_like(acc)
-    turned = [p_ref[r * BS : (r + 1) * BS, :].astype(jnp.float32).T for r in range(RB)]
-    two_bits = halo_bits(two_ref)
+    out_ref[:HALO, :] = p_ref[...]
     agg_copy.wait()
     first = agg_ref[0]
     low, high = row_bits(count, agg_ref)
+    turned = [p_ref[r * BS : (r + 1) * BS, :].astype(jnp.float32).T for r in range(RB)]
     zero = jnp.zeros((BS, BS), jnp.bfloat16)
     keep1 = (low == 0).astype(jnp.float32)
     keep2 = (high == 0).astype(jnp.float32)
@@ -138,8 +71,8 @@
     left[1, :BS, BS:] = zero
     left[1, BS:, :BS] = (turned[2] * (1 - keep2)).astype(jnp.bfloat16)
     left[1, BS:, BS:] = turned[3].astype(jnp.bfloat16)
-    side_ref[...] = jnp.full((8, BS), (first + 1) & 3, jnp.int32).astype(jnp.float32)
-
+    group_place = (first + 1) & 3
+    side_ref[...] = jnp.full((8, BS), group_place, jnp.int32).astype(jnp.float32)
     cols_copy.wait()
     for r in range(RB):
         for k in range(KT):
@@ -149,25 +82,68 @@
     outer = odd * 2 * RB
     for copy in copies:
         copy.wait()
-    for i in range(4):
-        start = (RB if i < 2 else inner) + 2 * (i % 2)
-        lhs = jnp.concatenate(
-            [
-                jnp.concatenate([tiles[r, place[r, start + c]] for c in range(2)], axis=1)
-                for r in range(RB)
-            ],
-            axis=0,
-        )
-        n = 1 if i < 2 else 2 * (1 - odd)
-        add_pair(n, 2 * (i % 2), (low, high) if i < 2 else two_bits, lhs, weights.at[i], left, acc)
-    for i in range(2):
+    for i in range(6):
+        start = (RB, inner, outer)[i // 2] + 2 * (i % 2)
         for r in range(RB):
             for c in range(2):
-                tile = tiles[r, place[r, outer + 2 * i + c]]
-                lhs_ref[i, r * BS : (r + 1) * BS, c * BS : (c + 1) * BS] = tile
+                lhs_ref[i, r * BS : (r + 1) * BS, c * BS : (c + 1) * BS] = tiles[r, place[r, start + c]]
+    top = group_place // 2 * 2
+    for r in range(2):
+        for c in range(RB):
+            to = HALO + (r * RB + c) * BS
+            out_ref[to : to + BS, :] = tiles[top + r, place[top + r, outer + c]]
+
+
+def halo_bits(ref):
+    flags = ref[RB * BS : HALO, :].astype(jnp.float32)
+    return (
+        jnp.max(flags[:8, :]).astype(jnp.int32),
+        jnp.max(flags[8:, :]).astype(jnp.int32),
+    )
+
+
+def fill_weights(w, tiles_ref, top):
+    w[:BS, :BS] = tiles_ref[top * BS : (top + 1) * BS, :]
+    w[BS:, BS:] = tiles_ref[(top + 1) * BS : (top + 2) * BS, :]
+
+
+def clear_weights(weights):
+    zero = jnp.zeros((BS, BS), jnp.bfloat16)
+    for i in range(weights.shape[0]):
+        weights[i, :BS, BS:] = zero
+        weights[i, BS:, :BS] = zero
+
+
+def add_pair(n, top, bits, lhs, w, left, acc):
+    prod = jnp.dot(lhs, w[...], preferred_element_type=jnp.float32).astype(jnp.bfloat16)
+    up = jnp.dot(left[0], prod[: 2 * BS], preferred_element_type=jnp.float32)
+    down = jnp.dot(left[1], prod[2 * BS :], preferred_element_type=jnp.float32)
+    slots = pair_slots(n, top, bits)
+    for c in range(2):
+        lanes = slice(c * BS, (c + 1) * BS)
+        acc[0, slots[c]] += up[:BS, lanes]
+        acc[1, slots[c]] += up[BS:, lanes] + down[:BS, lanes]
+        acc[2, slots[c]] += down[BS:, lanes]
+
+
+def pair_slots(n, top, bits):
+    b1, b2 = bits
+    return (n, n + b1) if top == 0 else (n + 1 + b2, n + 2)
+
+
+def near_kernel(lhs_ref, left, side_ref, p_ref, two_ref, acc, edge_ref, weights):
+    clear_weights(weights)
+    for i in range(4):
+        fill_weights(weights.at[i], (p_ref, two_ref)[i // 2], 2 * (i % 2))
+    acc[...] = jnp.zeros_like(acc)
+    side = jnp.max(side_ref[...]).astype(jnp.int32)
+    own_bits, two_bits = halo_bits(p_ref), halo_bits(two_ref)
+    for i in range(4):
+        n = 1 if i < 2 else 2 - 2 * (side & 1)
+        add_pair(n, 2 * (i % 2), own_bits if i < 2 else two_bits, lhs_ref[i], weights.at[i], left, acc)
     lower = side_ref[:1, :] < 2
-    for j in range(5):
-        edge_ref[j] = jnp.where(lower, acc[0, j], acc[2, j]).astype(jnp.bfloat16)
+    for j in range(4):
+        edge_ref[j] = jnp.where(lower, acc[0, j + 1], acc[2, j]).astype(jnp.bfloat16)
 
 
 def rest_kernel(lhs_ref, left, near, side_ref, p_ref, one_ref, out_ref, acc, weights):
@@ -196,7 +172,7 @@
         axis=1,
     )
     for i in range(2):
-        add_pair(2 * (side & 1), 2 * i, bits, lhs_ref[i], weights.at[i], left, acc)
+        add_pair(2 * (side & 1), 2 * i, bits, lhs_ref[4 + i], weights.at[i], left, acc)
         rows = [
             jnp.concatenate(
                 [
@@ -222,12 +198,15 @@
 
 
 def join_kernel(side_ref, got_ref, sums_ref, out_ref):
-    for side, base in ((0, 0), (3, 10)):
+    for side, base, shift in ((0, 0, 1), (3, 10, 0)):
         here = side_ref[:1, :] == side
         for j in range(5):
             for q in range(4):
-                new = got_ref[j, q * 32 : (q + 1) * 32, :].astype(jnp.float32)
                 old = sums_ref[q, base + j].astype(jnp.float32)
+                if 0 <= j - shift < 4:
+                    new = got_ref[j - shift, q * 32 : (q + 1) * 32, :].astype(jnp.float32)
+                else:
+                    new = jnp.zeros_like(old)
                 out_ref[q, base + j] = jnp.where(here, new, old).astype(jnp.bfloat16)
     for q in range(4):
         out_ref[q, 5:10] = sums_ref[q, 5:10]
@@ -251,8 +230,11 @@
             for term in terms[1:]:
                 total = total + term
             out_ref[c, j] = total
-        copies.append(pltpu.make_async_copy(out_ref.at[c], out_hbm.at[c], sems.at[c]))
-        copies[-1].start()
+            if j in (2, 6):
+                here = pl.ds(0, 3) if j == 2 else pl.ds(3, 4)
+                sem = sems.at[2 * c + j // 6]
+                copies.append(pltpu.make_async_copy(out_ref.at[c, here], out_hbm.at[c, here], sem))
+                copies[-1].start()
     for copy in copies:
         copy.wait()
 
@@ -278,46 +260,41 @@
         name="pack",
     )(p_agg, p_tiles)
     two = lax.ppermute(packed, axes, [(i, i ^ 1) for i in range(count)])
-    wide = pl.pallas_call(
+    wide, lhs, left, side = pl.pallas_call(
         functools.partial(extend_kernel, count),
-        out_shape=jax.ShapeDtypeStruct((HALO + 2 * RB * BS, BS), jnp.bfloat16),
+        out_shape=(
+            jax.ShapeDtypeStruct((HALO + 2 * RB * BS, BS), jnp.bfloat16),
+            jax.ShapeDtypeStruct((6, RB * BS, 2 * BS), jnp.bfloat16),
+            jax.ShapeDtypeStruct((2, 2 * BS, 2 * BS), jnp.bfloat16),
+            jax.ShapeDtypeStruct((8, BS), jnp.float32),
+        ),
         in_specs=[HBM, HBM, HBM, VMEM],
-        out_specs=VMEM,
-        scratch_shapes=[
-            pltpu.SMEM((RB, KT), jnp.int32),
-            pltpu.SMEM((RB,), jnp.int32),
-            pltpu.SMEM((2, KT), jnp.int32),
-            pltpu.SemaphoreType.DMA((2,)),
-            pltpu.SemaphoreType.DMA((2 * RB,)),
-        ],
-        compiler_params=params,
-        name="extend",
-    )(a_cols, p_agg, a_tiles, packed)
-    one = lax.ppermute(wide, axes, [(i, (i + 1 if i % 2 else i - 1) % count) for i in range(count)])
-    lhs, left, near, side, edge = pl.pallas_call(
-        functools.partial(near_kernel, count),
-        out_shape=(
-            jax.ShapeDtypeStruct((2, RB * BS, 2 * BS), jnp.bfloat16),
-            jax.ShapeDtypeStruct((2, 2 * BS, 2 * BS), jnp.bfloat16),
-            jax.ShapeDtypeStruct((3, 5, BS, BS), jnp.float32),
-            jax.ShapeDtypeStruct((8, BS), jnp.float32),
-            jax.ShapeDtypeStruct((5, BS, BS), jnp.bfloat16),
-        ),
-        in_specs=[HBM, HBM, HBM, VMEM, VMEM],
-        out_specs=(VMEM, VMEM, VMEM, VMEM, VMEM),
+        out_specs=(VMEM, VMEM, VMEM, VMEM),
         scratch_shapes=[
             pltpu.SMEM((RB, KT), jnp.int32),
             pltpu.SMEM((RB,), jnp.int32),
             pltpu.SMEM((RB, KT), jnp.int32),
             pltpu.VMEM((RB, KT, BS, BS), jnp.bfloat16),
-            pltpu.VMEM((4, 2 * BS, 2 * BS), jnp.bfloat16),
             pltpu.SemaphoreType.DMA((2,)),
-            pltpu.SemaphoreType.DMA((RB,)),
-        ],
+            pltpu.SemaphoreType.DMA((RB, 2)),
+        ],
+        compiler_params=params,
+        name="extend",
+    )(a_cols, p_agg, a_tiles, packed)
+    one = lax.ppermute(wide, axes, [(i, (i + 1 if i % 2 else i - 1) % count) for i in range(count)])
+    near, edge = pl.pallas_call(
+        near_kernel,
+        out_shape=(
+            jax.ShapeDtypeStruct((3, 5, BS, BS), jnp.float32),
+            jax.ShapeDtypeStruct((4, BS, BS), jnp.bfloat16),
+        ),
+        in_specs=[VMEM] * 5,
+        out_specs=(VMEM, VMEM),
+        scratch_shapes=[pltpu.VMEM((4, 2 * BS, 2 * BS), jnp.bfloat16)],
         compiler_params=params,
         cost_estimate=pl.CostEstimate(flops=2 * 10**10, bytes_accessed=10**8, transcendentals=0),
         name="near",
-    )(a_cols, p_agg, a_tiles, packed, two)
+    )(lhs, left, side, packed, two)
     cross = []
     for i in range(0, count, 4):
         cross.append((i, (i - 4) % count))
@@ -352,7 +329,7 @@
         out_specs=HBM,
         scratch_shapes=[
             pltpu.VMEM((4, 7, 32, BS), jnp.float32),
-            pltpu.SemaphoreType.DMA((4,)),
+            pltpu.SemaphoreType.DMA((8,)),
         ],
         compiler_params=params,
         name="band",

time: 46.9 us -> 45.3 us (0.966)
  blocking collectives: 17.1 us -> 15.5 us
  waiting for transfers between devices: 4.6 us -> 6.09 us
  Pallas kernels: 7.02 us -> 5.68 us
    all_to_all x1, blocking collectives: 17.1 us -> 15.5 us  [shards(): parts = lax.all_to_all(joined, 'grp', 0, 0, tiled=True)]
    ppermute x1, waiting for transfers between devices: 4.6 us -> 6.09 us  [shards(): lax.ppermute(wide, axes, [(i, (i + 1 if i % 2 else i - 1) % count) for i...]
    pallas_call x2, Pallas kernels: 4.24 us -> 2.88 us  [the longest x1 1.88 us: shards(): pl.pallas_call(functools.partial(extend_kernel, count), out_shape=(jax.Sh...]
  transfers between devices with their start and end apart: 3 -> 3, of which waited for: 1 -> 1; matrix products, arithmetic and copies ran while one was open for 0% -> 0% of each run, Pallas kernels for 11% -> 9%
where the time goes in v7:
time: 45.3 us; the launch traced here: 45 us
  starting transfers between devices  17.7 us (39%)
  blocking collectives  15.5 us (34%)
  waiting for transfers between devices  6.09 us (13%)
  Pallas kernels  5.68 us (13%)
    all_to_all x1, blocking collectives, shards(): parts = lax.all_to_all(joined, 'grp', 0, 0, tiled=True)  15.5 us
    ppermute x1, starting transfers between devices, shards(): two = lax.ppermute(packed, axes, [(i, i ^ 1) for i in range(count)])  15.1 us
    ppermute x1, waiting for transfers between devices, shards(): lax.ppermute(wide, axes, [(i, (i + 1 if i % 2 else i - 1) % count) for i...  6.09 us
    ppermute x1, starting transfers between devices, shards(): lax.ppermute(wide, axes, [(i, (i + 1 if i % 2 else i - 1) % count) for i...  1.92 us
    pallas_call x1, Pallas kernels, shards(): pl.pallas_call(functools.partial(extend_kernel, count), out_shape=(jax.Sh...  1.88 us
    pallas_call x1, Pallas kernels, shards(): pl.pallas_call(rest_kernel, out_shape=jax.ShapeDtypeStruct((4, 15, 32, BS...  1.03 us
    pallas_call x1, Pallas kernels, shards(): pl.pallas_call(near_kernel, out_shape=(jax.ShapeDtypeStruct((3, 5, BS, BS...  1 us
  transfers between devices with their start and end apart: 3, of which 1 were waited for; matrix products, arithmetic and copies ran while one was open for 0% of the time, Pallas kernels for 9%

profile of v7, /device:TPU:2, one launch (start us, length us, event | category | flops | bytes accessed | tf_op | source)
XLA Modules:
  0.0 45.0 jit_solution(2116011636361075405)
XLA Ops:
  0.0 0.9 %pack.1.p_ref = bf16[528,128]{1,0:T(8,128)(2,1)S(1)} custom-call(s32[4]{0:T(128)} %agg_hbm.3, bf16[4,128,128]{2,1,0:T(8,128)(2,1)} %p_hbm.1), custom_call_target="tpu_custom_call" | custom-call | tf_op jit(solution)/shard_map/pack/pallas_call | solution.py:249
  0.9 15.1 %collective-permute-start = (bf16[528,128]{1,0:T(8,128)(2,1)S(1)}, bf16[528,128]{1,0:T(8,128)(2,1)S(1)}, u32[]{:S(2)}, u32[]{:S(2)}) collective-permute-start(bf16[528,128]{1,0:T(8,128)(2,1)S(1)} %pack.1.p_ref), channel_id=1, source_target_pairs={{0,1},{1,0},{2,3},{3,2},{4,5},{5,4},{6,7},{7,6},{8,9},{9,8},{10,11... | collective-permute-start | bytes 405512 | tf_op jit(solution)/shard_map/ppermute | solution.py:262
  16.0 1.9 %extend.1 = (bf16[1552,128]{1,0:T(8,128)(2,1)S(1)}, bf16[6,512,256]{2,1,0:T(8,128)(2,1)S(1)}, bf16[2,256,256]{2,1,0:T(8,128)(2,1)S(1)}, f32[8,128]{1,0:T(8,128)S(1)}) custom-call(s32[4,12]{1,0:T(4,128)} %cols_hbm.1, s32[4]{0:T(128)} %agg_hbm.3, bf16[4,12,128,128]{3,2,1,0:T(8,128)(2,1)} %a_hbm.1, bf16[528,128]{1,0:T(8,128)(2,1)S(1)} %pack.1.p_ref), custom_call_target="tpu_custom_call" | custom-call | tf_op jit(solution)/shard_map/extend/pallas_call | solution.py:263
  17.8 1.9 %collective-permute-start.2 = (bf16[1552,128]{1,0:T(8,128)(2,1)S(1)}, bf16[1552,128]{1,0:T(8,128)(2,1)S(1)}, u32[]{:S(2)}, u32[]{:S(2)}) collective-permute-start(bf16[1552,128]{1,0:T(8,128)(2,1)S(1)} %get-tuple-element.16), channel_id=1, source_target_pairs={{0,1023},{1,2},{2,1},{3,4},{4,3},{5,6},{6,5},{7,8},{8,7},{9,10},{1... | collective-permute-start | bytes 1191944 | tf_op jit(solution)/shard_map/ppermute | solution.py:284
  19.8 0.0 collective-permute-done.two_ref
  19.8 1.0 %near.1 = (f32[3,5,128,128]{3,2,1,0:T(8,128)S(1)}, bf16[4,128,128]{2,1,0:T(8,128)(2,1)S(1)}) custom-call(bf16[6,512,256]{2,1,0:T(8,128)(2,1)S(1)} %get-tuple-element.12.lhs_ref, bf16[2,256,256]{2,1,0:T(8,128)(2,1)S(1)} %get-tuple-element.13.left, f32[8,128]{1,0:T(8,128)S(1)} %get-tuple-element.11.side_ref, bf16[528,128]{1,0:T(8,128)(2,1)S(1)} %pack.1.p_ref, ...), custom_call_target="tpu_custom_call" | custom-call | flops 20000000000 | bytes 100000000 | tf_op jit(solution)/shard_map/near/pallas_call | solution.py:285
  20.8 0.7 %collective-permute-start.1 = (bf16[4,128,128]{2,1,0:T(8,128)(2,1)S(1)}, bf16[4,128,128]{2,1,0:T(8,128)(2,1)S(1)}, u32[]{:S(2)}, u32[]{:S(2)}) collective-permute-start(bf16[4,128,128]{2,1,0:T(8,128)(2,1)S(1)} %get-tuple-element.14), channel_id=1, source_target_pairs={{0,1020},{3,7},{4,0},{7,11},{8,4},{11,15},{12,8},{15,19},{16,12},{... | collective-permute-start | bytes 393224 | tf_op jit(solution)/shard_map/ppermute | solution.py:302
  21.5 6.1 %collective-permute-done.2.one_ref = bf16[1552,128]{1,0:T(8,128)(2,1)S(1)} collective-permute-done((bf16[1552,128]{1,0:T(8,128)(2,1)S(1)}, bf16[1552,128]{1,0:T(8,128)(2,1)S(1)}, u32[]{:S(2)}, u32[]{:S(2)}) %collective-permute-start.2) | collective-permute-done | bytes 397344 | tf_op jit(solution)/shard_map/ppermute | solution.py:284
  27.6 1.0 %rest.1.sums_ref = bf16[4,15,32,128]{3,2,1,0:T(8,128)(2,1)S(1)} custom-call(bf16[6,512,256]{2,1,0:T(8,128)(2,1)S(1)} %get-tuple-element.12.lhs_ref, bf16[2,256,256]{2,1,0:T(8,128)(2,1)S(1)} %get-tuple-element.13.left, f32[3,5,128,128]{3,2,1,0:T(8,128)S(1)} %get-tuple-element.15.near, f32[8,128]{1,0:T(8,128)S(1)} %get-tuple-element.11.side_ref, ...), custom_call_target="tpu_custom_call" | custom-call | flops 200000000 | bytes 3000000 | tf_op jit(solution)/shard_map/rest/pallas_call | solution.py:303
  28.6 0.0 collective-permute-done.1.got_ref
  28.6 0.1 join.1
  28.7 15.5 %all_to_all.5.in_ref = bf16[4,15,32,128]{3,2,1,0:T(8,128)(2,1)S(1)} all-to-all(bf16[4,15,32,128]{3,2,1,0:T(8,128)(2,1)S(1)} %join.1), channel_id=1, replica_groups=mesh['rows'=256,'grp'=4] {'grp'}, dimensions={0} | all-to-all | bytes 983040 | tf_op jit(solution)/shard_map/all_to_all | solution.py:324
  44.2 0.8 %band.1 = f32[4,7,32,128]{3,2,1,0:T(8,128)} custom-call(bf16[4,15,32,128]{3,2,1,0:T(8,128)(2,1)S(1)} %all_to_all.5.in_ref), custom_call_target="tpu_custom_call" | custom-call | tf_op jit(solution)/shard_map/band/pallas_call | solution.py:325
Async XLA Ops:
  0.9 18.9 %collective-permute-start = (bf16[528,128]{1,0:T(8,128)(2,1)S(1)}, bf16[528,128]{1,0:T(8,128)(2,1)S(1)}, u32[]{:S(2)}, u32[]{:S(2)}) collective-permute-start(bf16[528,128]{1,0:T(8,128)(2,1)S(1)} %pack.1.p_ref), channel_id=1, source_target_pairs={{0,1},{1,0},{2,3},{3,2},{4,5},{5,4},{6,7},{7,6},{8,9},{9,8},{10,11... | collective-permute-start | bytes 405512 | tf_op jit(solution)/shard_map/ppermute | solution.py:262
  17.8 9.7 %collective-permute-start.2 = (bf16[1552,128]{1,0:T(8,128)(2,1)S(1)}, bf16[1552,128]{1,0:T(8,128)(2,1)S(1)}, u32[]{:S(2)}, u32[]{:S(2)}) collective-permute-start(bf16[1552,128]{1,0:T(8,128)(2,1)S(1)} %get-tuple-element.16), channel_id=1, source_target_pairs={{0,1023},{1,2},{2,1},{3,4},{4,3},{5,6},{6,5},{7,8},{8,7},{9,10},{1... | collective-permute-start | bytes 1191944 | tf_op jit(solution)/shard_map/ppermute | solution.py:284
  20.8 7.8 %collective-permute-start.1 = (bf16[4,128,128]{2,1,0:T(8,128)(2,1)S(1)}, bf16[4,128,128]{2,1,0:T(8,128)(2,1)S(1)}, u32[]{:S(2)}, u32[]{:S(2)}) collective-permute-start(bf16[4,128,128]{2,1,0:T(8,128)(2,1)S(1)} %get-tuple-element.14), channel_id=1, source_target_pairs={{0,1020},{3,7},{4,0},{7,11},{8,4},{11,15},{12,8},{15,19},{16,12},{... | collective-permute-start | bytes 393224 | tf_op jit(solution)/shard_map/ppermute | solution.py:302

commit v8 on v7

--- a/solution.py
+++ b/solution.py
@@ -87,11 +87,15 @@
         for r in range(RB):
             for c in range(2):
                 lhs_ref[i, r * BS : (r + 1) * BS, c * BS : (c + 1) * BS] = tiles[r, place[r, start + c]]
-    top = group_place // 2 * 2
-    for r in range(2):
-        for c in range(RB):
-            to = HALO + (r * RB + c) * BS
-            out_ref[to : to + BS, :] = tiles[top + r, place[top + r, outer + c]]
+    h = group_place // 2
+    border = jnp.where((group_place == 0) | (group_place == 3), 1, 0).astype(jnp.float32)
+    part = left[h, pl.ds(pl.multiple_of(h * BS, BS), BS), :]
+    rows = pl.ds(pl.multiple_of(h * 2 * BS, 2 * BS), 2 * BS)
+    for i in range(2):
+        both = jnp.dot(part, lhs_ref[4 + i, rows, :], preferred_element_type=jnp.float32) * border
+        for c in range(2):
+            to = HALO + (2 * i + c) * BS
+            out_ref[to : to + BS, :] = both[:, c * BS : (c + 1) * BS].astype(jnp.bfloat16)
 
 
 def halo_bits(ref):
@@ -155,38 +159,12 @@
     side = jnp.max(side_ref[...]).astype(jnp.int32)
     bits = halo_bits(one_ref)
     own_bits = halo_bits(p_ref)
-    before, after = side == 0, side == 3
-    top = jnp.where(before, 2 * BS, 0)
-    keep = (
-        jnp.where(before, bits[1], jnp.where(after, 1, 0)),
-        jnp.where(before, 1, jnp.where(after, 1 - bits[0], 0)),
-    )
-    part = jnp.concatenate(
-        [
-            (
-                one_ref[pl.ds(pl.multiple_of(top + r * BS, BS), BS), :].astype(jnp.float32).T
-                * keep[r].astype(jnp.float32)
-            ).astype(jnp.bfloat16)
-            for r in range(2)
-        ],
-        axis=1,
-    )
     for i in range(2):
         add_pair(2 * (side & 1), 2 * i, bits, lhs_ref[4 + i], weights.at[i], left, acc)
-        rows = [
-            jnp.concatenate(
-                [
-                    one_ref[HALO + (r * RB + 2 * i + c) * BS : HALO + (r * RB + 2 * i + c + 1) * BS, :]
-                    for c in range(2)
-                ],
-                axis=1,
-            )
-            for r in range(2)
-        ]
-        prod = jnp.dot(
-            jnp.concatenate(rows, axis=0), weights[2 + i], preferred_element_type=jnp.float32
-        ).astype(jnp.bfloat16)
-        sums = jnp.dot(part, prod, preferred_element_type=jnp.float32)
+        both = jnp.concatenate(
+            [one_ref[HALO + (2 * i + c) * BS : HALO + (2 * i + c + 1) * BS, :] for c in range(2)], axis=1
+        )
+        sums = jnp.dot(both, weights[2 + i], preferred_element_type=jnp.float32)
         slots = pair_slots(1, 2 * i, own_bits)
         for c in range(2):
             acc[1, slots[c]] += sums[:, c * BS : (c + 1) * BS]
@@ -263,7 +241,7 @@
     wide, lhs, left, side = pl.pallas_call(
         functools.partial(extend_kernel, count),
         out_shape=(
-            jax.ShapeDtypeStruct((HALO + 2 * RB * BS, BS), jnp.bfloat16),
+            jax.ShapeDtypeStruct((HALO + RB * BS, BS), jnp.bfloat16),
             jax.ShapeDtypeStruct((6, RB * BS, 2 * BS), jnp.bfloat16),
             jax.ShapeDtypeStruct((2, 2 * BS, 2 * BS), jnp.bfloat16),
             jax.ShapeDtypeStruct((8, BS), jnp.float32),

time: 45.3 us -> 45.3 us (level)
  waiting for transfers between devices: 6.09 us -> 4.69 us
  blocking collectives: 15.5 us -> 16.8 us
    ppermute x1, waiting for transfers between devices: 6.09 us -> 4.68 us  [shards(): lax.ppermute(wide, axes, [(i, (i + 1 if i % 2 else i - 1) % count) for i...]
    all_to_all x1, blocking collectives: 15.5 us -> 16.8 us  [shards(): parts = lax.all_to_all(joined, 'grp', 0, 0, tiled=True)]
where the time goes in v8:
time: 45.3 us; the launch traced here: 45 us
  starting transfers between devices  17.7 us (39%)
  blocking collectives  16.8 us (37%)
  Pallas kernels  5.78 us (13%)
  waiting for transfers between devices  4.69 us (10%)
    all_to_all x1, blocking collectives, shards(): parts = lax.all_to_all(joined, 'grp', 0, 0, tiled=True)  16.8 us
    ppermute x1, starting transfers between devices, shards(): two = lax.ppermute(packed, axes, [(i, i ^ 1) for i in range(count)])  15.1 us
    ppermute x1, waiting for transfers between devices, shards(): lax.ppermute(wide, axes, [(i, (i + 1 if i % 2 else i - 1) % count) for i...  4.68 us
    pallas_call x1, Pallas kernels, shards(): pl.pallas_call(functools.partial(extend_kernel, count), out_shape=(jax.Sh...  2.04 us
    ppermute x1, starting transfers between devices, shards(): lax.ppermute(wide, axes, [(i, (i + 1 if i % 2 else i - 1) % count) for i...  1.92 us
    pallas_call x1, Pallas kernels, shards(): pl.pallas_call(near_kernel, out_shape=(jax.ShapeDtypeStruct((3, 5, BS, BS...  1 us
    pallas_call x1, Pallas kernels, shards(): pl.pallas_call(rest_kernel, out_shape=jax.ShapeDtypeStruct((4, 15, 32, BS...  0.97 us
  transfers between devices with their start and end apart: 3, of which 1 were waited for; matrix products, arithmetic and copies ran while one was open for 0% of the time, Pallas kernels for 9%

profile of v8, /device:TPU:2, one launch (start us, length us, event | category | flops | bytes accessed | tf_op | source)
XLA Modules:
  0.0 45.0 jit_solution(382557099483417107)
XLA Ops:
  0.0 0.9 %pack.1.p_ref = bf16[528,128]{1,0:T(8,128)(2,1)S(1)} custom-call(s32[4]{0:T(128)} %agg_hbm.3, bf16[4,128,128]{2,1,0:T(8,128)(2,1)} %p_hbm.1), custom_call_target="tpu_custom_call" | custom-call | tf_op jit(solution)/shard_map/pack/pallas_call | solution.py:227
  0.9 15.1 %collective-permute-start = (bf16[528,128]{1,0:T(8,128)(2,1)S(1)}, bf16[528,128]{1,0:T(8,128)(2,1)S(1)}, u32[]{:S(2)}, u32[]{:S(2)}) collective-permute-start(bf16[528,128]{1,0:T(8,128)(2,1)S(1)} %pack.1.p_ref), channel_id=1, source_target_pairs={{0,1},{1,0},{2,3},{3,2},{4,5},{5,4},{6,7},{7,6},{8,9},{9,8},{10,11... | collective-permute-start | bytes 405512 | tf_op jit(solution)/shard_map/ppermute | solution.py:240
  16.0 2.0 %extend.1 = (bf16[1040,128]{1,0:T(8,128)(2,1)S(1)}, bf16[6,512,256]{2,1,0:T(8,128)(2,1)S(1)}, bf16[2,256,256]{2,1,0:T(8,128)(2,1)S(1)}, f32[8,128]{1,0:T(8,128)S(1)}) custom-call(s32[4,12]{1,0:T(4,128)} %cols_hbm.1, s32[4]{0:T(128)} %agg_hbm.3, bf16[4,12,128,128]{3,2,1,0:T(8,128)(2,1)} %a_hbm.1, bf16[528,128]{1,0:T(8,128)(2,1)S(1)} %pack.1.p_ref), custom_call_target="tpu_custom_call" | custom-call | tf_op jit(solution)/shard_map/extend/pallas_call | solution.py:241
  18.0 1.9 %collective-permute-start.2 = (bf16[1040,128]{1,0:T(8,128)(2,1)S(1)}, bf16[1040,128]{1,0:T(8,128)(2,1)S(1)}, u32[]{:S(2)}, u32[]{:S(2)}) collective-permute-start(bf16[1040,128]{1,0:T(8,128)(2,1)S(1)} %get-tuple-element.16), channel_id=1, source_target_pairs={{0,1023},{1,2},{2,1},{3,4},{4,3},{5,6},{6,5},{7,8},{8,7},{9,10},{1... | collective-permute-start | bytes 798728 | tf_op jit(solution)/shard_map/ppermute | solution.py:262
  19.9 0.0 collective-permute-done.two_ref
  20.0 1.0 %near.1 = (f32[3,5,128,128]{3,2,1,0:T(8,128)S(1)}, bf16[4,128,128]{2,1,0:T(8,128)(2,1)S(1)}) custom-call(bf16[6,512,256]{2,1,0:T(8,128)(2,1)S(1)} %get-tuple-element.12.lhs_ref, bf16[2,256,256]{2,1,0:T(8,128)(2,1)S(1)} %get-tuple-element.13.left, f32[8,128]{1,0:T(8,128)S(1)} %get-tuple-element.11.side_ref, bf16[528,128]{1,0:T(8,128)(2,1)S(1)} %pack.1.p_ref, ...), custom_call_target="tpu_custom_call" | custom-call | flops 20000000000 | bytes 100000000 | tf_op jit(solution)/shard_map/near/pallas_call | solution.py:263
  21.0 0.7 %collective-permute-start.1 = (bf16[4,128,128]{2,1,0:T(8,128)(2,1)S(1)}, bf16[4,128,128]{2,1,0:T(8,128)(2,1)S(1)}, u32[]{:S(2)}, u32[]{:S(2)}) collective-permute-start(bf16[4,128,128]{2,1,0:T(8,128)(2,1)S(1)} %get-tuple-element.14), channel_id=1, source_target_pairs={{0,1020},{3,7},{4,0},{7,11},{8,4},{11,15},{12,8},{15,19},{16,12},{... | collective-permute-start | bytes 393224 | tf_op jit(solution)/shard_map/ppermute | solution.py:280
  21.6 4.7 %collective-permute-done.2.one_ref = bf16[1040,128]{1,0:T(8,128)(2,1)S(1)} collective-permute-done((bf16[1040,128]{1,0:T(8,128)(2,1)S(1)}, bf16[1040,128]{1,0:T(8,128)(2,1)S(1)}, u32[]{:S(2)}, u32[]{:S(2)}) %collective-permute-start.2) | collective-permute-done | bytes 266272 | tf_op jit(solution)/shard_map/ppermute | solution.py:262
  26.3 1.0 %rest.1.sums_ref = bf16[4,15,32,128]{3,2,1,0:T(8,128)(2,1)S(1)} custom-call(bf16[6,512,256]{2,1,0:T(8,128)(2,1)S(1)} %get-tuple-element.12.lhs_ref, bf16[2,256,256]{2,1,0:T(8,128)(2,1)S(1)} %get-tuple-element.13.left, f32[3,5,128,128]{3,2,1,0:T(8,128)S(1)} %get-tuple-element.15.near, f32[8,128]{1,0:T(8,128)S(1)} %get-tuple-element.11.side_ref, ...), custom_call_target="tpu_custom_call" | custom-call | flops 200000000 | bytes 3000000 | tf_op jit(solution)/shard_map/rest/pallas_call | solution.py:281
  27.3 0.0 collective-permute-done.1.got_ref
  27.3 0.1 join.1
  27.4 16.8 %all_to_all.5.in_ref = bf16[4,15,32,128]{3,2,1,0:T(8,128)(2,1)S(1)} all-to-all(bf16[4,15,32,128]{3,2,1,0:T(8,128)(2,1)S(1)} %join.1), channel_id=1, replica_groups=mesh['rows'=256,'grp'=4] {'grp'}, dimensions={0} | all-to-all | bytes 983040 | tf_op jit(solution)/shard_map/all_to_all | solution.py:302
  44.2 0.8 %band.1 = f32[4,7,32,128]{3,2,1,0:T(8,128)} custom-call(bf16[4,15,32,128]{3,2,1,0:T(8,128)(2,1)S(1)} %all_to_all.5.in_ref), custom_call_target="tpu_custom_call" | custom-call | tf_op jit(solution)/shard_map/band/pallas_call | solution.py:303
Async XLA Ops:
  0.9 19.1 %collective-permute-start = (bf16[528,128]{1,0:T(8,128)(2,1)S(1)}, bf16[528,128]{1,0:T(8,128)(2,1)S(1)}, u32[]{:S(2)}, u32[]{:S(2)}) collective-permute-start(bf16[528,128]{1,0:T(8,128)(2,1)S(1)} %pack.1.p_ref), channel_id=1, source_target_pairs={{0,1},{1,0},{2,3},{3,2},{4,5},{5,4},{6,7},{7,6},{8,9},{9,8},{10,11... | collective-permute-start | bytes 405512 | tf_op jit(solution)/shard_map/ppermute | solution.py:240
  18.0 8.3 %collective-permute-start.2 = (bf16[1040,128]{1,0:T(8,128)(2,1)S(1)}, bf16[1040,128]{1,0:T(8,128)(2,1)S(1)}, u32[]{:S(2)}, u32[]{:S(2)}) collective-permute-start(bf16[1040,128]{1,0:T(8,128)(2,1)S(1)} %get-tuple-element.16), channel_id=1, source_target_pairs={{0,1023},{1,2},{2,1},{3,4},{4,3},{5,6},{6,5},{7,8},{8,7},{9,10},{1... | collective-permute-start | bytes 798728 | tf_op jit(solution)/shard_map/ppermute | solution.py:262
  21.0 6.3 %collective-permute-start.1 = (bf16[4,128,128]{2,1,0:T(8,128)(2,1)S(1)}, bf16[4,128,128]{2,1,0:T(8,128)(2,1)S(1)}, u32[]{:S(2)}, u32[]{:S(2)}) collective-permute-start(bf16[4,128,128]{2,1,0:T(8,128)(2,1)S(1)} %get-tuple-element.14), channel_id=1, source_target_pairs={{0,1020},{3,7},{4,0},{7,11},{8,4},{11,15},{12,8},{15,19},{16,12},{... | collective-permute-start | bytes 393224 | tf_op jit(solution)/shard_map/ppermute | solution.py:280

commit v9 on v8

--- a/solution.py
+++ b/solution.py
@@ -49,9 +49,9 @@
     cols_copy.start()
     agg_copy.start()
     copies = [
-        pltpu.make_async_copy(a_hbm.at[r, pl.ds(6 * h, 6)], tiles.at[r, pl.ds(6 * h, 6)], a_sems.at[r, h])
+        pltpu.make_async_copy(a_hbm.at[r, pl.ds(3 * h, 3)], tiles.at[r, pl.ds(3 * h, 3)], a_sems.at[r, h])
         for r in range(RB)
-        for h in range(2)
+        for h in range(4)
     ]
     for copy in copies:
         copy.start()
@@ -80,11 +80,11 @@
     odd = (first + 1) & 1
     inner = (1 - odd) * 2 * RB
     outer = odd * 2 * RB
-    for copy in copies:
-        copy.wait()
-    for i in range(6):
-        start = (RB, inner, outer)[i // 2] + 2 * (i % 2)
-        for r in range(RB):
+    for r in range(RB):
+        for copy in copies[4 * r : 4 * r + 4]:
+            copy.wait()
+        for i in range(6):
+            start = (RB, inner, outer)[i // 2] + 2 * (i % 2)
             for c in range(2):
                 lhs_ref[i, r * BS : (r + 1) * BS, c * BS : (c + 1) * BS] = tiles[r, place[r, start + c]]
     h = group_place // 2
@@ -254,7 +254,7 @@
             pltpu.SMEM((RB, KT), jnp.int32),
             pltpu.VMEM((RB, KT, BS, BS), jnp.bfloat16),
             pltpu.SemaphoreType.DMA((2,)),
-            pltpu.SemaphoreType.DMA((RB, 2)),
+            pltpu.SemaphoreType.DMA((RB, 4)),
         ],
         compiler_params=params,
         name="extend",

time: 45.3 us -> 45.2 us (level)
  no operation moved by 1% of the time
where the time goes in v9:
time: 45.2 us; the launch traced here: 44.8 us
  starting transfers between devices  17.7 us (39%)
  blocking collectives  16.8 us (37%)
  Pallas kernels  5.62 us (12%)
  waiting for transfers between devices  4.69 us (10%)
    all_to_all x1, blocking collectives, shards(): parts = lax.all_to_all(joined, 'grp', 0, 0, tiled=True)  16.8 us
    ppermute x1, starting transfers between devices, shards(): two = lax.ppermute(packed, axes, [(i, i ^ 1) for i in range(count)])  15.1 us
    ppermute x1, waiting for transfers between devices, shards(): lax.ppermute(wide, axes, [(i, (i + 1 if i % 2 else i - 1) % count) for i...  4.68 us
    ppermute x1, starting transfers between devices, shards(): lax.ppermute(wide, axes, [(i, (i + 1 if i % 2 else i - 1) % count) for i...  1.92 us
    pallas_call x1, Pallas kernels, shards(): pl.pallas_call(functools.partial(extend_kernel, count), out_shape=(jax.Sh...  1.88 us
    pallas_call x1, Pallas kernels, shards(): pl.pallas_call(near_kernel, out_shape=(jax.ShapeDtypeStruct((3, 5, BS, BS...  1 us
    pallas_call x1, Pallas kernels, shards(): pl.pallas_call(rest_kernel, out_shape=jax.ShapeDtypeStruct((4, 15, 32, BS...  0.97 us
  transfers between devices with their start and end apart: 3, of which 1 were waited for; matrix products, arithmetic and copies ran while one was open for 0% of the time, Pallas kernels for 9%

profile of v9, /device:TPU:2, one launch (start us, length us, event | category | flops | bytes accessed | tf_op | source)
XLA Modules:
  0.0 44.8 jit_solution(16706243618167799832)
XLA Ops:
  0.0 0.9 %pack.1.p_ref = bf16[528,128]{1,0:T(8,128)(2,1)S(1)} custom-call(s32[4]{0:T(128)} %agg_hbm.3, bf16[4,128,128]{2,1,0:T(8,128)(2,1)} %p_hbm.1), custom_call_target="tpu_custom_call" | custom-call | tf_op jit(solution)/shard_map/pack/pallas_call | solution.py:227
  0.9 15.1 %collective-permute-start = (bf16[528,128]{1,0:T(8,128)(2,1)S(1)}, bf16[528,128]{1,0:T(8,128)(2,1)S(1)}, u32[]{:S(2)}, u32[]{:S(2)}) collective-permute-start(bf16[528,128]{1,0:T(8,128)(2,1)S(1)} %pack.1.p_ref), channel_id=1, source_target_pairs={{0,1},{1,0},{2,3},{3,2},{4,5},{5,4},{6,7},{7,6},{8,9},{9,8},{10,11... | collective-permute-start | bytes 405512 | tf_op jit(solution)/shard_map/ppermute | solution.py:240
  16.0 1.9 %extend.1 = (bf16[1040,128]{1,0:T(8,128)(2,1)S(1)}, bf16[6,512,256]{2,1,0:T(8,128)(2,1)S(1)}, bf16[2,256,256]{2,1,0:T(8,128)(2,1)S(1)}, f32[8,128]{1,0:T(8,128)S(1)}) custom-call(s32[4,12]{1,0:T(4,128)} %cols_hbm.1, s32[4]{0:T(128)} %agg_hbm.3, bf16[4,12,128,128]{3,2,1,0:T(8,128)(2,1)} %a_hbm.1, bf16[528,128]{1,0:T(8,128)(2,1)S(1)} %pack.1.p_ref), custom_call_target="tpu_custom_call" | custom-call | tf_op jit(solution)/shard_map/extend/pallas_call | solution.py:241
  17.9 1.9 %collective-permute-start.2 = (bf16[1040,128]{1,0:T(8,128)(2,1)S(1)}, bf16[1040,128]{1,0:T(8,128)(2,1)S(1)}, u32[]{:S(2)}, u32[]{:S(2)}) collective-permute-start(bf16[1040,128]{1,0:T(8,128)(2,1)S(1)} %get-tuple-element.16), channel_id=1, source_target_pairs={{0,1023},{1,2},{2,1},{3,4},{4,3},{5,6},{6,5},{7,8},{8,7},{9,10},{1... | collective-permute-start | bytes 798728 | tf_op jit(solution)/shard_map/ppermute | solution.py:262
  19.8 0.0 collective-permute-done.two_ref
  19.8 1.0 %near.1 = (f32[3,5,128,128]{3,2,1,0:T(8,128)S(1)}, bf16[4,128,128]{2,1,0:T(8,128)(2,1)S(1)}) custom-call(bf16[6,512,256]{2,1,0:T(8,128)(2,1)S(1)} %get-tuple-element.12.lhs_ref, bf16[2,256,256]{2,1,0:T(8,128)(2,1)S(1)} %get-tuple-element.13.left, f32[8,128]{1,0:T(8,128)S(1)} %get-tuple-element.11.side_ref, bf16[528,128]{1,0:T(8,128)(2,1)S(1)} %pack.1.p_ref, ...), custom_call_target="tpu_custom_call" | custom-call | flops 20000000000 | bytes 100000000 | tf_op jit(solution)/shard_map/near/pallas_call | solution.py:263
  20.8 0.7 %collective-permute-start.1 = (bf16[4,128,128]{2,1,0:T(8,128)(2,1)S(1)}, bf16[4,128,128]{2,1,0:T(8,128)(2,1)S(1)}, u32[]{:S(2)}, u32[]{:S(2)}) collective-permute-start(bf16[4,128,128]{2,1,0:T(8,128)(2,1)S(1)} %get-tuple-element.14), channel_id=1, source_target_pairs={{0,1020},{3,7},{4,0},{7,11},{8,4},{11,15},{12,8},{15,19},{16,12},{... | collective-permute-start | bytes 393224 | tf_op jit(solution)/shard_map/ppermute | solution.py:280
  21.5 4.7 %collective-permute-done.2.one_ref = bf16[1040,128]{1,0:T(8,128)(2,1)S(1)} collective-permute-done((bf16[1040,128]{1,0:T(8,128)(2,1)S(1)}, bf16[1040,128]{1,0:T(8,128)(2,1)S(1)}, u32[]{:S(2)}, u32[]{:S(2)}) %collective-permute-start.2) | collective-permute-done | bytes 266272 | tf_op jit(solution)/shard_map/ppermute | solution.py:262
  26.2 1.0 %rest.1.sums_ref = bf16[4,15,32,128]{3,2,1,0:T(8,128)(2,1)S(1)} custom-call(bf16[6,512,256]{2,1,0:T(8,128)(2,1)S(1)} %get-tuple-element.12.lhs_ref, bf16[2,256,256]{2,1,0:T(8,128)(2,1)S(1)} %get-tuple-element.13.left, f32[3,5,128,128]{3,2,1,0:T(8,128)S(1)} %get-tuple-element.15.near, f32[8,128]{1,0:T(8,128)S(1)} %get-tuple-element.11.side_ref, ...), custom_call_target="tpu_custom_call" | custom-call | flops 200000000 | bytes 3000000 | tf_op jit(solution)/shard_map/rest/pallas_call | solution.py:281
  27.1 0.0 collective-permute-done.1.got_ref
  27.1 0.1 join.1
  27.2 16.8 %all_to_all.5.in_ref = bf16[4,15,32,128]{3,2,1,0:T(8,128)(2,1)S(1)} all-to-all(bf16[4,15,32,128]{3,2,1,0:T(8,128)(2,1)S(1)} %join.1), channel_id=1, replica_groups=mesh['rows'=256,'grp'=4] {'grp'}, dimensions={0} | all-to-all | bytes 983040 | tf_op jit(solution)/shard_map/all_to_all | solution.py:302
  44.0 0.8 %band.1 = f32[4,7,32,128]{3,2,1,0:T(8,128)} custom-call(bf16[4,15,32,128]{3,2,1,0:T(8,128)(2,1)S(1)} %all_to_all.5.in_ref), custom_call_target="tpu_custom_call" | custom-call | tf_op jit(solution)/shard_map/band/pallas_call | solution.py:303
Async XLA Ops:
  0.9 18.9 %collective-permute-start = (bf16[528,128]{1,0:T(8,128)(2,1)S(1)}, bf16[528,128]{1,0:T(8,128)(2,1)S(1)}, u32[]{:S(2)}, u32[]{:S(2)}) collective-permute-start(bf16[528,128]{1,0:T(8,128)(2,1)S(1)} %pack.1.p_ref), channel_id=1, source_target_pairs={{0,1},{1,0},{2,3},{3,2},{4,5},{5,4},{6,7},{7,6},{8,9},{9,8},{10,11... | collective-permute-start | bytes 405512 | tf_op jit(solution)/shard_map/ppermute | solution.py:240
  17.9 8.3 %collective-permute-start.2 = (bf16[1040,128]{1,0:T(8,128)(2,1)S(1)}, bf16[1040,128]{1,0:T(8,128)(2,1)S(1)}, u32[]{:S(2)}, u32[]{:S(2)}) collective-permute-start(bf16[1040,128]{1,0:T(8,128)(2,1)S(1)} %get-tuple-element.16), channel_id=1, source_target_pairs={{0,1023},{1,2},{2,1},{3,4},{4,3},{5,6},{6,5},{7,8},{8,7},{9,10},{1... | collective-permute-start | bytes 798728 | tf_op jit(solution)/shard_map/ppermute | solution.py:262
  20.8 6.3 %collective-permute-start.1 = (bf16[4,128,128]{2,1,0:T(8,128)(2,1)S(1)}, bf16[4,128,128]{2,1,0:T(8,128)(2,1)S(1)}, u32[]{:S(2)}, u32[]{:S(2)}) collective-permute-start(bf16[4,128,128]{2,1,0:T(8,128)(2,1)S(1)} %get-tuple-element.14), channel_id=1, source_target_pairs={{0,1020},{3,7},{4,0},{7,11},{8,4},{11,15},{12,8},{15,19},{16,12},{... | collective-permute-start | bytes 393224 | tf_op jit(solution)/shard_map/ppermute | solution.py:280

commit v10 on v9

--- a/solution.py
+++ b/solution.py
@@ -23,12 +23,17 @@
     return low, high
 
 
-def pack_kernel(count, agg_hbm, p_hbm, out_ref, agg_ref, agg_sem, p_sem):
+def pack_kernel(count, agg_hbm, p_hbm, a_hbm, out_ref, tiles_ref, agg_ref, agg_sem, p_sem, a_sems):
     agg_copy = pltpu.make_async_copy(agg_hbm, agg_ref, agg_sem)
     agg_copy.start()
     copies = [
         pltpu.make_async_copy(p_hbm.at[r], out_ref.at[pl.ds(r * BS, BS)], p_sem.at[r])
         for r in range(RB)
+    ]
+    copies += [
+        pltpu.make_async_copy(a_hbm.at[r, pl.ds(6 * h, 6)], tiles_ref.at[r, pl.ds(6 * h, 6)], a_sems.at[r, h])
+        for r in range(2)
+        for h in range(2)
     ]
     for copy in copies:
         copy.start()
@@ -41,7 +46,7 @@
 
 
 def extend_kernel(
-    count, cols_hbm, agg_hbm, a_hbm, p_ref, out_ref, lhs_ref, left, side_ref,
+    count, cols_hbm, agg_hbm, a_hbm, p_ref, head_ref, out_ref, lhs_ref, left, side_ref,
     cols_ref, agg_ref, place, tiles, sems, a_sems,
 ):
     cols_copy = pltpu.make_async_copy(cols_hbm, cols_ref, sems.at[0])
@@ -49,9 +54,9 @@
     cols_copy.start()
     agg_copy.start()
     copies = [
-        pltpu.make_async_copy(a_hbm.at[r, pl.ds(3 * h, 3)], tiles.at[r, pl.ds(3 * h, 3)], a_sems.at[r, h])
-        for r in range(RB)
-        for h in range(4)
+        pltpu.make_async_copy(a_hbm.at[2 + r, pl.ds(6 * h, 6)], tiles.at[r, pl.ds(6 * h, 6)], a_sems.at[r, h])
+        for r in range(2)
+        for h in range(2)
     ]
     for copy in copies:
         copy.start()
@@ -81,12 +86,14 @@
     inner = (1 - odd) * 2 * RB
     outer = odd * 2 * RB
     for r in range(RB):
-        for copy in copies[4 * r : 4 * r + 4]:
-            copy.wait()
+        if r == 2:
+            for copy in copies:
+                copy.wait()
         for i in range(6):
             start = (RB, inner, outer)[i // 2] + 2 * (i % 2)
             for c in range(2):
-                lhs_ref[i, r * BS : (r + 1) * BS, c * BS : (c + 1) * BS] = tiles[r, place[r, start + c]]
+                tile = (head_ref if r < 2 else tiles)[r % 2, place[r, start + c]]
+                lhs_ref[i, r * BS : (r + 1) * BS, c * BS : (c + 1) * BS] = tile
     h = group_place // 2
     border = jnp.where((group_place == 0) | (group_place == 3), 1, 0).astype(jnp.float32)
     part = left[h, pl.ds(pl.multiple_of(h * BS, BS), BS), :]
@@ -224,19 +231,23 @@
     a_tiles, a_cols, p_tiles, p_agg = (
         pltpu.with_memory_space_constraint(x, pltpu.HBM) for x in (a_tiles, a_cols, p_tiles, p_agg)
     )
-    packed = pl.pallas_call(
+    packed, head = pl.pallas_call(
         functools.partial(pack_kernel, count),
-        out_shape=jax.ShapeDtypeStruct((HALO, BS), jnp.bfloat16),
-        in_specs=[HBM, HBM],
-        out_specs=VMEM,
+        out_shape=(
+            jax.ShapeDtypeStruct((HALO, BS), jnp.bfloat16),
+            jax.ShapeDtypeStruct((2, KT, BS, BS), jnp.bfloat16),
+        ),
+        in_specs=[HBM, HBM, HBM],
+        out_specs=(VMEM, VMEM),
         scratch_shapes=[
             pltpu.SMEM((RB,), jnp.int32),
             pltpu.SemaphoreType.DMA,
             pltpu.SemaphoreType.DMA((RB,)),
+            pltpu.SemaphoreType.DMA((2, 2)),
         ],
         compiler_params=params,
         name="pack",
-    )(p_agg, p_tiles)
+    )(p_agg, p_tiles, a_tiles)
     two = lax.ppermute(packed, axes, [(i, i ^ 1) for i in range(count)])
     wide, lhs, left, side = pl.pallas_call(
         functools.partial(extend_kernel, count),
@@ -246,19 +257,19 @@
             jax.ShapeDtypeStruct((2, 2 * BS, 2 * BS), jnp.bfloat16),
             jax.ShapeDtypeStruct((8, BS), jnp.float32),
         ),
-        in_specs=[HBM, HBM, HBM, VMEM],
+        in_specs=[HBM, HBM, HBM, VMEM, VMEM],
         out_specs=(VMEM, VMEM, VMEM, VMEM),
         scratch_shapes=[
             pltpu.SMEM((RB, KT), jnp.int32),
             pltpu.SMEM((RB,), jnp.int32),
             pltpu.SMEM((RB, KT), jnp.int32),
-            pltpu.VMEM((RB, KT, BS, BS), jnp.bfloat16),
+            pltpu.VMEM((2, KT, BS, BS), jnp.bfloat16),
             pltpu.SemaphoreType.DMA((2,)),
-            pltpu.SemaphoreType.DMA((RB, 4)),
+            pltpu.SemaphoreType.DMA((2, 2)),
         ],
         compiler_params=params,
         name="extend",
-    )(a_cols, p_agg, a_tiles, packed)
+    )(a_cols, p_agg, a_tiles, packed, head)
     one = lax.ppermute(wide, axes, [(i, (i + 1 if i % 2 else i - 1) % count) for i in range(count)])
     near, edge = pl.pallas_call(
         near_kernel,

time: 45.2 us -> 45.4 us (level)
    pallas_call x1, Pallas kernels: 0.85 us -> 1.36 us  [shards(): pl.pallas_call(functools.partial(pack_kernel, count), out_shape=(jax.Shap...]
  transfers between devices with their start and end apart: 3 -> 3, of which waited for: 1 -> 1; matrix products, arithmetic and copies ran while one was open for 0% -> 0% of each run, Pallas kernels for 9% -> 8%
where the time goes in v10:
time: 45.4 us; the launch traced here: 45.1 us
  starting transfers between devices  17.7 us (39%)
  blocking collectives  16.8 us (37%)
  Pallas kernels  5.91 us (13%)
  waiting for transfers between devices  4.68 us (10%)
    all_to_all x1, blocking collectives, shards(): parts = lax.all_to_all(joined, 'grp', 0, 0, tiled=True)  16.8 us
    ppermute x1, starting transfers between devices, shards(): two = lax.ppermute(packed, axes, [(i, i ^ 1) for i in range(count)])  15.1 us
    ppermute x1, waiting for transfers between devices, shards(): lax.ppermute(wide, axes, [(i, (i + 1 if i % 2 else i - 1) % count) for i...  4.68 us
    ppermute x1, starting transfers between devices, shards(): lax.ppermute(wide, axes, [(i, (i + 1 if i % 2 else i - 1) % count) for i...  1.92 us
    pallas_call x1, Pallas kernels, shards(): pl.pallas_call(functools.partial(extend_kernel, count), out_shape=(jax.Sh...  1.65 us
    pallas_call x1, Pallas kernels, shards(): pl.pallas_call(functools.partial(pack_kernel, count), out_shape=(jax.Shap...  1.36 us
    pallas_call x1, Pallas kernels, shards(): pl.pallas_call(near_kernel, out_shape=(jax.ShapeDtypeStruct((3, 5, BS, BS...  1.01 us
    pallas_call x1, Pallas kernels, shards(): pl.pallas_call(rest_kernel, out_shape=jax.ShapeDtypeStruct((4, 15, 32, BS...  0.97 us
  transfers between devices with their start and end apart: 3, of which 1 were waited for; matrix products, arithmetic and copies ran while one was open for 0% of the time, Pallas kernels for 8%

profile of v10, /device:TPU:2, one launch (start us, length us, event | category | flops | bytes accessed | tf_op | source)
XLA Modules:
  0.0 45.1 jit_solution(13857539427602608082)
XLA Ops:
  0.0 1.4 %pack.1 = (bf16[528,128]{1,0:T(8,128)(2,1)S(1)}, bf16[2,12,128,128]{3,2,1,0:T(8,128)(2,1)S(1)}) custom-call(s32[4]{0:T(128)} %agg_hbm.3, bf16[4,128,128]{2,1,0:T(8,128)(2,1)} %p_hbm.1, bf16[4,12,128,128]{3,2,1,0:T(8,128)(2,1)} %a_hbm.3), custom_call_target="tpu_custom_call" | custom-call | tf_op jit(solution)/shard_map/pack/pallas_call | solution.py:234
  1.4 15.1 %collective-permute-start = (bf16[528,128]{1,0:T(8,128)(2,1)S(1)}, bf16[528,128]{1,0:T(8,128)(2,1)S(1)}, u32[]{:S(2)}, u32[]{:S(2)}) collective-permute-start(bf16[528,128]{1,0:T(8,128)(2,1)S(1)} %get-tuple-element.13.p_ref), channel_id=1, source_target_pairs={{0,1},{1,0},{2,3},{3,2},{4,5},{5,4},{6,7},{7,6},{8,9},{9,8},{10,11... | collective-permute-start | bytes 405512 | tf_op jit(solution)/shard_map/ppermute | solution.py:251
  16.5 1.6 %extend.1 = (bf16[1040,128]{1,0:T(8,128)(2,1)S(1)}, bf16[6,512,256]{2,1,0:T(8,128)(2,1)S(1)}, bf16[2,256,256]{2,1,0:T(8,128)(2,1)S(1)}, f32[8,128]{1,0:T(8,128)S(1)}) custom-call(s32[4,12]{1,0:T(4,128)} %cols_hbm.1, s32[4]{0:T(128)} %agg_hbm.3, bf16[4,12,128,128]{3,2,1,0:T(8,128)(2,1)} %a_hbm.3, bf16[528,128]{1,0:T(8,128)(2,1)S(1)} %get-tuple-element.13.p_ref, ...), custom_call_target="tpu_custom_call" | custom-call | tf_op jit(solution)/shard_map/extend/pallas_call | solution.py:252
  18.1 1.9 %collective-permute-start.2 = (bf16[1040,128]{1,0:T(8,128)(2,1)S(1)}, bf16[1040,128]{1,0:T(8,128)(2,1)S(1)}, u32[]{:S(2)}, u32[]{:S(2)}) collective-permute-start(bf16[1040,128]{1,0:T(8,128)(2,1)S(1)} %get-tuple-element.20), channel_id=1, source_target_pairs={{0,1023},{1,2},{2,1},{3,4},{4,3},{5,6},{6,5},{7,8},{8,7},{9,10},{1... | collective-permute-start | bytes 798728 | tf_op jit(solution)/shard_map/ppermute | solution.py:273
  20.1 0.0 collective-permute-done.two_ref
  20.1 1.0 %near.1 = (f32[3,5,128,128]{3,2,1,0:T(8,128)S(1)}, bf16[4,128,128]{2,1,0:T(8,128)(2,1)S(1)}) custom-call(bf16[6,512,256]{2,1,0:T(8,128)(2,1)S(1)} %get-tuple-element.16.lhs_ref, bf16[2,256,256]{2,1,0:T(8,128)(2,1)S(1)} %get-tuple-element.17.left, f32[8,128]{1,0:T(8,128)S(1)} %get-tuple-element.15.side_ref, bf16[528,128]{1,0:T(8,128)(2,1)S(1)} %get-tuple-element.13.p_ref, ...), custom_call_target="tpu_custom_call" | custom-call | flops 20000000000 | bytes 100000000 | tf_op jit(solution)/shard_map/near/pallas_call | solution.py:274
  21.1 0.7 %collective-permute-start.1 = (bf16[4,128,128]{2,1,0:T(8,128)(2,1)S(1)}, bf16[4,128,128]{2,1,0:T(8,128)(2,1)S(1)}, u32[]{:S(2)}, u32[]{:S(2)}) collective-permute-start(bf16[4,128,128]{2,1,0:T(8,128)(2,1)S(1)} %get-tuple-element.18), channel_id=1, source_target_pairs={{0,1020},{3,7},{4,0},{7,11},{8,4},{11,15},{12,8},{15,19},{16,12},{... | collective-permute-start | bytes 393224 | tf_op jit(solution)/shard_map/ppermute | solution.py:291
  21.8 4.7 %collective-permute-done.2.one_ref = bf16[1040,128]{1,0:T(8,128)(2,1)S(1)} collective-permute-done((bf16[1040,128]{1,0:T(8,128)(2,1)S(1)}, bf16[1040,128]{1,0:T(8,128)(2,1)S(1)}, u32[]{:S(2)}, u32[]{:S(2)}) %collective-permute-start.2) | collective-permute-done | bytes 266272 | tf_op jit(solution)/shard_map/ppermute | solution.py:273
  26.4 1.0 %rest.1.sums_ref = bf16[4,15,32,128]{3,2,1,0:T(8,128)(2,1)S(1)} custom-call(bf16[6,512,256]{2,1,0:T(8,128)(2,1)S(1)} %get-tuple-element.16.lhs_ref, bf16[2,256,256]{2,1,0:T(8,128)(2,1)S(1)} %get-tuple-element.17.left, f32[3,5,128,128]{3,2,1,0:T(8,128)S(1)} %get-tuple-element.19.near, f32[8,128]{1,0:T(8,128)S(1)} %get-tuple-element.15.side_ref, ...), custom_call_target="tpu_custom_call" | custom-call | flops 200000000 | bytes 3000000 | tf_op jit(solution)/shard_map/rest/pallas_call | solution.py:292
  27.4 0.0 collective-permute-done.1.got_ref
  27.4 0.1 join.1
  27.5 16.8 %all_to_all.5.in_ref = bf16[4,15,32,128]{3,2,1,0:T(8,128)(2,1)S(1)} all-to-all(bf16[4,15,32,128]{3,2,1,0:T(8,128)(2,1)S(1)} %join.1), channel_id=1, replica_groups=mesh['rows'=256,'grp'=4] {'grp'}, dimensions={0} | all-to-all | bytes 983040 | tf_op jit(solution)/shard_map/all_to_all | solution.py:313
  44.3 0.8 %band.1 = f32[4,7,32,128]{3,2,1,0:T(8,128)} custom-call(bf16[4,15,32,128]{3,2,1,0:T(8,128)(2,1)S(1)} %all_to_all.5.in_ref), custom_call_target="tpu_custom_call" | custom-call | tf_op jit(solution)/shard_map/band/pallas_call | solution.py:314
Async XLA Ops:
  1.4 18.7 %collective-permute-start = (bf16[528,128]{1,0:T(8,128)(2,1)S(1)}, bf16[528,128]{1,0:T(8,128)(2,1)S(1)}, u32[]{:S(2)}, u32[]{:S(2)}) collective-permute-start(bf16[528,128]{1,0:T(8,128)(2,1)S(1)} %get-tuple-element.13.p_ref), channel_id=1, source_target_pairs={{0,1},{1,0},{2,3},{3,2},{4,5},{5,4},{6,7},{7,6},{8,9},{9,8},{10,11... | collective-permute-start | bytes 405512 | tf_op jit(solution)/shard_map/ppermute | solution.py:251
  18.1 8.3 %collective-permute-start.2 = (bf16[1040,128]{1,0:T(8,128)(2,1)S(1)}, bf16[1040,128]{1,0:T(8,128)(2,1)S(1)}, u32[]{:S(2)}, u32[]{:S(2)}) collective-permute-start(bf16[1040,128]{1,0:T(8,128)(2,1)S(1)} %get-tuple-element.20), channel_id=1, source_target_pairs={{0,1023},{1,2},{2,1},{3,4},{4,3},{5,6},{6,5},{7,8},{8,7},{9,10},{1... | collective-permute-start | bytes 798728 | tf_op jit(solution)/shard_map/ppermute | solution.py:273
  21.1 6.3 %collective-permute-start.1 = (bf16[4,128,128]{2,1,0:T(8,128)(2,1)S(1)}, bf16[4,128,128]{2,1,0:T(8,128)(2,1)S(1)}, u32[]{:S(2)}, u32[]{:S(2)}) collective-permute-start(bf16[4,128,128]{2,1,0:T(8,128)(2,1)S(1)} %get-tuple-element.18), channel_id=1, source_target_pairs={{0,1020},{3,7},{4,0},{7,11},{8,4},{11,15},{12,8},{15,19},{16,12},{... | collective-permute-start | bytes 393224 | tf_op jit(solution)/shard_map/ppermute | solution.py:291
